TPU v7x, 32 devices: a whole 2x2x4 slice. The times are simulated.
32 devices in a mesh: dp: 2 (over core), fsdp: 16 (over z, y, x).
Axes of the slice: x: 2, y: 2, z: 4, core: 2. Of those that a mesh axis runs over, the one named last changes fastest.
Arguments:
- tokens: bfloat16 [32, 1024, 512], P(('dp', 'fsdp'))
- lengths: int32 [32, 256], P(('dp', 'fsdp')), may hold values from 0 to 250, as said below
- attend_weight: float32 [512, 1536], P('fsdp'), may hold values from -0.1875 to 0.1875
- merger_weight: float32 [512, 512], P('fsdp'), may hold values from -1 to 1
- expand_weight: float32 [512, 2048], P('fsdp'), may hold values from -0.25 to 0.25
- shrink_weight: float32 [2048, 512], P('fsdp'), may hold values from -0.125 to 0.125
- vectors: float32 [6, 512], P(None, 'fsdp')
- attend_rows: float32 [512], P('fsdp'), may hold values from 2.2230691e-07 to 8.8922764e-07
- attend_columns: float32 [1536], P('fsdp'), may hold values from 2.2230691e-07 to 8.8922764e-07
- merger_rows: float32 [512], P('fsdp'), may hold values from 1.1115345e-08 to 4.446138e-08
- merger_columns: float32 [512], P('fsdp'), may hold values from 1.1115345e-08 to 4.446138e-08
- expand_rows: float32 [512], P('fsdp'), may hold values from 1.2703252e-08 to 5.0813007e-08
- expand_columns: float32 [2048], P('fsdp'), may hold values from 1.2703252e-08 to 5.0813007e-08
- shrink_rows: float32 [2048], P('fsdp'), may hold values from 3.175813e-08 to 1.2703252e-07
- shrink_columns: float32 [512], P('fsdp'), may hold values from 3.175813e-08 to 1.2703252e-07
- vector_moments: float32 [6, 512], P(None, 'fsdp'), may hold values from 8.8922764e-07 to 3.4933944e-06
- cotangent: bfloat16 [32, 1024, 512], P(('dp', 'fsdp')), may hold values from -6 to 6
Outputs:
- block_output: bfloat16 [32, 1024, 512], P(('dp', 'fsdp'))
- input_gradient: float32 [32, 1024, 512], P(('dp', 'fsdp'))
- global_norm: float32 [], replicated
- attend_gradient: float32 [512, 1536], P('fsdp')
- attend_newrows: float32 [512], P('fsdp')
- attend_newcols: float32 [1536], P('fsdp')
- attend_updated: float32 [512, 1536], P('fsdp')
- attend_bfloat: bfloat16 [512, 1536], P('fsdp')
- merger_gradient: float32 [512, 512], P('fsdp')
- merger_newrows: float32 [512], P('fsdp')
- merger_newcols: float32 [512], P('fsdp')
- merger_updated: float32 [512, 512], P('fsdp')
- merger_bfloat: bfloat16 [512, 512], P('fsdp')
- expand_gradient: float32 [512, 2048], P('fsdp')
- expand_newrows: float32 [512], P('fsdp')
- expand_newcols: float32 [2048], P('fsdp')
- expand_updated: float32 [512, 2048], P('fsdp')
- expand_bfloat: bfloat16 [512, 2048], P('fsdp')
- shrink_gradient: float32 [2048, 512], P('fsdp')
- shrink_newrows: float32 [2048], P('fsdp')
- shrink_newcols: float32 [512], P('fsdp')
- shrink_updated: float32 [2048, 512], P('fsdp')
- shrink_bfloat: bfloat16 [2048, 512], P('fsdp')
- vector_gradient: float32 [6, 512], P(None, 'fsdp')
- vector_variance: float32 [6, 512], P(None, 'fsdp')
- vector_updated: float32 [6, 512], P(None, 'fsdp')
Inputs may be any that keep to these rules, and one draw needn't show every extreme that they name: Each row of 1024 slots holds documents of these lengths in order, then padding; a row's lengths sum to at most 1024; exactly one entry of each row equals 250, the others are shorter; zeros come only after the last document.
All inputs are finite; a program needn't handle non-finite values.
Results may differ from a plain program's by a relative error of at most 0.012.
The roundings to bfloat16 on the way count: a program that leaves them out, or rounds other values in their place, can miss the bound.
Values may be sent and summed in bfloat16 or wider, within the bound.
A program may use at most 192 MiB of HBM per device.

v0:
```python
import jax
import jax.numpy as jnp
from jax import lax
from jax.sharding import PartitionSpec as P

HEAD_DIM = 64
STEP = 3


EPSILON = 1e-05
TINY_VALUE = 1e-30
NEGATIVE = -1e30
THRESHOLD = 1.0
UPDATE_LIMIT = 1.0
LEARN_RATE = 0.5


def layout(lengths_row, slot_count):
    doc_ends = jnp.cumsum(lengths_row, dtype=jnp.int32)
    places = jnp.arange(slot_count, dtype=jnp.int32)
    segment = jnp.sum(
        (doc_ends[None, :] <= places[:, None]).astype(jnp.int32), axis=1, dtype=jnp.int32
    )
    valid_slot = places < doc_ends[-1]
    allowed = (
        (segment[:, None] == segment[None, :])
        & (places[None, :] <= places[:, None])
        & valid_slot[None, :]
    )
    allowed = allowed | (places[:, None] == places[None, :])
    return (allowed, valid_slot)


def norm_forward(values, gain_row, shift_row):
    centered = values - jnp.mean(values, axis=-1, keepdims=True)
    scale_inv = lax.rsqrt(jnp.mean(centered * centered, axis=-1, keepdims=True) + EPSILON)
    normed = centered * scale_inv
    return (normed * gain_row + shift_row, normed, scale_inv)


def norm_backward(upstream, normed, scale_inv, gain_row):
    scaled = upstream * gain_row
    inner = (
        scaled
        - jnp.mean(scaled, axis=-1, keepdims=True)
        - normed * jnp.mean(scaled * normed, axis=-1, keepdims=True)
    )
    return (inner * scale_inv, jnp.sum(upstream * normed, axis=0), jnp.sum(upstream, axis=0))


def attend_forward(queries, keys_all, values_all, allowed):
    length = queries.shape[0]
    block_rows = min(512, length)
    pieces = []
    totals = []
    for start_row in range(0, length, block_rows):
        raw_scores = jnp.einsum(
            "qhd,khd->hqk",
            queries[start_row : start_row + block_rows],
            keys_all,
            preferred_element_type=jnp.float32,
        )
        scores = jnp.where(
            allowed[None, start_row : start_row + block_rows], raw_scores * 0.125, NEGATIVE
        )
        highest = jnp.max(scores, axis=-1, keepdims=True)
        logsum = highest + jnp.log(jnp.sum(jnp.exp(scores - highest), axis=-1, keepdims=True))
        weights = jnp.exp(scores - logsum).astype(jnp.bfloat16)
        pieces.append(
            jnp.einsum("hqk,khd->qhd", weights, values_all, preferred_element_type=jnp.float32)
        )
        totals.append(logsum)
    return (jnp.concatenate(pieces, axis=0), jnp.concatenate(totals, axis=1))


def attend_backward(queries, keys_all, values_all, allowed, logsum, upstream):
    length = queries.shape[0]
    block_rows = min(512, length)
    query_parts = []
    grad_keys = jnp.zeros(keys_all.shape, jnp.float32)
    grad_values = jnp.zeros(values_all.shape, jnp.float32)
    for start_row in range(0, length, block_rows):
        rows_query = queries[start_row : start_row + block_rows]
        rows_upstream = upstream[start_row : start_row + block_rows]
        raw_scores = jnp.einsum(
            "qhd,khd->hqk", rows_query, keys_all, preferred_element_type=jnp.float32
        )
        scores = jnp.where(
            allowed[None, start_row : start_row + block_rows], raw_scores * 0.125, NEGATIVE
        )
        probs = jnp.exp(scores - logsum[:, start_row : start_row + block_rows, :])
        probs_low = probs.astype(jnp.bfloat16)
        grad_probs = jnp.einsum(
            "qhd,khd->hqk", rows_upstream, values_all, preferred_element_type=jnp.float32
        )
        inner = jnp.sum(probs * grad_probs, axis=-1, keepdims=True)
        grad_scores = (probs * (grad_probs - inner) * 0.125).astype(jnp.bfloat16)
        query_parts.append(
            jnp.einsum("hqk,khd->qhd", grad_scores, keys_all, preferred_element_type=jnp.float32)
        )
        grad_keys = grad_keys + jnp.einsum(
            "hqk,qhd->khd", grad_scores, rows_query, preferred_element_type=jnp.float32
        )
        grad_values = grad_values + jnp.einsum(
            "hqk,qhd->khd", probs_low, rows_upstream, preferred_element_type=jnp.float32
        )
    return (jnp.concatenate(query_parts, axis=0), grad_keys, grad_values)


def row_forward(tokens_row, allowed, matrices, vector_rows):
    attend_matrix, merger_matrix, expand_matrix, shrink_matrix = matrices
    width = attend_matrix.shape[0]
    heads = width // HEAD_DIM
    length = tokens_row.shape[0]
    inputs = tokens_row.astype(jnp.float32)
    projected = jnp.dot(tokens_row, attend_matrix, preferred_element_type=jnp.float32).astype(
        jnp.bfloat16
    )
    queries = projected[:, :width].reshape(length, heads, HEAD_DIM)
    keys_all = projected[:, width : 2 * width].reshape(length, heads, HEAD_DIM)
    values_all = projected[:, 2 * width :].reshape(length, heads, HEAD_DIM)
    context, logsum = attend_forward(queries, keys_all, values_all, allowed)
    context_low = context.reshape(length, width).astype(jnp.bfloat16)
    branch = jnp.dot(context_low, merger_matrix, preferred_element_type=jnp.float32)
    first_out, first_normed, first_inv = norm_forward(
        vector_rows[0] * inputs + branch, vector_rows[1], vector_rows[2]
    )
    first_low = first_out.astype(jnp.bfloat16)
    hidden = jnp.dot(first_low, expand_matrix, preferred_element_type=jnp.float32)
    active_low = jax.nn.gelu(hidden).astype(jnp.bfloat16)
    second_sum = vector_rows[3] * first_out + jnp.dot(
        active_low, shrink_matrix, preferred_element_type=jnp.float32
    )
    result, second_normed, second_inv = norm_forward(second_sum, vector_rows[4], vector_rows[5])
    return dict(
        inputs=inputs,
        queries=queries,
        keys_all=keys_all,
        values_all=values_all,
        logsum=logsum,
        context_low=context_low,
        first_out=first_out,
        first_normed=first_normed,
        first_inv=first_inv,
        first_low=first_low,
        hidden=hidden,
        active_low=active_low,
        second_normed=second_normed,
        second_inv=second_inv,
        result=result,
    )


def row_backward(tokens_row, allowed, valid_slot, cotangent_row, matrices, vector_rows):
    attend_matrix, merger_matrix, expand_matrix, shrink_matrix = matrices
    width = attend_matrix.shape[0]
    heads = width // HEAD_DIM
    length = tokens_row.shape[0]
    saved = row_forward(tokens_row, allowed, matrices, vector_rows)
    upstream = cotangent_row.astype(jnp.float32) * valid_slot[:, None].astype(jnp.float32)
    grad_second, grad_gain_two, grad_shift_two = norm_backward(
        upstream, saved["second_normed"], saved["second_inv"], vector_rows[4]
    )
    grad_omega_two = jnp.sum(saved["first_out"] * grad_second, axis=0)
    second_low = grad_second.astype(jnp.bfloat16)
    shrink_grad = jnp.einsum(
        "tf,td->fd", saved["active_low"], second_low, preferred_element_type=jnp.float32
    )
    grad_active = jnp.einsum(
        "td,fd->tf", second_low, shrink_matrix, preferred_element_type=jnp.float32
    )
    gelu_value, gelu_pull = jax.vjp(jax.nn.gelu, saved["hidden"])
    hidden_low = gelu_pull(grad_active)[0].astype(jnp.bfloat16)
    expand_grad = jnp.einsum(
        "td,tf->df", saved["first_low"], hidden_low, preferred_element_type=jnp.float32
    )
    grad_first = (
        jnp.einsum("tf,df->td", hidden_low, expand_matrix, preferred_element_type=jnp.float32)
        + vector_rows[3] * grad_second
    )
    grad_first_sum, grad_gain_one, grad_shift_one = norm_backward(
        grad_first, saved["first_normed"], saved["first_inv"], vector_rows[1]
    )
    grad_omega_one = jnp.sum(saved["inputs"] * grad_first_sum, axis=0)
    branch_low = grad_first_sum.astype(jnp.bfloat16)
    merger_grad = jnp.einsum(
        "te,td->ed", saved["context_low"], branch_low, preferred_element_type=jnp.float32
    )
    context_grad = jnp.einsum(
        "td,ed->te", branch_low, merger_matrix, preferred_element_type=jnp.float32
    )
    context_grad = context_grad.astype(jnp.bfloat16).reshape(length, heads, HEAD_DIM)
    grad_query, grad_key, grad_value = attend_backward(
        saved["queries"],
        saved["keys_all"],
        saved["values_all"],
        allowed,
        saved["logsum"],
        context_grad,
    )
    projected_grad = jnp.concatenate(
        [
            grad_query.reshape(length, width),
            grad_key.reshape(length, width),
            grad_value.reshape(length, width),
        ],
        axis=1,
    ).astype(jnp.bfloat16)
    attend_grad = jnp.einsum(
        "td,te->de", tokens_row, projected_grad, preferred_element_type=jnp.float32
    )
    input_grad = vector_rows[0] * grad_first_sum + jnp.einsum(
        "te,de->td", projected_grad, attend_matrix, preferred_element_type=jnp.float32
    )
    vector_grad = jnp.stack(
        [
            grad_omega_one,
            grad_gain_one,
            grad_shift_one,
            grad_omega_two,
            grad_gain_two,
            grad_shift_two,
        ]
    )
    return ((attend_grad, merger_grad, expand_grad, shrink_grad, vector_grad), input_grad)


def shards(
    tokens,
    lengths,
    attend_weight,
    merger_weight,
    expand_weight,
    shrink_weight,
    vectors,
    attend_rows,
    attend_columns,
    merger_rows,
    merger_columns,
    expand_rows,
    expand_columns,
    shrink_rows,
    shrink_columns,
    vector_moments,
    cotangent,
):
    masters = (attend_weight, merger_weight, expand_weight, shrink_weight)
    gathered = (
        lax.all_gather(attend_weight.astype(jnp.bfloat16), "fsdp", axis=0, tiled=True),
        lax.all_gather(merger_weight.astype(jnp.bfloat16), "fsdp", axis=0, tiled=True),
        lax.all_gather(expand_weight.astype(jnp.bfloat16), "fsdp", axis=0, tiled=True),
        lax.all_gather(shrink_weight.astype(jnp.bfloat16), "fsdp", axis=0, tiled=True),
        lax.all_gather(vectors.astype(jnp.bfloat16), "fsdp", axis=1, tiled=True),
    )
    forward_mats = (gathered[0], gathered[1], gathered[2], gathered[3])
    forward_vecs = gathered[4].astype(jnp.float32)

    def forward_one(pieces):
        tokens_row, lengths_row = pieces
        allowed, valid_slot = layout(lengths_row, tokens_row.shape[0])
        return row_forward(tokens_row, allowed, forward_mats, forward_vecs)["result"].astype(
            jnp.bfloat16
        )

    block_output = lax.map(forward_one, (tokens, lengths))
    again = (
        lax.all_gather(attend_weight.astype(jnp.bfloat16), "fsdp", axis=0, tiled=True),
        lax.all_gather(merger_weight.astype(jnp.bfloat16), "fsdp", axis=0, tiled=True),
        lax.all_gather(expand_weight.astype(jnp.bfloat16), "fsdp", axis=0, tiled=True),
        lax.all_gather(shrink_weight.astype(jnp.bfloat16), "fsdp", axis=0, tiled=True),
        lax.all_gather(vectors.astype(jnp.bfloat16), "fsdp", axis=1, tiled=True),
    )
    backward_mats = (again[0], again[1], again[2], again[3])
    backward_vecs = again[4].astype(jnp.float32)

    def backward_one(running, pieces):
        tokens_row, lengths_row, cotangent_row = pieces
        allowed, valid_slot = layout(lengths_row, tokens_row.shape[0])
        row_grads, input_grad = row_backward(
            tokens_row, allowed, valid_slot, cotangent_row, backward_mats, backward_vecs
        )
        return (jax.tree.map(jnp.add, running, row_grads), input_grad)

    starting = tuple((jnp.zeros(matrix_item.shape, jnp.float32) for matrix_item in again))
    accumulated, input_gradient = lax.scan(backward_one, starting, (tokens, lengths, cotangent))
    paired = (
        lax.psum(accumulated[0].astype(jnp.bfloat16), "dp").astype(jnp.float32),
        lax.psum(accumulated[1].astype(jnp.bfloat16), "dp").astype(jnp.float32),
        lax.psum(accumulated[2].astype(jnp.bfloat16), "dp").astype(jnp.float32),
        lax.psum(accumulated[3].astype(jnp.bfloat16), "dp").astype(jnp.float32),
        lax.psum(accumulated[4].astype(jnp.bfloat16), "dp").astype(jnp.float32),
    )
    owned = (
        lax.psum_scatter(paired[0], "fsdp", scatter_dimension=0, tiled=True),
        lax.psum_scatter(paired[1], "fsdp", scatter_dimension=0, tiled=True),
        lax.psum_scatter(paired[2], "fsdp", scatter_dimension=0, tiled=True),
        lax.psum_scatter(paired[3], "fsdp", scatter_dimension=0, tiled=True),
        lax.psum_scatter(paired[4], "fsdp", scatter_dimension=1, tiled=True),
    )
    matrix_grads = owned[:4]
    vector_grad = owned[4]
    rows_old = (attend_rows, merger_rows, expand_rows, shrink_rows)
    cols_old = (attend_columns, merger_columns, expand_columns, shrink_columns)
    forget = 1.0 - float(STEP) ** (-0.8)
    devices = lax.axis_size("fsdp")
    fsdp_index = lax.axis_index("fsdp")
    row_totals = [float(weight_item.shape[0] * devices) for weight_item in masters]
    square_part = jnp.sum(vector_grad * vector_grad)
    for grad_item in matrix_grads:
        square_part = square_part + jnp.sum(grad_item * grad_item)
    weight_part = jnp.stack([jnp.sum(weight_item * weight_item) for weight_item in masters])
    vector_part = jnp.sum(vectors * vectors, axis=1)

    def spread(old_cols):
        whole = jnp.zeros((old_cols.shape[0] * devices,), jnp.float32)
        return lax.dynamic_update_slice_in_dim(
            whole, forget * old_cols, fsdp_index * old_cols.shape[0], 0
        )

    square_sum, weight_sum, vector_sum = lax.psum((square_part, weight_part, vector_part), "fsdp")
    clip = jnp.minimum(1.0, THRESHOLD / jnp.sqrt(square_sum))
    clipped = [clip * grad_item for grad_item in matrix_grads]
    new_rows = [
        forget * rows_old[slot_index]
        + (1.0 - forget) * jnp.mean(clipped[slot_index] * clipped[slot_index] + TINY_VALUE, axis=1)
        for slot_index in range(4)
    ]
    column_terms = [
        spread(cols_old[slot_index])
        + (1.0 - forget)
        / row_totals[slot_index]
        * jnp.sum(clipped[slot_index] * clipped[slot_index] + TINY_VALUE, axis=0)
        for slot_index in range(4)
    ]
    row_part = jnp.stack([jnp.sum(rows_item) for rows_item in new_rows])
    col_zero, col_one, col_two, col_three, row_sum = lax.psum(
        (column_terms[0], column_terms[1], column_terms[2], column_terms[3], row_part), "fsdp"
    )
    new_cols = [col_zero, col_one, col_two, col_three]
    global_norm = jnp.sqrt(square_sum)
    steps_raw = []
    for slot_index in range(4):
        estimate = (
            new_rows[slot_index][:, None]
            * new_cols[slot_index][None, :]
            / (row_sum[slot_index] / row_totals[slot_index])
        )
        steps_raw.append(clipped[slot_index] * lax.rsqrt(estimate))
    vector_clipped = clip * vector_grad
    vector_variance = forget * vector_moments + (1.0 - forget) * (
        vector_clipped * vector_clipped + TINY_VALUE
    )
    vector_step = vector_clipped * lax.rsqrt(vector_variance)
    step_part = jnp.stack([jnp.sum(step_item * step_item) for step_item in steps_raw])
    vector_step_part = jnp.sum(vector_step * vector_step, axis=1)
    step_sum, vector_step_sum = lax.psum((step_part, vector_step_part), "fsdp")
    results = []
    for slot_index in range(4):
        weight_item = masters[slot_index]
        count_all = row_totals[slot_index] * weight_item.shape[1]
        update = steps_raw[slot_index] / jnp.maximum(
            1.0, jnp.sqrt(step_sum[slot_index] / count_all) / UPDATE_LIMIT
        )
        stride = LEARN_RATE * jnp.maximum(0.001, jnp.sqrt(weight_sum[slot_index] / count_all))
        updated = weight_item - stride * update
        own_cols = lax.dynamic_slice_in_dim(
            new_cols[slot_index],
            fsdp_index * cols_old[slot_index].shape[0],
            cols_old[slot_index].shape[0],
        )
        results.extend(
            [
                clipped[slot_index],
                new_rows[slot_index],
                own_cols,
                updated,
                updated.astype(jnp.bfloat16),
            ]
        )
    vector_width = float(vectors.shape[1] * devices)
    vector_update = (
        vector_step
        / jnp.maximum(1.0, jnp.sqrt(vector_step_sum / vector_width) / UPDATE_LIMIT)[:, None]
    )
    vector_stride = LEARN_RATE * jnp.maximum(0.001, jnp.sqrt(vector_sum / vector_width))[:, None]
    vector_updated = vectors - vector_stride * vector_update
    return (
        block_output,
        input_gradient,
        global_norm,
        results[0],
        results[1],
        results[2],
        results[3],
        results[4],
        results[5],
        results[6],
        results[7],
        results[8],
        results[9],
        results[10],
        results[11],
        results[12],
        results[13],
        results[14],
        results[15],
        results[16],
        results[17],
        results[18],
        results[19],
        vector_clipped,
        vector_variance,
        vector_updated,
    )


def solution(mesh):
    in_specs = (
        P(("dp", "fsdp"), None, None),
        P(("dp", "fsdp"), None),
        P("fsdp", None),
        P("fsdp", None),
        P("fsdp", None),
        P("fsdp", None),
        P(None, "fsdp"),
        P("fsdp"),
        P("fsdp"),
        P("fsdp"),
        P("fsdp"),
        P("fsdp"),
        P("fsdp"),
        P("fsdp"),
        P("fsdp"),
        P(None, "fsdp"),
        P(("dp", "fsdp"), None, None),
    )
    out_specs = (
        P(("dp", "fsdp"), None, None),
        P(("dp", "fsdp"), None, None),
        P(),
        P("fsdp", None),
        P("fsdp"),
        P("fsdp"),
        P("fsdp", None),
        P("fsdp", None),
        P("fsdp", None),
        P("fsdp"),
        P("fsdp"),
        P("fsdp", None),
        P("fsdp", None),
        P("fsdp", None),
        P("fsdp"),
        P("fsdp"),
        P("fsdp", None),
        P("fsdp", None),
        P("fsdp", None),
        P("fsdp"),
        P("fsdp"),
        P("fsdp", None),
        P("fsdp", None),
        P(None, "fsdp"),
        P(None, "fsdp"),
        P(None, "fsdp"),
    )
    return jax.shard_map(shards, mesh=mesh, in_specs=in_specs, out_specs=out_specs, check_vma=False)
```

profile of v0, /device:TPU:0, one launch (start us, length us, event | category | flops | bytes accessed | tf_op | source)
XLA Modules:
  0.0 1116.4 jit_solution(6540638374536516023)
XLA Ops:
  19.3 42.9 %all-gather = bf16[16,32,6]{1,2,0:T(8,128)(2,1)S(1)} all-gather(bf16[1,32,6]{1,2,0:T(8,128)(2,1)S(1)} %get-tuple-element.309), channel_id=1, replica_groups=mesh['dp'=2,'fsdp'=16] {'fsdp'}, dimensions={0}, use_global_device_ids=true | all-gather | bytes 6528 | tf_op jit(solution)/shard_map/all_gather | solution.py:253
  63.8 41.4 %all_gather.22 = bf16[512,512]{1,0:T(8,128)(2,1)} all-gather(bf16[32,512]{1,0:T(8,128)(2,1)S(1)} %get-tuple-element.301), channel_id=1, replica_groups=mesh['dp'=2,'fsdp'=16] {'fsdp'}, dimensions={0}, use_global_device_ids=true | all-gather | bytes 557056 | tf_op jit(solution)/shard_map/all_gather | solution.py:250
  130.2 7.3 fusion.8
  137.5 8.0 exponential_reduce_fusion.1
  150.4 8.3 fusion.83
  168.3 31.0 %all-gather.9.cloned.1.call-done = bf16[2048,512]{1,0:T(8,128)(2,1)} async-done(((bf16[128,512]{1,0:T(8,128)(2,1)}), bf16[2048,512]{1,0:T(8,128)(2,1)}) %all-gather.9.cloned.1.call-update) | async-done | bytes 2097168 | tf_op jit(solution)/shard_map/all_gather | solution.py:252
  199.3 7.6 fusion.134
  213.6 7.7 fusion.28
  235.9 8.1 fusion.135
  244.0 29.6 %fusion.74 = bf16[512,8,64]{0,2,1:T(8,128)(2,1)} fusion(bf16[1024,8,64]{0,2,1:T(8,128)(2,1)S(1)} %bitcast.136, f32[8,512,1024]{2,1,0:T(8,128)} %fusion.135, f32[8,512,1024]{2,1,0:T(8,128)} %get-tuple-element.325, f32[8,512]{1,0:T(8,128)S(1)} %log_add_fusion.1, pred[512,1024]{1,0:T(8,128)(4,1)S(1)} %copy-done.15), kind=kOutput, calls=%fused_computation.91 | convolution fusion | flops 583275520 | bytes 35667968 | tf_op jit(solution)/shard_map/while/body/eval_jaxpr/hqk,khd->qhd/dot_general | solution.py:99
  273.6 31.4 %fusion.11 = f32[8,64,1024]{2,1,0:T(8,128)} fusion(bf16[512,8,64]{0,2,1:T(8,128)(2,1)} %bitcast.144, f32[8,512,1024]{2,1,0:T(8,128)} %fusion.135, f32[8,512,1024]{2,1,0:T(8,128)} %get-tuple-element.325, f32[8,512]{1,0:T(8,128)S(1)} %log_add_fusion.1, pred[512,1024]{1,0:T(8,128)(4,1)S(1)} %copy-done.15), kind=kOutput, calls=%fused_computation.18 | convolution fusion | flops 583013376 | bytes 36716544 | tf_op jit(solution)/shard_map/while/body/eval_jaxpr/hqk,qhd->khd/dot_general | solution.py:101
  305.0 8.4 fusion.33
  313.5 8.1 fusion.136
  327.4 28.7 %fusion.77 = bf16[512,8,64]{0,2,1:T(8,128)(2,1)S(1)} fusion(bf16[1024,8,64]{0,2,1:T(8,128)(2,1)S(1)} %bitcast.137, f32[8,512,1024]{2,1,0:T(8,128)} %fusion.136, f32[8,512,1024]{2,1,0:T(8,128)} %copy-done, f32[8,512]{1,0:T(8,128)S(1)} %log_add_fusion, pred[512,1024]{1,0:T(8,128)(4,1)S(1)} %copy-done.13), kind=kOutput, calls=%fused_computation.92 | convolution fusion | flops 583275520 | bytes 35667968 | tf_op jit(solution)/shard_map/while/body/eval_jaxpr/hqk,khd->qhd/dot_general | solution.py:99
  356.2 38.8 %add_convert_fusion.1 = bf16[8,64,1024]{2,1,0:T(8,128)(2,1)} fusion(f32[8,64,1024]{2,1,0:T(8,128)} %fusion.11, bf16[512,8,64]{0,2,1:T(8,128)(2,1)S(1)} %bitcast.143, f32[8,512,1024]{2,1,0:T(8,128)} %fusion.136, f32[8,512,1024]{2,1,0:T(8,128)} %copy-done, f32[8,512]{1,0:T(8,128)S(1)} %log_add_fusion, pred[512,1024]{1,0:T(8,128)(4,1)S(1)} %copy-done.13), kind=kOutput, calls=%fused_computation.72 | convolution fusion | flops 584061952 | bytes 37765120 | tf_op jit(solution)/shard_map/while/body/eval_jaxpr/hqk,qhd->khd/dot_general | solution.py:101
  404.2 27.5 %all-reduce.5.cloned.1.call-done = (bf16[512,1536]{0,1:T(8,128)(2,1)}, bf16[512,512]{1,0:T(8,128)(2,1)}, bf16[512,2048]{1,0:T(8,128)(2,1)}, bf16[2048,512]{1,0:T(8,128)(2,1)}) async-done(((bf16[512,1536]{0,1:T(8,128)(2,1)}, bf16[512,512]{1,0:T(8,128)(2,1)}, bf16[512,2048]{1,0:T(8,128)(2,1)}, bf16[2048,512]{1,0:T(8,128)(2,1)}), (bf16[512,1536]{0,1:T(8,128)(2,1)}, bf16[512,512]{1,0:T(8,128)(2,1)}, ...) | async-done | bytes 6291472 | tf_op jit(solution)/shard_map/psum | solution.py:287
  455.6 56.2 %reduce-scatter.16.cloned.1.call-done = f32[32,6]{1,0:T(8,128)} async-done(((f32[512,6]{1,0:T(8,128)}), f32[32,6]{1,0:T(8,128)}) %reduce-scatter.16.cloned.1.call-update) | async-done | bytes 784
  513.2 74.9 %reduce-scatter.10.cloned.1.call-done = f32[32,512]{1,0:T(8,128)} async-done(((f32[512,512]{1,0:T(8,128)}), f32[32,512]{1,0:T(8,128)}) %reduce-scatter.10.cloned.1.call-update) | async-done | bytes 65552 | tf_op jit(solution)/shard_map/reduce_scatter | solution.py:295
  589.5 131.1 %reduce-scatter.18.cloned.1.call-done = f32[32,1536]{1,0:T(8,128)} async-done(((f32[512,1536]{1,0:T(8,128)}), f32[32,1536]{1,0:T(8,128)}) %reduce-scatter.18.cloned.1.call-update) | async-done | bytes 196624
  724.6 92.8 %reduce-scatter.12.cloned.1.call-done = f32[32,2048]{1,0:T(8,128)} async-done(((f32[512,2048]{1,0:T(8,128)}), f32[32,2048]{1,0:T(8,128)}) %reduce-scatter.12.cloned.1.call-update) | async-done | bytes 262160 | tf_op jit(solution)/shard_map/reduce_scatter | solution.py:296
  819.7 94.8 %reduce-scatter.14.cloned.1.call-done = f32[128,512]{1,0:T(8,128)} async-done(((f32[2048,512]{1,0:T(8,128)}), f32[128,512]{1,0:T(8,128)}) %reduce-scatter.14.cloned.1.call-update) | async-done | bytes 262160 | tf_op jit(solution)/shard_map/reduce_scatter | solution.py:297
  919.9 40.5 %psum.110 = f32[]{:T(128)} all-reduce(f32[]{:T(128)S(6)} %add.285), channel_id=1, replica_groups=mesh['dp'=2,'fsdp'=16] {'fsdp'}, use_global_device_ids=true, to_apply=%region_38.39 | all-reduce | flops 1 | bytes 8 | tf_op jit(solution)/shard_map/psum | solution.py:320
  971.0 71.8 %all-reduce.1 = (f32[1536]{0:T(1024)S(1)}, f32[4]{0:T(128)S(1)}, f32[512]{0:T(512)S(1)}, f32[2048]{0:T(1024)S(1)}, f32[512]{0:T(512)S(1)}) all-reduce(f32[1536]{0:T(1024)S(1)} %add_dynamic-update-slice_fusion.3, f32[4]{0:T(128)S(1)} %pad_maximum_fusion.6, ...), channel_id=1, replica_groups=mesh['dp'=2,'fsdp'=16] {'fsdp'}, use_global_device_ids=true, to_apply=%region_41.42 | all-reduce | flops 4612 | bytes 36896 | tf_op jit(solution)/shard_map/psum | solution.py:336
  1054.9 36.7 %all-reduce = (f32[4]{0:T(128)S(1)}, f32[4]{0:T(128)S(1)}, f32[6]{0:T(128)S(1)}, f32[6]{0:T(128)S(1)}) all-reduce(f32[4]{0:T(128)S(1)} %pad_maximum_fusion.7, f32[4]{0:T(128)} %pad_maximum_fusion.5, f32[6]{0:T(128)S(1)} %get-tuple-element.268, f32[6]{0:T(128)} %get-tuple-element.308), channel_id=1, replica_groups=mesh['dp'=2,'fsdp'=16] {'fsdp'}, use_global_device_ids=true, to_apply=%region_65.66 | all-reduce | flops 20 | bytes 160 | tf_op jit(solution)/shard_map/psum | solution.py:356
  (255 shorter events, 154.7 us)
Async XLA Ops:
  7.2 101.3 %copy-start.28 = (bf16[1,1024,512]{2,1,0:T(8,128)(2,1)S(1)}, bf16[1,1024,512]{2,1,0:T(8,128)(2,1)}, u32[]{:S(2)}) copy-start(bf16[1,1024,512]{2,1,0:T(8,128)(2,1)} %param.17) | copy-start | bytes 3145732
  7.2 102.6 %all-gather.5.cloned.1.call-start = ((), (), s32[]{:S(2)}) async-start(), calls=%async_computation.5 | async-start | bytes 1671168 | tf_op jit(solution)/shard_map/all_gather | solution.py:249
  9.7 151.2 %all-gather.7.cloned.1.call-start = ((), (), s32[]{:S(2)}) async-start(), calls=%async_computation.6 | async-start | bytes 2228224 | tf_op jit(solution)/shard_map/all_gather | solution.py:251
  12.1 187.2 %all-gather.9.cloned.1.call-start = ((), (), s32[]{:S(2)}) async-start(), calls=%async_computation.7 | async-start | bytes 2228224 | tf_op jit(solution)/shard_map/all_gather | solution.py:252
  14.5 417.3 %all-reduce.5.cloned.1.call-start = ((), (), s32[]{:S(2)}) async-start(), calls=%async_computation.13 | async-start | bytes 12582912 | tf_op jit(solution)/shard_map/psum | solution.py:287
  400.7 111.1 %reduce-scatter.16.cloned.1.call-start = ((), (), s32[]{:S(2)}) async-start(), calls=%async_computation.11 | async-start | bytes 278528
  404.2 183.9 %reduce-scatter.10.cloned.1.call-start = ((), (), s32[]{:S(2)}) async-start(), calls=%async_computation.8 | async-start | bytes 1114112 | tf_op jit(solution)/shard_map/reduce_scatter | solution.py:295
  433.9 286.8 %reduce-scatter.18.cloned.1.call-start = ((), (), s32[]{:S(2)}) async-start(), calls=%async_computation.12 | async-start | bytes 3342336
  437.2 380.2 %reduce-scatter.12.cloned.1.call-start = ((), (), s32[]{:S(2)}) async-start(), calls=%async_computation.9 | async-start | bytes 4456448 | tf_op jit(solution)/shard_map/reduce_scatter | solution.py:296
  441.4 473.1 %reduce-scatter.14.cloned.1.call-start = ((), (), s32[]{:S(2)}) async-start(), calls=%async_computation.10 | async-start | bytes 4456448 | tf_op jit(solution)/shard_map/reduce_scatter | solution.py:297
  589.5 372.1 %copy-start.36 = (f32[32,512]{1,0:T(8,128)S(1)}, f32[32,512]{1,0:T(8,128)}, u32[]{:S(2)}) copy-start(f32[32,512]{1,0:T(8,128)} %reduce-scatter.10.cloned.1.call-done) | copy-start | bytes 196612
  589.5 372.2 %copy-start.45 = (f32[6,32]{1,0:T(8,128)S(1)}, f32[6,32]{1,0:T(8,128)}, u32[]{:S(2)}) copy-start(f32[6,32]{1,0:T(8,128)} %param.32) | copy-start | bytes 2308
  721.9 248.9 %copy-start.46 = (f32[32]{0:T(128)S(1)}, f32[32]{0:T(128)}, u32[]{:S(2)}) copy-start(f32[32]{0:T(128)} %param.31) | copy-start | bytes 388
  721.9 248.9 %copy-start.47 = (f32[32]{0:T(128)S(1)}, f32[32]{0:T(128)}, u32[]{:S(2)}) copy-start(f32[32]{0:T(128)} %param.27) | copy-start | bytes 388
  817.4 145.1 %copy-start.31 = (f32[32,2048]{1,0:T(8,128)S(1)}, f32[32,2048]{1,0:T(8,128)}, u32[]{:S(2)}) copy-start(f32[32,2048]{1,0:T(8,128)} %reduce-scatter.12.cloned.1.call-done) | copy-start | bytes 786436
  916.9 182.5 %copy-start.20 = (f32[32,1536]{0,1:T(8,128)S(1)}, f32[32,1536]{0,1:T(8,128)}, u32[]{:S(2)}) copy-start(f32[32,1536]{0,1:T(8,128)} %copy.124) | copy-start | bytes 589828
  961.4 142.3 %copy-start.26 = (f32[32,2048]{1,0:T(8,128)S(1)}, f32[32,2048]{1,0:T(8,128)}, u32[]{:S(2)}) copy-start(f32[32,2048]{1,0:T(8,128)} %param.21) | copy-start | bytes 786436
  961.6 143.7 %copy-start.21 = (f32[128,512]{1,0:T(8,128)}, f32[128,512]{1,0:T(8,128)S(1)}, u32[]{:S(2)}) copy-start(f32[128,512]{1,0:T(8,128)S(1)} %get-tuple-element.281) | copy-start | bytes 786436
  961.7 137.7 %copy-start.34 = (f32[32,512]{1,0:T(8,128)}, f32[32,512]{1,0:T(8,128)S(1)}, u32[]{:S(2)}) copy-start(f32[32,512]{1,0:T(8,128)S(1)} %get-tuple-element.275) | copy-start | bytes 196612
  962.6 144.5 %copy-start.22 = (f32[32,2048]{1,0:T(8,128)}, f32[32,2048]{1,0:T(8,128)S(1)}, u32[]{:S(2)}) copy-start(f32[32,2048]{1,0:T(8,128)S(1)} %get-tuple-element.278) | copy-start | bytes 786436
  964.0 135.5 %copy-start.41 = (f32[128]{0:T(128)}, f32[128]{0:T(128)S(1)}, u32[]{:S(2)}) copy-start(f32[128]{0:T(128)S(1)} %get-tuple-element.280) | copy-start | bytes 1540
  965.2 134.2 %copy-start.42 = (f32[32]{0:T(128)}, f32[32]{0:T(128)S(1)}, u32[]{:S(2)}) copy-start(f32[32]{0:T(128)S(1)} %get-tuple-element.277) | copy-start | bytes 388
  968.1 131.3 %copy-start.43 = (f32[32]{0:T(128)}, f32[32]{0:T(128)S(1)}, u32[]{:S(2)}) copy-start(f32[32]{0:T(128)S(1)} %get-tuple-element.331) | copy-start | bytes 388
  968.1 131.3 %copy-start.44 = (f32[32]{0:T(128)}, f32[32]{0:T(128)S(1)}, u32[]{:S(2)}) copy-start(f32[32]{0:T(128)S(1)} %get-tuple-element.272) | copy-start | bytes 388
  (41 other events, 797.9 us)
Sparse Core Ops, SparseCore 0:
  11.4 62.1 all-gather.4
  76.9 59.4 all-gather.6
  139.8 59.4 all-gather.8
  400.8 30.9 all-reduce.4
  434.5 77.2 reduce-scatter.15
  513.9 74.1 reduce-scatter.9
  593.8 126.8 reduce-scatter.17
  723.1 94.2 reduce-scatter.11
  819.8 94.7 reduce-scatter.13
where the time goes:
time: 1130 us; the launch traced here: 1120 us
  waiting for transfers between devices  508 us (45%)
  blocking collectives  236 us (21%)
  matrix products  235 us (21%)
  other arithmetic  74.9 us (7%)
  local copies, waits for them, and re-layouts  34 us (3%)
  between operations  28.2 us (2%)
    unnamed x11, waiting for transfers between devices  187 us
    reduce_scatter x1, waiting for transfers between devices, shards(): lax.psum_scatter(paired[3], 'fsdp', scatter_dimension=0, tiled=True)  94.8 us
    reduce_scatter x1, waiting for transfers between devices, shards(): lax.psum_scatter(paired[2], 'fsdp', scatter_dimension=0, tiled=True)  92.8 us
    reduce_scatter x1, waiting for transfers between devices, shards(): lax.psum_scatter(paired[1], 'fsdp', scatter_dimension=0, tiled=True)  74.9 us
    psum x1, blocking collectives, shards(): lax.psum((column_terms[0], column_terms[1], column_terms[2], column_terms...  71.8 us
    dot_general x2, matrix products, attend_backward(): jnp.einsum('hqk,qhd->khd', grad_scores, rows_query, preferred_element_typ...  70.3 us
    dot_general x2, matrix products, attend_backward(): jnp.einsum('hqk,khd->qhd', grad_scores, keys_all, preferred_element_type=...  58.3 us
    all_gather x1, blocking collectives, shards(): lax.all_gather(vectors.astype(jnp.bfloat16), 'fsdp', axis=1, tiled=True)  42.9 us
  transfers between devices with their start and end apart: 9, of which 7 were waited for; matrix products, arithmetic and copies ran while one was open for 9% of the time, Pallas kernels for 0%

commit v1 on v0

v1 whole, which is shorter than its diff:
```python
import functools

import jax
import jax.numpy as jnp
from jax import lax
from jax.experimental import pallas as pl
from jax.experimental.pallas import tpu as pltpu
from jax.sharding import PartitionSpec as P

F32 = jnp.float32
BF16 = jnp.bfloat16
HEAD_DIM = 64
STEP = 3
EPSILON = 1e-05
TINY_VALUE = 1e-30
NEGATIVE = -1e30
THRESHOLD = 1.0
UPDATE_LIMIT = 1.0
LEARN_RATE = 0.5
FORGET = 1.0 - float(STEP) ** (-0.8)
LOG2_E = 1.4426950408889634
GELU_A = 0.7978845608028654
GELU_B = 0.044715 * GELU_A

REACH = 256
QUERY_BLOCK = 256
TILE = 256
GROUP = 4
DP, FSDP = "dp", "fsdp"
ATTEND, MERGER, EXPAND, SHRINK = "attend", "merger", "expand", "shrink"
MATRICES = (ATTEND, MERGER, EXPAND, SHRINK)
MESH = pl.DeviceIdType.MESH
VMEM_LIMIT = 63 << 20


def dot_general(left, right, left_dim, right_dim):
    return lax.dot_general(
        left, right, (((left_dim,), (right_dim,)), ((), ())), preferred_element_type=F32
    )


def dot_nn(left, right):
    return dot_general(left, right, 1, 0)


def dot_nt(left, right):
    return dot_general(left, right, 1, 1)


def dot_tn(left, right):
    return dot_general(left, right, 0, 0)


def flat(value):
    return value.reshape(-1, value.shape[-1])


def fold_rows(value):
    return jnp.sum(value.reshape(value.shape[0] // 8, 8, value.shape[1]), axis=0)


def fold_lanes(row):
    total = row[:, :128]
    for start in range(128, row.shape[1], 128):
        total = total + row[:, start : start + 128]
    return total


def diagonal(size):
    return lax.broadcasted_iota(jnp.int32, (size, size), 0) == lax.broadcasted_iota(
        jnp.int32, (size, size), 1
    )


def column_of(row):
    size = row.shape[1]
    return jnp.sum(jnp.where(diagonal(size), row, 0.0), axis=1, keepdims=True)


def row_of(column):
    size = column.shape[0]
    return jnp.sum(jnp.where(diagonal(size), column, 0.0), axis=0, keepdims=True)


def lane_mean(value):
    return jnp.mean(value, axis=-1, keepdims=True)


def aligned(start, size):
    return pl.ds(pl.multiple_of(start, size), size)


def band(slots):
    pieces = []
    place = 0
    for first in range(0, slots, QUERY_BLOCK):
        low = max(0, first - REACH)
        high = first + QUERY_BLOCK
        pieces.append((first, low, high, place))
        place += high - low
    return pieces, place


def prepare(r):
    slots = r.tokens.shape[0]
    count = r.lengths.shape[1]
    for start in range(0, slots, TILE):
        r.tokens_t[:, start : start + TILE] = r.tokens[start : start + TILE, :].T
    lengths = r.lengths[...].astype(F32)
    rows = jnp.broadcast_to(lengths, (8, count)).astype(BF16)
    upto = lax.broadcasted_iota(jnp.int32, (count, count), 1) <= lax.broadcasted_iota(
        jnp.int32, (count, count), 0
    )
    ends = dot_nt(jnp.where(upto, 1.0, 0.0).astype(BF16), rows)[:, 0:1]
    places = lax.broadcasted_iota(jnp.int32, (count, slots), 1).astype(F32)
    ended = jnp.where(ends <= places, 1.0, 0.0).astype(BF16)
    begin = dot_nn(rows, ended)[0:1, :]
    total = jnp.sum(lengths, axis=1, keepdims=True)
    r.total[...] = jnp.broadcast_to(total, r.total.shape)
    slot = lax.broadcasted_iota(jnp.int32, (1, slots), 1).astype(F32)
    begin = jnp.where(slot < total, begin, slot)
    for first, low, high, place in band(slots)[0]:
        key = (lax.broadcasted_iota(jnp.int32, (high - low, QUERY_BLOCK), 0) + low).astype(F32)
        query = slot[:, first : first + QUERY_BLOCK]
        fits = (key >= begin[:, first : first + QUERY_BLOCK]) & (key <= query)
        r.mask[place : place + high - low, :] = jnp.where(fits, 1.0, 0.0).astype(BF16)


def project(r):
    width = r.tokens.shape[1]

    def tile(step, carry):
        columns = aligned(step * TILE, TILE)
        r.projected_t[columns, :] = dot_tn(flat(r.attend[..., columns]), r.tokens_t[...]).astype(
            BF16
        )
        return carry

    lax.fori_loop(0, 3 * width // TILE, tile, 0)

    def turn(step, carry):
        columns = aligned(step * TILE, TILE)
        r.key_value[:, columns] = r.projected_t[aligned(width + step * TILE, TILE), :].T
        return carry

    lax.fori_loop(0, 2 * width // TILE, turn, 0)


def beside_zeros(value, head):
    zeros = jnp.zeros_like(value)
    return jnp.concatenate([value, zeros] if head == 0 else [zeros, value], axis=0)


def attend_forward(r, hooks):
    slots, width = r.tokens.shape
    factor = HEAD_DIM ** -0.5 * LOG2_E

    def pair(step, carry):
        for at, hook in hooks:
            pl.when(step == at)(hook)
        start = pl.multiple_of(step * 128, 128)
        for first, low, high, place in band(slots)[0]:
            keys = r.key_value[low:high, pl.ds(start, 128)]
            fits = r.mask[place : place + high - low, :].astype(F32) > 0.5
            for head in (0, 1):
                mine = pl.ds(start + 64 * head, 64)
                queries = r.projected_t[mine, first : first + QUERY_BLOCK]
                scores = dot_nn(keys, beside_zeros(queries, head))
                scores = jnp.where(fits, scores * factor, NEGATIVE)
                highest = jnp.max(scores, axis=0, keepdims=True)
                weights = jnp.exp2(scores - highest)
                inverse = 1.0 / jnp.sum(weights, axis=0, keepdims=True)
                probs = (weights * inverse).astype(BF16)
                r.probs[2 * step + head, place : place + high - low, :] = probs
                values = r.projected_t[pl.ds(2 * width + start + 64 * head, 64), low:high]
                r.context_t[mine, first : first + QUERY_BLOCK] = dot_nn(values, probs).astype(BF16)
        return carry

    lax.fori_loop(0, width // 128, pair, 0)


def attend_backward(r, hooks):
    slots, width = r.tokens.shape
    scale = HEAD_DIM ** -0.5

    def pair(step, carry):
        for at, hook in hooks:
            pl.when(step == at)(hook)
        start = pl.multiple_of(step * 128, 128)
        for head in (0, 1):
            mine = pl.ds(start + 64 * head, 64)
            mine_keys = pl.ds(width + start + 64 * head, 64)
            mine_values = pl.ds(2 * width + start + 64 * head, 64)
            queries = r.projected_t[mine, :]
            keys_t = r.projected_t[mine_keys, :]
            upstream = r.d_context_t[mine, :]
            open_keys = None
            open_values = None
            for first, low, high, place in band(slots)[0]:
                values = r.key_value[low:high, pl.ds(width + start, 128)]
                arriving = upstream[:, first : first + QUERY_BLOCK]
                d_probs = dot_nn(values, beside_zeros(arriving, head))
                probs = r.probs[2 * step + head, place : place + high - low, :]
                wide = probs.astype(F32)
                inner = jnp.sum(wide * d_probs, axis=0, keepdims=True)
                d_scores = (wide * (d_probs - inner)).astype(BF16)
                r.projected_t[mine, first : first + QUERY_BLOCK] = (
                    dot_nn(keys_t[:, low:high], d_scores) * scale
                ).astype(BF16)
                d_keys = dot_nt(queries[:, first : first + QUERY_BLOCK], d_scores)
                d_values = dot_nt(arriving, probs)
                done = first - low
                if done:
                    r.projected_t[mine_keys, low:first] = (
                        (open_keys + d_keys[:, :done]) * scale
                    ).astype(BF16)
                    r.projected_t[mine_values, low:first] = (
                        open_values + d_values[:, :done]
                    ).astype(BF16)
                open_keys = d_keys[:, done:]
                open_values = d_values[:, done:]
            r.projected_t[mine_keys, slots - QUERY_BLOCK :] = (open_keys * scale).astype(BF16)
            r.projected_t[mine_values, slots - QUERY_BLOCK :] = open_values.astype(BF16)
        return carry

    lax.fori_loop(0, width // 128, pair, 0)


def feed_forward(r):
    slots, width = r.tokens.shape
    r.vector_sums[...] = jnp.zeros_like(r.vector_sums)

    def block(step, carry):
        rows = aligned(step * TILE, TILE)
        omega_one, gain_one, shift_one, omega_two, gain_two, shift_two = [
            r.vectors[place : place + 1, :] for place in range(6)
        ]
        inputs = r.tokens[rows, :].astype(F32)
        first_sum = omega_one * inputs + dot_tn(r.context_t[:, rows], flat(r.merger[...]))
        centered = first_sum - lane_mean(first_sum)
        first_inv = lax.rsqrt(lane_mean(centered * centered) + EPSILON)
        first_normed = centered * first_inv
        first_out = first_normed * gain_one + shift_one
        first_low = first_out.astype(BF16)
        r.first_t[:, rows] = first_low.T
        hidden = dot_nn(first_low, flat(r.expand[...]))
        square = hidden * hidden
        bend = jnp.tanh(hidden * (GELU_A + GELU_B * square))
        half = 0.5 * hidden
        lifted = 1.0 + bend
        active = (half * lifted).astype(BF16)
        r.slope[...] = 0.5 * lifted + half * (1.0 - bend * bend) * (GELU_A + 3 * GELU_B * square)
        r.active[rows, :] = active
        second_sum = omega_two * first_out + dot_nn(active, flat(r.shrink[...]))
        centered = second_sum - lane_mean(second_sum)
        second_inv = lax.rsqrt(lane_mean(centered * centered) + EPSILON)
        second_normed = centered * second_inv
        arriving = r.cotangent[rows, :].astype(F32)
        r.result[rows, :] = (second_normed * gain_two + shift_two).astype(BF16)
        place = (lax.broadcasted_iota(jnp.int32, (TILE, 1), 0) + step * TILE).astype(F32)
        upstream = arriving * jnp.where(place < r.total[0:1, 0:1], 1.0, 0.0)
        scaled = upstream * gain_two
        d_second = second_inv * (
            scaled - lane_mean(scaled) - second_normed * lane_mean(scaled * second_normed)
        )
        r.vector_sums[4] += fold_rows(upstream * second_normed)
        r.vector_sums[5] += fold_rows(upstream)
        r.vector_sums[3] += fold_rows(first_out * d_second)
        second_low = d_second.astype(BF16)
        r.d_second_t[:, rows] = second_low.T
        d_hidden = (dot_nt(second_low, flat(r.shrink[...])) * r.slope[...]).astype(BF16)
        r.d_hidden[rows, :] = d_hidden
        d_first = dot_nt(d_hidden, flat(r.expand[...])) + omega_two * d_second
        r.vector_sums[1] += fold_rows(d_first * first_normed)
        r.vector_sums[2] += fold_rows(d_first)
        scaled = d_first * gain_one
        d_first_sum = first_inv * (
            scaled - lane_mean(scaled) - first_normed * lane_mean(scaled * first_normed)
        )
        r.vector_sums[0] += fold_rows(inputs * d_first_sum)
        r.straight[rows, :] = omega_one * d_first_sum
        branch_low = d_first_sum.astype(BF16)
        r.d_branch[rows, :] = branch_low
        r.d_context_t[:, rows] = dot_nt(flat(r.merger[...]), branch_low).astype(BF16)
        return carry

    lax.fori_loop(0, slots // TILE, block, 0)


def vector_total(r):
    rows = [jnp.sum(r.vector_sums[place], axis=0, keepdims=True) for place in range(6)]
    return jnp.concatenate(rows + [jnp.zeros((2, rows[0].shape[1]), F32)], axis=0)


def by_columns(columns, store):
    def tile(step, carry):
        store(step)
        return carry

    lax.fori_loop(0, columns // TILE, tile, 0)


def put_tile(ref, columns, value):
    ref[..., columns] = value.astype(ref.dtype).reshape(ref.shape[:-1] + (value.shape[1],))


def shrink_gradient(r):
    width, wide = r.tokens.shape[1], r.active.shape[1]
    if len(r.g_shrink.shape) == 2:

        def store(step):
            columns = aligned(step * TILE, TILE)
            r.g_shrink[:, columns] = dot_nn(r.d_second_t[...], r.active[:, columns]).astype(
                r.g_shrink.dtype
            )

        by_columns(wide, store)
        return
    owned = r.g_shrink.shape[-1]
    per_tile = max(1, TILE // owned)
    span = owned * per_tile

    def tile(step, carry):
        value = dot_nn(r.d_second_t[...], r.active[:, aligned(step * span, span)]).astype(BF16)
        for piece in range(per_tile):
            owner = step * per_tile + piece
            r.g_shrink[owner // GROUP, lax.rem(owner, GROUP)] = value[
                :, piece * owned : (piece + 1) * owned
            ].reshape(2, width // 2, owned)
        return carry

    lax.fori_loop(0, wide // span, tile, 0)


def expand_gradient(r):
    def store(step):
        columns = aligned(step * TILE, TILE)
        put_tile(r.g_expand, columns, dot_nn(r.first_t[...], r.d_hidden[:, columns]))

    by_columns(r.active.shape[1], store)


def merger_gradient(r):
    def store(step):
        columns = aligned(step * TILE, TILE)
        put_tile(r.g_merger, columns, dot_nn(r.context_t[...], r.d_branch[:, columns]))

    by_columns(r.tokens.shape[1], store)


def attend_gradient(r):
    def store(step):
        columns = aligned(step * TILE, TILE)
        put_tile(r.g_attend, columns, dot_nt(r.tokens_t[...], r.projected_t[columns, :]))

    by_columns(3 * r.tokens.shape[1], store)


def input_gradient(r):
    def tile(step, carry):
        rows = aligned(step * TILE, TILE)
        r.straight[rows, :] += dot_nn(flat(r.attend[...]), r.projected_t[:, rows]).T
        return carry

    lax.fori_loop(0, r.tokens.shape[0] // TILE, tile, 0)


def row_scratch(slots, width, wide):
    packed = band(slots)[1]
    heads = width // HEAD_DIM
    return dict(
        tokens_t=pltpu.VMEM((width, slots), BF16),
        mask=pltpu.VMEM((packed, QUERY_BLOCK), BF16),
        total=pltpu.VMEM((8, 128), F32),
        projected_t=pltpu.VMEM((3 * width, slots), BF16),
        key_value=pltpu.VMEM((slots, 2 * width), BF16),
        probs=pltpu.VMEM((heads, packed, QUERY_BLOCK), BF16),
        context_t=pltpu.VMEM((width, slots), BF16),
        d_context_t=pltpu.VMEM((width, slots), BF16),
        active=pltpu.VMEM((slots, wide), BF16),
        d_hidden=pltpu.VMEM((slots, wide), BF16),
        first_t=pltpu.VMEM((width, slots), BF16),
        d_second_t=pltpu.VMEM((width, slots), BF16),
        vector_sums=pltpu.VMEM((6, 8, width), F32),
        slope=pltpu.VMEM((TILE, wide), F32),
    )


class Refs:
    def __init__(self, names, refs):
        for name, ref in zip(names, refs, strict=True):
            setattr(self, name, ref)


def spread_rows(width, columns_of):
    places = {}
    start = 0
    for name in MATRICES:
        places[name] = (start, columns_of[name] // width)
        start += columns_of[name] // width
    return places, start


def joined(ref, start, count):
    return jnp.concatenate([ref[place : place + 1, :] for place in range(start, start + count)], 1)


def split_into(ref, start, row, width):
    for piece in range(row.shape[1] // width):
        ref[start + piece : start + piece + 1, :] = row[:, piece * width : (piece + 1) * width]


def scalar_sum(value):
    return jnp.sum(jnp.sum(value, axis=1, keepdims=True), axis=0, keepdims=True)


def clip_of(columns_ref, places, vector_gradient):
    squares = {
        name: scalar_sum(joined(columns_ref, *places[name])) for name in MATRICES
    }
    total = scalar_sum(vector_gradient * vector_gradient)
    for name in MATRICES:
        total = total + squares[name]
    norm = jnp.sqrt(total)
    return norm, jnp.minimum(1.0, THRESHOLD / norm), squares


def factored_step(name, gradient, rows_old, columns_ref, early_ref, places, clip, squares, rows_all):
    start, count = places[name]
    wide = gradient.shape[1]
    power = clip * clip
    row_mean = jnp.sum(gradient * gradient, axis=1, keepdims=True) * (1.0 / wide)
    new_rows = FORGET * column_of(rows_old) + (1.0 - FORGET) * (power * row_mean + TINY_VALUE)
    new_columns = FORGET * joined(early_ref, start, count) + (1.0 - FORGET) * (
        power * (joined(columns_ref, start, count) * (1.0 / rows_all)) + TINY_VALUE
    )
    old = early_ref[ROW_SUMS : ROW_SUMS + 1, :]
    at = MATRICES.index(name) * 128
    old_mean = jnp.sum(old[:, at : at + 128], axis=1, keepdims=True) * (1.0 / rows_all)
    mean = FORGET * old_mean + (1.0 - FORGET) * (
        power * (squares[name] * (1.0 / (rows_all * wide))) + TINY_VALUE
    )
    clipped = clip * gradient
    step = clipped * lax.rsqrt(new_rows * new_columns * (1.0 / mean))
    return clipped, new_rows, new_columns, step


def vector_steps(gradient, moments, clip):
    clipped = clip * gradient
    variance = FORGET * moments + (1.0 - FORGET) * (clipped * clipped + TINY_VALUE)
    return clipped, variance, clipped * lax.rsqrt(variance)


SQUARES = 9
ROW_SUMS = 10
VECTORS = 16
MOMENTS = 24
EARLY_ROWS = 32
COLUMN_ROWS = 16


def shard_kernel(layout_sizes, names, *refs):
    outer, width, wide = layout_sizes
    r = Refs(names, refs)
    r.result = r.cotangent
    r.d_branch = r.tokens
    core = lax.axis_index(DP)
    chip = lax.axis_index(FSDP)
    far = chip // GROUP
    near = lax.rem(chip, GROUP)
    sibling = (1 - core, chip)
    near_steps = range(1, GROUP)
    far_steps = range(1, outer)

    def at_near(step):
        return jnp.bitwise_xor(near, step)

    def at_far(step):
        return lax.rem(far + step, outer)

    def from_far(step):
        return lax.rem(far + outer - step, outer)

    def near_device(step):
        return (core, far * GROUP + at_near(step))

    def far_device(step):
        return (core, at_far(step) * GROUP + near)

    def remote(source, target, device, sends, receives, index):
        return pltpu.make_async_remote_copy(
            src_ref=source,
            dst_ref=target,
            send_sem=sends.at[index],
            recv_sem=receives.at[index],
            device_id=device,
            device_id_type=MESH,
        )

    def start(copy):
        copy.start()

    def local(source, target, index):
        return pltpu.make_async_copy(source, target, r.local_sems.at[index])

    load_tokens = local(r.tokens_in, r.tokens, 0)
    load_cotangent = local(r.cotangent_in, r.cotangent, 1)
    load_tokens.start()
    load_cotangent.start()

    barrier = pltpu.get_barrier_semaphore()
    for step in near_steps:
        pl.semaphore_signal(barrier, inc=1, device_id=near_device(step), device_id_type=MESH)
    for step in far_steps:
        pl.semaphore_signal(barrier, inc=1, device_id=far_device(step), device_id_type=MESH)
    pl.semaphore_signal(barrier, inc=1, device_id=sibling, device_id_type=MESH)
    pl.semaphore_wait(barrier, len(near_steps) + len(far_steps) + 1)


    class Sum:
        def __init__(self, name):
            self.near = getattr(r, name + "_near")
            self.far = getattr(r, name + "_far")
            self.sends = getattr(r, name + "_sends")
            self.receives = getattr(r, name + "_receives")

        def begin(self, value=None):
            if value is not None:
                self.near[near] = value
            for step in near_steps:
                start(
                    remote(
                        self.near.at[near], self.near.at[near], near_device(step),
                        self.sends, self.receives, step - 1,
                    )
                )

        def turn(self):
            for step in near_steps:
                slot = self.near.at[at_near(step)]
                remote(
                    slot, slot, near_device(step), self.sends, self.receives, step - 1
                ).wait_recv()
            self.far[far] = jnp.sum(self.near[...], axis=0)
            for step in far_steps:
                start(
                    remote(
                        self.far.at[far], self.far.at[far], far_device(step),
                        self.sends, self.receives, GROUP + step - 1,
                    )
                )

        def end(self):
            for step in far_steps:
                slot = self.far.at[from_far(step)]
                remote(
                    slot, slot, far_device(step), self.sends, self.receives, GROUP + step - 1
                ).wait_recv()
            return jnp.sum(self.far[...], axis=0)


    class Gather:
        def __init__(self, name):
            self.held = getattr(r, name)
            self.sends = getattr(r, name + "_sends")
            self.receives = getattr(r, name + "_receives")

        def far_copy(self, step, slot):
            ref = self.held.at[slot, near, core]
            return remote(ref, ref, far_device(step), self.sends, self.receives, step - 1)

        def near_copy(self, step, back, slot):
            ref = self.held.at[slot, near if back is None else back, core]
            index = outer + (step - 1) * outer
            return remote(ref, ref, near_device(step), self.sends, self.receives, index)

        def cross(self, step, half, whose):
            ref = self.held.at[:, whose, half]
            index = outer * GROUP + step
            return remote(ref, ref, sibling, self.sends, self.receives, index)

        def near_piece(self, step, hop, whose, half):
            ref = self.held.at[from_far(hop) if hop else far, whose, half]
            index = outer + (step - 1) * outer + hop
            return remote(ref, ref, near_device(step), self.sends, self.receives, index)

        def place(self, shard):
            rows = shard.shape[0] // 2
            mine = shard[pl.ds(pl.multiple_of(core * rows, rows), rows), :]
            self.held[far, near, core] = mine.astype(BF16)

        def begin(self):
            for step in far_steps:
                start(self.far_copy(step, far))
            for step in near_steps:
                start(self.near_piece(step, 0, near, core))

        def turn(self):
            for hop in far_steps:
                self.far_copy(hop, from_far(hop)).wait_recv()
                for step in near_steps:
                    start(self.near_piece(step, hop, near, core))
            start(self.cross(0, core, near))

        def pass_on(self):
            for step in near_steps:
                for hop in range(outer):
                    self.near_piece(step, hop, at_near(step), core).wait_recv()
                start(self.cross(step, core, at_near(step)))

        def end(self):
            for step in range(GROUP):
                self.cross(step, 1 - core, at_near(step) if step else near).wait_recv()


    class Reduce:
        def __init__(self, name):
            for part in ("g", "pair", "near", "far", "done"):
                setattr(self, part, getattr(r, part + "_" + name))
            self.sends = getattr(r, "sum_" + name + "_sends")
            self.receives = getattr(r, "sum_" + name + "_receives")

        def pair_copy(self):
            return remote(
                self.g.at[:, :, 1 - core], self.pair, sibling, self.sends, self.receives, 0
            )

        def near_copy(self, step):
            return remote(
                self.pair.at[:, at_near(step)], self.near.at[step - 1], near_device(step),
                self.sends, self.receives, step,
            )

        def far_copy(self, step):
            return remote(
                self.pair.at[at_far(step), near], self.far.at[step - 1], far_device(step),
                self.sends, self.receives, GROUP + step - 1,
            )

        def done_copy(self, half):
            ref = self.done.at[half]
            return remote(ref, ref, sibling, self.sends, self.receives, GROUP + outer)

        def begin(self):
            start(self.pair_copy())

        def turn(self):
            self.pair_copy().wait_recv()

            def block(step, carry):
                both = self.g[step, :, core].astype(F32) + self.pair[step].astype(F32)
                self.pair[step] = both.astype(BF16)
                return carry

            lax.fori_loop(0, outer, block, 0)
            for step in near_steps:
                start(self.near_copy(step))

        def pass_on(self):
            for step in near_steps:
                self.near_copy(step).wait_recv()

            def block(step, carry):
                total = self.pair[step, near].astype(F32)
                for other in near_steps:
                    total = total + self.near[other - 1, step].astype(F32)
                self.pair[step, near] = total.astype(BF16)
                return carry

            lax.fori_loop(0, outer, block, 0)
            for step in far_steps:
                start(self.far_copy(step))

        def collect(self):
            for step in far_steps:
                self.far_copy(step).wait_recv()
            total = self.pair[far, near].astype(F32)
            for step in far_steps:
                total = total + self.far[step - 1].astype(F32)
            self.done[core] = total
            start(self.done_copy(core))

        def end(self):
            self.done_copy(1 - core).wait_recv()

    early = Sum("early")
    vector_sum = Sum("vector")
    column_sum = Sum("column")
    step_sum = Sum("step")
    gathers = {name: Gather(name) for name in MATRICES}
    sums = {name: Reduce(name) for name in MATRICES}
    shards = {name: getattr(r, name + "_weight") for name in MATRICES}

    gathers[ATTEND].place(shards[ATTEND])
    gathers[ATTEND].begin()


    columns_of = {name: getattr(r, name + "_columns").shape[1] * outer * GROUP for name in MATRICES}
    places, _ = spread_rows(width, columns_of)
    r.early_own[...] = jnp.zeros_like(r.early_own)
    r.spread[...] = jnp.zeros_like(r.spread)
    for name in MATRICES:
        row, count = places[name]
        own = getattr(r, name + "_columns")
        size = own.shape[1]
        if count == 1:
            r.early_own[row : row + 1, 0:size] = own[...]
        else:
            r.spread[0:1, 0:size] = own[...]
            whole = pltpu.roll(r.spread[:, : columns_of[name]], chip * size, 1)[0:1, :]
            split_into(r.early_wide, row, whole, width)
            r.spread[0:1, 0:size] = jnp.zeros_like(own)
        at = MATRICES.index(name) * 128
        shard = shards[name][...]
        r.early_wide[SQUARES : SQUARES + 1, at : at + 128] = fold_lanes(
            jnp.sum(fold_rows(shard * shard), axis=0, keepdims=True)
        )
        rows_old = getattr(r, name + "_rows")
        sums_row = jnp.broadcast_to(jnp.sum(rows_old[...], axis=1, keepdims=True), (1, 128))
        first_lane = lax.broadcasted_iota(jnp.int32, (1, 128), 1) == 0
        r.early_wide[ROW_SUMS : ROW_SUMS + 1, at : at + 128] = jnp.where(first_lane, sums_row, 0.0)
    thin = r.vectors_own.shape[1]
    r.early_own[VECTORS : VECTORS + 6, 0:thin] = r.vectors_own[...]
    r.early_own[MOMENTS : MOMENTS + 6, 0:thin] = r.moments_own[...]
    narrow = pltpu.roll(r.early_own[...], chip * thin, 1)
    kind = lax.broadcasted_iota(jnp.int32, narrow.shape, 0)
    taken = kind >= VECTORS
    for name in MATRICES:
        row, count = places[name]
        if count == 1:
            taken = taken | (kind == row)
    filled = kind <= ROW_SUMS
    early.begin(
        jnp.where(taken, narrow, jnp.where(filled, r.early_wide[...], 0.0))
    )


    for name in (MERGER, EXPAND, SHRINK):
        gathers[name].place(shards[name])
    load_tokens.wait()
    prepare(r)
    gathers[ATTEND].turn()
    gathers[MERGER].begin()
    gathers[EXPAND].begin()
    early.turn()
    gathers[ATTEND].pass_on()
    gathers[SHRINK].begin()
    gathers[ATTEND].end()
    project(r)
    gathers[MERGER].turn()
    gathers[EXPAND].turn()

    def second_hook():
        gathers[SHRINK].turn()

    def third_hook():
        gathers[MERGER].pass_on()

    attend_forward(r, ((1, second_hook), (2, third_hook)))
    gathers[EXPAND].pass_on()
    gathers[SHRINK].pass_on()
    r.early[...] = early.end()
    r.vectors[...] = r.early[VECTORS : VECTORS + 8, :].astype(BF16).astype(F32)
    for name in (MERGER, EXPAND, SHRINK):
        gathers[name].end()
    load_cotangent.wait()
    feed_forward(r)
    store_result = local(r.result, r.result_out, 0)
    store_result.start()


    r.vector_pair[core] = vector_total(r)
    vector_copy = remote(
        r.vector_pair.at[core], r.vector_pair.at[core], sibling,
        r.vector_sends, r.vector_receives, GROUP + outer,
    )
    vector_copy.start()
    shrink_gradient(r)
    sums[SHRINK].begin()
    expand_gradient(r)
    sums[EXPAND].begin()
    sums[SHRINK].turn()
    merger_gradient(r)
    sums[MERGER].begin()
    sums[EXPAND].turn()
    remote(
        r.vector_pair.at[1 - core], r.vector_pair.at[1 - core], sibling,
        r.vector_sends, r.vector_receives, GROUP + outer,
    ).wait_recv()
    vector_sum.begin(r.vector_pair[0] + r.vector_pair[1])

    def merger_hook():
        sums[MERGER].turn()
        vector_sum.turn()

    def shrink_hook():
        sums[SHRINK].pass_on()

    attend_backward(r, ((1, merger_hook), (3, shrink_hook)))
    attend_gradient(r)
    sums[ATTEND].begin()
    sums[EXPAND].pass_on()
    sums[ATTEND].turn()
    sums[MERGER].pass_on()
    input_gradient(r)
    store_input = local(r.straight, r.input_out, 1)
    store_input.start()
    r.vector_out[...] = vector_sum.end()
    sums[SHRINK].collect()
    sums[EXPAND].collect()
    sums[ATTEND].pass_on()
    sums[MERGER].collect()
    sums[ATTEND].collect()


    r.column_near[near] = jnp.zeros(r.column_near.shape[1:], F32)
    grads = {}
    for name in (SHRINK, EXPAND, MERGER, ATTEND):
        sums[name].end()
        if name == SHRINK:
            whole = flat(r.done_shrink[...]).T
        else:
            whole = flat(getattr(r, "done_" + name)[...])
        grads[name] = whole
        getattr(r, "out_" + name)[...] = whole
        row, _ = places[name]
        squares = jnp.sum(whole * whole, axis=0, keepdims=True)
        split_into(r.column_near.at[near], row, squares, width)
    column_sum.begin()
    column_sum.turn()
    r.column_out[...] = column_sum.end()
    r.early_out[...] = r.early[...]
    norm, clip, squares = clip_of(r.column_out, places, r.vector_out[...])
    for name in MATRICES:
        rows_all = float(getattr(r, name + "_rows").shape[1] * outer * GROUP)
        _, _, _, step = factored_step(
            name, grads[name], getattr(r, name + "_rows")[...], r.column_out, r.early, places,
            clip, squares, rows_all,
        )
        at = MATRICES.index(name)
        r.step_near[near, at : at + 1, :] = fold_lanes(
            jnp.sum(step * step, axis=0, keepdims=True)
        )
    r.step_near[near, 4:8, :] = jnp.zeros((4, 128), F32)
    step_sum.begin()
    step_sum.turn()
    r.step_out[...] = step_sum.end()


    for name in MATRICES:
        gather, total = gathers[name], sums[name]
        for step in far_steps:
            gather.far_copy(step, far).wait_send()
            total.far_copy(step).wait_send()
        for step in near_steps:
            for hop in range(outer):
                gather.near_piece(step, hop, near, core).wait_send()
            total.near_copy(step).wait_send()
        for step in range(GROUP):
            gather.cross(step, core, at_near(step) if step else near).wait_send()
        total.pair_copy().wait_send()
        total.done_copy(core).wait_send()
    for small in (early, vector_sum, column_sum, step_sum):
        for step in near_steps:
            slot = small.near.at[near]
            remote(
                slot, slot, near_device(step), small.sends, small.receives, step - 1
            ).wait_send()
        for step in far_steps:
            slot = small.far.at[far]
            remote(
                slot, slot, far_device(step), small.sends, small.receives, GROUP + step - 1
            ).wait_send()
    vector_copy.wait_send()
    store_result.wait()
    store_input.wait()


def update_kernel(layout_sizes, names, *refs):
    outer, width, wide = layout_sizes
    r = Refs(names, refs)
    chip = lax.axis_index(FSDP)
    columns_of = {name: getattr(r, name + "_columns").shape[1] * outer * GROUP for name in MATRICES}
    places, _ = spread_rows(width, columns_of)
    copies = [
        pltpu.make_async_copy(r.result_in, r.block_output, r.sems.at[0]),
        pltpu.make_async_copy(r.input_in, r.input_gradient, r.sems.at[1]),
    ]
    for copy in copies:
        copy.start()
    vector_gradient = r.vector_sum[...]
    norm, clip, squares = clip_of(r.column_sum, places, vector_gradient)
    r.global_norm[...] = norm
    for name in MATRICES:
        weight = getattr(r, name + "_weight")[...]
        rows_all = float(weight.shape[0] * outer * GROUP)
        count = rows_all * weight.shape[1]
        clipped, new_rows, new_columns, step = factored_step(
            name, getattr(r, name + "_sum")[...], getattr(r, name + "_rows")[...], r.column_sum,
            r.early, places, clip, squares, rows_all,
        )
        at = MATRICES.index(name)
        step_square = jnp.sum(r.step_sum[at : at + 1, :], axis=1, keepdims=True)
        weight_square = jnp.sum(
            r.early[SQUARES : SQUARES + 1, at * 128 : at * 128 + 128], axis=1, keepdims=True
        )
        shrunk = jnp.maximum(1.0, jnp.sqrt(step_square * (1.0 / count)) * (1.0 / UPDATE_LIMIT))
        stride = LEARN_RATE * jnp.maximum(0.001, jnp.sqrt(weight_square * (1.0 / count)))
        updated = weight - (stride / shrunk) * step
        getattr(r, name + "_gradient")[...] = clipped
        getattr(r, name + "_updated")[...] = updated
        getattr(r, name + "_bfloat")[...] = updated.astype(BF16)
        getattr(r, name + "_newrows")[...] = row_of(new_rows)
        size = getattr(r, name + "_newcols").shape[1]
        wide_row = jnp.broadcast_to(new_columns, (8, new_columns.shape[1]))
        own = pltpu.roll(wide_row, lax.rem(new_columns.shape[1] - chip * size, columns_of[name]), 1)
        getattr(r, name + "_newcols")[...] = own[0:1, 0:size]
    vectors = r.early[VECTORS : VECTORS + 8, :]
    clipped, variance, step = vector_steps(
        vector_gradient, r.early[MOMENTS : MOMENTS + 8, :], clip
    )
    shrunk = jnp.maximum(1.0, jnp.sqrt(lane_mean(step * step)) * (1.0 / UPDATE_LIMIT))
    stride = LEARN_RATE * jnp.maximum(0.001, jnp.sqrt(lane_mean(vectors * vectors)))
    updated = vectors - stride * (step / shrunk)
    thin = r.vector_updated.shape[1]
    turn = lax.rem(width - chip * thin, width)
    for ref, value in (
        (r.vector_gradient, clipped),
        (r.vector_variance, variance),
        (r.vector_updated, updated),
    ):
        ref[...] = pltpu.roll(value, turn, 1)[0:6, 0:thin]
    for copy in copies:
        copy.wait()


def in_vmem():
    return pl.BlockSpec(memory_space=pltpu.VMEM)


def anywhere():
    return pl.BlockSpec(memory_space=pl.ANY)


def call(kernel, sizes, inputs, outputs, scratch, held, params, name):
    names = list(inputs) + list(outputs) + list(scratch)
    results = pl.pallas_call(
        functools.partial(kernel, sizes, names),
        in_specs=[anywhere() if key in held else in_vmem() for key in inputs],
        out_specs=[anywhere() if key in held else in_vmem() for key in outputs],
        out_shape=list(outputs.values()),
        scratch_shapes=list(scratch.values()),
        compiler_params=params,
        name=name,
    )(*inputs.values())
    return dict(zip(outputs, results, strict=True))


def staged_shards(devices, tokens, lengths, weights, vectors, rows, columns, moments, cotangent):
    outer = devices // GROUP
    slots, width = tokens.shape[1:]
    wide = weights[EXPAND].shape[1]
    sizes = (outer, width, wide)
    shape = jax.ShapeDtypeStruct
    row_in = {name + "_rows": rows[name].reshape(1, -1) for name in MATRICES}
    column_in = {name + "_columns": columns[name].reshape(1, -1) for name in MATRICES}
    weight_in = {name + "_weight": weights[name] for name in MATRICES}
    inputs = dict(
        tokens_in=tokens[0], lengths=lengths, cotangent_in=cotangent[0],
        vectors_own=vectors, moments_own=moments, **weight_in, **row_in, **column_in,
    )
    outputs = dict(
        result_out=shape((slots, width), BF16),
        input_out=shape((slots, width), F32),
        vector_out=shape((8, width), F32),
        early_out=shape((EARLY_ROWS, width), F32),
        column_out=shape((COLUMN_ROWS, width), F32),
        step_out=shape((8, 128), F32),
        **{"out_" + name: shape(weights[name].shape, F32) for name in MATRICES},
    )
    scratch = row_scratch(slots, width, wide)
    scratch.update(
        tokens=pltpu.VMEM((slots, width), BF16),
        cotangent=pltpu.VMEM((slots, width), BF16),
        straight=pltpu.VMEM((slots, width), F32),
        vectors=pltpu.VMEM((8, width), F32),
        early=pltpu.VMEM((EARLY_ROWS, width), F32),
        early_own=pltpu.VMEM((EARLY_ROWS, width), F32),
        early_wide=pltpu.VMEM((EARLY_ROWS, width), F32),
        spread=pltpu.VMEM((8, wide), F32),
        vector_pair=pltpu.VMEM((2, 8, width), F32),
        local_sems=pltpu.SemaphoreType.DMA((2,)),
    )
    for name, size in (
        ("early", (EARLY_ROWS, width)),
        ("vector", (8, width)),
        ("column", (COLUMN_ROWS, width)),
        ("step", (8, 128)),
    ):
        scratch[name + "_near"] = pltpu.VMEM((GROUP,) + size, F32)
        scratch[name + "_far"] = pltpu.VMEM((outer,) + size, F32)
        scratch[name + "_sends"] = pltpu.SemaphoreType.DMA((GROUP + outer + 1,))
        scratch[name + "_receives"] = pltpu.SemaphoreType.DMA((GROUP + outer + 1,))
    for name in MATRICES:
        held, wide_now = weights[name].shape
        scratch[name] = pltpu.VMEM((outer, GROUP, 2, held // 2, wide_now), BF16)
        half = (held // 2, wide_now)
        if name == SHRINK:
            half = (wide_now // 2, held)
        scratch["g_" + name] = pltpu.VMEM((outer, GROUP, 2) + half, BF16)
        scratch["pair_" + name] = pltpu.VMEM((outer, GROUP) + half, BF16)
        scratch["near_" + name] = pltpu.VMEM((GROUP - 1, outer) + half, BF16)
        scratch["far_" + name] = pltpu.VMEM((max(1, outer - 1),) + half, BF16)
        scratch["done_" + name] = pltpu.VMEM((2,) + half, F32)
        for kind, count in (("", GROUP * outer + GROUP), ("sum_", GROUP + outer + 1)):
            for way in ("_sends", "_receives"):
                scratch[kind + name + way] = pltpu.SemaphoreType.DMA((count,))
    got = call(
        shard_kernel, sizes, inputs, outputs, scratch,
        ("tokens_in", "cotangent_in", "result_out", "input_out"),
        pltpu.CompilerParams(
            collective_id=1, has_side_effects=True, vmem_limit_bytes=VMEM_LIMIT
        ),
        "row_and_sums",
    )
    inputs = dict(
        result_in=got["result_out"], input_in=got["input_out"], vector_sum=got["vector_out"],
        early=got["early_out"], column_sum=got["column_out"], step_sum=got["step_out"],
        **{name + "_sum": got["out_" + name] for name in MATRICES},
        **weight_in, **row_in, **column_in,
    )
    outputs = dict(
        block_output=shape((slots, width), BF16),
        input_gradient=shape((slots, width), F32),
        global_norm=shape((1, 1), F32),
    )
    for name in MATRICES:
        outputs[name + "_gradient"] = shape(weights[name].shape, F32)
        outputs[name + "_newrows"] = shape(row_in[name + "_rows"].shape, F32)
        outputs[name + "_newcols"] = shape(column_in[name + "_columns"].shape, F32)
        outputs[name + "_updated"] = shape(weights[name].shape, F32)
        outputs[name + "_bfloat"] = shape(weights[name].shape, BF16)
    for name in ("vector_gradient", "vector_variance", "vector_updated"):
        outputs[name] = shape(vectors.shape, F32)
    out = call(
        update_kernel, sizes, inputs, outputs, dict(sems=pltpu.SemaphoreType.DMA((2,))),
        ("result_in", "input_in", "block_output", "input_gradient"),
        pltpu.CompilerParams(vmem_limit_bytes=VMEM_LIMIT // 2),
        "update",
    )
    out["block_output"] = out["block_output"][None]
    out["input_gradient"] = out["input_gradient"][None]
    out["global_norm"] = out["global_norm"].reshape(())
    for name in MATRICES:
        for kind in ("_newrows", "_newcols"):
            out[name + kind] = out[name + kind].reshape(-1)
    return tuple(out.values())


def row_kernel(names, *refs):
    r = Refs(names, refs)
    prepare(r)
    project(r)
    attend_forward(r, ())
    feed_forward(r)
    r.g_vectors[...] = vector_total(r)
    shrink_gradient(r)
    expand_gradient(r)
    merger_gradient(r)
    attend_backward(r, ())
    attend_gradient(r)
    input_gradient(r)


def plain_shards(devices, tokens, lengths, weights, vectors, rows, columns, moments, cotangent):
    slots, width = tokens.shape[1:]
    wide = weights[EXPAND].shape[1]
    shape = jax.ShapeDtypeStruct
    whole = {
        name: lax.all_gather(weights[name].astype(BF16), FSDP, axis=0, tiled=True)
        for name in MATRICES
    }
    vector_rows = lax.all_gather(vectors.astype(BF16), FSDP, axis=1, tiled=True).astype(F32)
    vector_rows = jnp.concatenate([vector_rows, jnp.zeros((2, width), F32)], axis=0)
    inputs = dict(
        tokens=tokens[0], lengths=lengths, cotangent=cotangent[0], vectors=vector_rows, **whole
    )
    outputs = dict(
        result=shape((slots, width), BF16),
        straight=shape((slots, width), F32),
        g_vectors=shape((8, width), F32),
        g_attend=shape((width, 3 * width), BF16),
        g_merger=shape((width, width), BF16),
        g_expand=shape((width, wide), BF16),
        g_shrink=shape((width, wide), BF16),
    )
    scratch = row_scratch(slots, width, wide)
    scratch["d_branch"] = pltpu.VMEM((slots, width), BF16)
    names = list(inputs) + list(outputs) + list(scratch)
    got = pl.pallas_call(
        functools.partial(row_kernel, names),
        in_specs=[in_vmem()] * len(inputs),
        out_specs=[in_vmem()] * len(outputs),
        out_shape=list(outputs.values()),
        scratch_shapes=list(scratch.values()),
        compiler_params=pltpu.CompilerParams(vmem_limit_bytes=VMEM_LIMIT),
        name="row",
    )(*inputs.values())
    got = dict(zip(outputs, got, strict=True))
    grads = []
    for name in MATRICES:
        value = lax.psum(got["g_" + name], DP).astype(F32)
        if name == SHRINK:
            grads.append(lax.psum_scatter(value.T, FSDP, scatter_dimension=0, tiled=True))
        else:
            grads.append(lax.psum_scatter(value, FSDP, scatter_dimension=0, tiled=True))
    vector_all = lax.psum(got["g_vectors"][:6], (DP, FSDP))
    index = lax.axis_index(FSDP)

    def spread(own, dim):
        size = own.shape[dim]
        extent = own.shape[:dim] + (size * devices,) + own.shape[dim + 1 :]
        return lax.dynamic_update_slice_in_dim(
            jnp.zeros(extent, F32), own, index * size, dim
        )

    early = (
        [spread(columns[name], 0) for name in MATRICES],
        [jnp.sum(weights[name] * weights[name]) for name in MATRICES],
        [jnp.sum(rows[name]) for name in MATRICES],
        [jnp.sum(grad * grad, axis=0) for grad in grads],
        jnp.sum(vectors * vectors, axis=1),
    )
    old_columns, weight_squares, row_sums, columns_now, vector_squares = lax.psum(early, FSDP)
    squares = [jnp.sum(value) for value in columns_now]
    total = jnp.sum(vector_all * vector_all)
    for value in squares:
        total = total + value
    norm = jnp.sqrt(total)
    clip = jnp.minimum(1.0, THRESHOLD / norm)
    power = clip * clip
    pieces = []
    for at, name in enumerate(MATRICES):
        grad = grads[at]
        rows_all = float(grad.shape[0] * devices)
        count = rows_all * grad.shape[1]
        new_rows = FORGET * rows[name] + (1.0 - FORGET) * (
            power * jnp.mean(grad * grad, axis=1) + TINY_VALUE
        )
        new_columns = FORGET * old_columns[at] + (1.0 - FORGET) * (
            power * columns_now[at] / rows_all + TINY_VALUE
        )
        mean = FORGET * row_sums[at] / rows_all + (1.0 - FORGET) * (
            power * squares[at] / count + TINY_VALUE
        )
        clipped = clip * grad
        step = clipped * lax.rsqrt(new_rows[:, None] * new_columns[None, :] / mean)
        pieces.append((clipped, new_rows, new_columns, step, count))
    thin = vectors.shape[1]
    vector_clipped = clip * lax.dynamic_slice_in_dim(vector_all, index * thin, thin, 1)
    variance = FORGET * moments + (1.0 - FORGET) * (vector_clipped * vector_clipped + TINY_VALUE)
    vector_step = vector_clipped * lax.rsqrt(variance)
    step_squares, vector_step_squares = lax.psum(
        (
            [jnp.sum(piece[3] * piece[3]) for piece in pieces],
            jnp.sum(vector_step * vector_step, axis=1),
        ),
        FSDP,
    )
    results = [got["result"][None], got["straight"][None], norm]
    for at, name in enumerate(MATRICES):
        clipped, new_rows, new_columns, step, count = pieces[at]
        shrunk = jnp.maximum(1.0, jnp.sqrt(step_squares[at] / count) / UPDATE_LIMIT)
        stride = LEARN_RATE * jnp.maximum(0.001, jnp.sqrt(weight_squares[at] / count))
        updated = weights[name] - stride * (step / shrunk)
        size = columns[name].shape[0]
        own = lax.dynamic_slice_in_dim(new_columns, index * size, size, 0)
        results.extend([clipped, new_rows, own, updated, updated.astype(BF16)])
    extent = float(width)
    shrunk = jnp.maximum(1.0, jnp.sqrt(vector_step_squares / extent) / UPDATE_LIMIT)[:, None]
    stride = LEARN_RATE * jnp.maximum(0.001, jnp.sqrt(vector_squares / extent))[:, None]
    results.extend([vector_clipped, variance, vectors - stride * (vector_step / shrunk)])
    return tuple(results)


def shards(
    devices,
    tokens,
    lengths,
    attend_weight,
    merger_weight,
    expand_weight,
    shrink_weight,
    vectors,
    attend_rows,
    attend_columns,
    merger_rows,
    merger_columns,
    expand_rows,
    expand_columns,
    shrink_rows,
    shrink_columns,
    vector_moments,
    cotangent,
):
    weights = dict(
        attend=attend_weight, merger=merger_weight, expand=expand_weight, shrink=shrink_weight
    )
    rows = dict(attend=attend_rows, merger=merger_rows, expand=expand_rows, shrink=shrink_rows)
    columns = dict(
        attend=attend_columns, merger=merger_columns, expand=expand_columns, shrink=shrink_columns
    )
    assert tokens.shape[0] == 1
    fits = devices % GROUP == 0 and all(
        weight.shape[0] % 32 == 0 for weight in weights.values()
    ) and shrink_weight.shape[0] % 128 == 0
    body = staged_shards if fits else plain_shards
    return body(
        devices, tokens, lengths, weights, vectors, rows, columns, vector_moments, cotangent
    )


def solution(mesh):
    split = P(FSDP, None)
    row = P((DP, FSDP), None, None)
    one = P(FSDP)
    thin = P(None, FSDP)
    in_specs = (
        (row, P((DP, FSDP), None)) + (split,) * 4 + (thin,) + (one,) * 8 + (thin, row)
    )
    out_specs = (row, row, P()) + (split, one, one, split, split) * 4 + (thin,) * 3
    return jax.shard_map(
        functools.partial(shards, mesh.shape[FSDP]),
        mesh=mesh, in_specs=in_specs, out_specs=out_specs, check_vma=False,
    )
```

time: 1130 us -> 164 us (0.15); the launches traced: 1120 us -> 164 us
  waiting for transfers between devices: 508 us -> 0 us
  blocking collectives: 236 us -> 0 us
  matrix products: 235 us -> 0 us
  Pallas kernels: 0 us -> 153 us
  other arithmetic: 74.9 us -> 0 us
  between operations: 28.2 us -> 1.05 us
  local copies, waits for them, and re-layouts: 34 us -> 9.5 us
    reduce_scatter x3 -> x0, waiting for transfers between devices: 262 us -> none  [the longest x1 94.8 us: shards(): lax.psum_scatter(paired[3], 'fsdp', scatter_dimension=0, tiled=True)]
    dot_general x24 -> x0, matrix products: 235 us -> none  [the longest x2 70.3 us: attend_backward(): jnp.einsum('hqk,qhd->khd', grad_scores, rows_query, preferred_element_typ...]
    unnamed x11 -> x0, waiting for transfers between devices: 187 us -> none
    pallas_call x0 -> x2, Pallas kernels: none -> 153 us  [call(): pl.pallas_call(functools.partial(kernel, sizes, names), in_specs=[anywher...]
    psum x4 -> x0, blocking collectives: 151 us -> none  [the longest x1 71.8 us: shards(): lax.psum((column_terms[0], column_terms[1], column_terms[2], column_terms...]
    all_gather x2 -> x0, blocking collectives: 84.2 us -> none  [the longest x1 42.9 us: shards(): lax.all_gather(vectors.astype(jnp.bfloat16), 'fsdp', axis=1, tiled=True)]
    reduce_sum x30 -> x0, other arithmetic: 42.6 us -> none  [the longest x2 12.3 us: attend_forward(): jnp.sum(jnp.exp(scores - highest), axis=-1, keepdims=True)]
    all_gather x3 -> x0, waiting for transfers between devices: 31 us -> none  [the longest x1 31 us: shards(): lax.all_gather(shrink_weight.astype(jnp.bfloat16), 'fsdp', axis=0, tiled=...]
  transfers between devices with their start and end apart: 9 -> 0, of which waited for: 7 -> 0; matrix products, arithmetic and copies ran while one was open for 9% -> 0% of each run, Pallas kernels for 0% -> 0%
where the time goes in v1:
time: 164 us
  Pallas kernels  153 us (93%)
  local copies, waits for them, and re-layouts  9.5 us (6%)
    pallas_call x2, Pallas kernels, call(): pl.pallas_call(functools.partial(kernel, sizes, names), in_specs=[anywher...  153 us
    unnamed x44, local copies, waits for them, and re-layouts  9.5 us

profile of v1, /device:TPU:0, one launch (start us, length us, event | category | flops | bytes accessed | tf_op | source)
XLA Modules:
  0.0 163.7 jit_solution(3505664523391827487)
XLA Ops:
  0.7 0.0 copy-start.3
  0.7 0.0 copy-start.2
  0.7 0.0 copy-start.7
  0.7 0.0 copy-start.4
  0.7 0.0 copy-start.21
  0.7 0.0 copy-start.17
  0.7 0.0 copy-start.20
  0.7 0.0 copy-start.16
  0.8 0.0 copy-start.19
  0.8 0.0 copy-start.15
  0.8 0.0 copy-start.18
  0.8 0.0 copy-start.14
  0.8 149.7 %row_and_sums.1 = (bf16[1024,512]{1,0:T(8,128)(2,1)}, f32[1024,512]{1,0:T(8,128)}, f32[8,512]{1,0:T(8,128)}, f32[32,512]{1,0:T(8,128)}, f32[16,512]{1,0:T(8,128)...) custom-call(bf16[1024,512]{1,0:T(8,128)(2,1)} %bitcast.37, ...), custom_call_target="tpu_custom_call" | custom-call | tf_op jit(solution)/shard_map/row_and_sums/pallas_call | solution.py:947
  150.7 1.6 copy-done
  152.2 1.2 copy-done.1
  153.5 0.9 copy-done.5
  154.4 0.9 copy-done.6
  155.4 0.9 copy-done.8
  156.3 0.8 copy-done.9
  157.1 0.8 copy-done.10
  158.0 0.8 copy-done.11
  158.7 0.7 copy-done.12
  159.4 0.7 copy-done.13
  160.1 3.4 %update.1 = (bf16[1024,512]{1,0:T(8,128)(2,1)}, f32[1024,512]{1,0:T(8,128)}, f32[1,1]{1,0:T(1,128)}, f32[32,1536]{1,0:T(8,128)}, f32[1,32]{1,0:T(1,128)}, /*inde...) custom-call(bf16[1024,512]{1,0:T(8,128)(2,1)S(1)} %copy-done.1, ...), custom_call_target="tpu_custom_call" | custom-call | tf_op jit(solution)/shard_map/update/pallas_call | solution.py:947
  (22 shorter events, 0.0 us)
Async XLA Ops:
  0.7 149.8 %copy-start.3 = (f32[128,512]{1,0:T(8,128)S(1)}, f32[128,512]{1,0:T(8,128)}, u32[]{:S(2)}) copy-start(f32[128,512]{1,0:T(8,128)} %refs_13_.1) | copy-start | bytes 786436
  0.7 149.8 %copy-start.2 = (f32[32,2048]{1,0:T(8,128)S(1)}, f32[32,2048]{1,0:T(8,128)}, u32[]{:S(2)}) copy-start(f32[32,2048]{1,0:T(8,128)} %refs_12_.1) | copy-start | bytes 786436
  0.7 149.8 %copy-start.7 = (f32[32,512]{1,0:T(8,128)S(1)}, f32[32,512]{1,0:T(8,128)}, u32[]{:S(2)}) copy-start(f32[32,512]{1,0:T(8,128)} %refs_11_.1) | copy-start | bytes 196612
  0.7 149.8 %copy-start.4 = (f32[32,1536]{1,0:T(8,128)S(1)}, f32[32,1536]{1,0:T(8,128)}, u32[]{:S(2)}) copy-start(f32[32,1536]{1,0:T(8,128)} %refs_10_.1) | copy-start | bytes 589828
  0.7 149.8 %copy-start.21 = (f32[32]{0:T(128)S(1)}, f32[32]{0:T(128)}, u32[]{:S(2)}) copy-start(f32[32]{0:T(128)} %param.31) | copy-start | bytes 388
  0.7 149.8 %copy-start.17 = (f32[128]{0:T(128)S(1)}, f32[128]{0:T(128)}, u32[]{:S(2)}) copy-start(f32[128]{0:T(128)} %param.30) | copy-start | bytes 1540
  0.7 149.8 %copy-start.20 = (f32[128]{0:T(128)S(1)}, f32[128]{0:T(128)}, u32[]{:S(2)}) copy-start(f32[128]{0:T(128)} %param.29) | copy-start | bytes 1540
  0.7 149.8 %copy-start.16 = (f32[32]{0:T(128)S(1)}, f32[32]{0:T(128)}, u32[]{:S(2)}) copy-start(f32[32]{0:T(128)} %param.28) | copy-start | bytes 388
  0.8 149.8 %copy-start.19 = (f32[32]{0:T(128)S(1)}, f32[32]{0:T(128)}, u32[]{:S(2)}) copy-start(f32[32]{0:T(128)} %param.27) | copy-start | bytes 388
  0.8 149.8 %copy-start.15 = (f32[32]{0:T(128)S(1)}, f32[32]{0:T(128)}, u32[]{:S(2)}) copy-start(f32[32]{0:T(128)} %param.26) | copy-start | bytes 388
  0.8 149.8 %copy-start.18 = (f32[96]{0:T(128)S(1)}, f32[96]{0:T(128)}, u32[]{:S(2)}) copy-start(f32[96]{0:T(128)} %param.25) | copy-start | bytes 1156
  0.8 149.8 %copy-start.14 = (f32[32]{0:T(128)S(1)}, f32[32]{0:T(128)}, u32[]{:S(2)}) copy-start(f32[32]{0:T(128)} %param.24) | copy-start | bytes 388
  150.6 1.6 copy-start
  152.2 1.2 copy-start.1
  153.5 0.9 copy-start.5
  154.4 0.9 copy-start.6
  155.4 0.9 copy-start.8
  156.3 0.8 copy-start.9
  157.1 0.8 copy-start.10
  158.0 0.8 copy-start.11
  158.7 0.7 copy-start.12
  159.4 0.7 copy-start.13

commit v2 on v1

--- a/solution.py
+++ b/solution.py
@@ -156,13 +156,14 @@
     factor = HEAD_DIM ** -0.5 * LOG2_E
 
     def pair(step, carry):
-        for at, hook in hooks:
-            pl.when(step == at)(hook)
         start = pl.multiple_of(step * 128, 128)
-        for first, low, high, place in band(slots)[0]:
-            keys = r.key_value[low:high, pl.ds(start, 128)]
-            fits = r.mask[place : place + high - low, :].astype(F32) > 0.5
-            for head in (0, 1):
+        for head in (0, 1):
+            for at, hook in hooks:
+                if at % 2 == head:
+                    pl.when(step == at // 2)(hook)
+            for first, low, high, place in band(slots)[0]:
+                keys = r.key_value[low:high, pl.ds(start, 128)]
+                fits = r.mask[place : place + high - low, :].astype(F32) > 0.5
                 mine = pl.ds(start + 64 * head, 64)
                 queries = r.projected_t[mine, first : first + QUERY_BLOCK]
                 scores = dot_nn(keys, beside_zeros(queries, head))
@@ -184,10 +185,11 @@
     scale = HEAD_DIM ** -0.5
 
     def pair(step, carry):
-        for at, hook in hooks:
-            pl.when(step == at)(hook)
         start = pl.multiple_of(step * 128, 128)
         for head in (0, 1):
+            for at, hook in hooks:
+                if at % 2 == head:
+                    pl.when(step == at // 2)(hook)
             mine = pl.ds(start + 64 * head, 64)
             mine_keys = pl.ds(width + start + 64 * head, 64)
             mine_values = pl.ds(2 * width + start + 64 * head, 64)
@@ -226,32 +228,50 @@
     lax.fori_loop(0, width // 128, pair, 0)
 
 
-def feed_forward(r):
-    slots, width = r.tokens.shape
-    r.vector_sums[...] = jnp.zeros_like(r.vector_sums)
-
+def vector_rows(r):
+    return [r.vectors[place : place + 1, :] for place in range(6)]
+
+
+def by_tokens(r, body):
     def block(step, carry):
-        rows = aligned(step * TILE, TILE)
-        omega_one, gain_one, shift_one, omega_two, gain_two, shift_two = [
-            r.vectors[place : place + 1, :] for place in range(6)
-        ]
+        body(step, aligned(step * TILE, TILE))
+        return carry
+
+    lax.fori_loop(0, r.tokens.shape[0] // TILE, block, 0)
+
+
+def first_half(r):
+    omega_one, gain_one, shift_one = vector_rows(r)[:3]
+
+    def body(step, rows):
         inputs = r.tokens[rows, :].astype(F32)
         first_sum = omega_one * inputs + dot_tn(r.context_t[:, rows], flat(r.merger[...]))
         centered = first_sum - lane_mean(first_sum)
         first_inv = lax.rsqrt(lane_mean(centered * centered) + EPSILON)
         first_normed = centered * first_inv
-        first_out = first_normed * gain_one + shift_one
-        first_low = first_out.astype(BF16)
+        r.first_inv[rows, :] = jnp.broadcast_to(first_inv, (TILE, 128))
+        r.straight[rows, :] = first_normed
+        first_low = (first_normed * gain_one + shift_one).astype(BF16)
         r.first_t[:, rows] = first_low.T
         hidden = dot_nn(first_low, flat(r.expand[...]))
         square = hidden * hidden
         bend = jnp.tanh(hidden * (GELU_A + GELU_B * square))
         half = 0.5 * hidden
         lifted = 1.0 + bend
-        active = (half * lifted).astype(BF16)
-        r.slope[...] = 0.5 * lifted + half * (1.0 - bend * bend) * (GELU_A + 3 * GELU_B * square)
-        r.active[rows, :] = active
-        second_sum = omega_two * first_out + dot_nn(active, flat(r.shrink[...]))
+        r.active[rows, :] = (half * lifted).astype(BF16)
+        slope = 0.5 * lifted + half * (1.0 - bend * bend) * (GELU_A + 3 * GELU_B * square)
+        r.d_hidden[rows, :] = slope.astype(BF16)
+
+    by_tokens(r, body)
+
+
+def second_half(r):
+    _, gain_one, shift_one, omega_two, gain_two, shift_two = vector_rows(r)
+    r.vector_sums[...] = jnp.zeros_like(r.vector_sums)
+
+    def body(step, rows):
+        first_out = r.straight[rows, :] * gain_one + shift_one
+        second_sum = omega_two * first_out + dot_nn(r.active[rows, :], flat(r.shrink[...]))
         centered = second_sum - lane_mean(second_sum)
         second_inv = lax.rsqrt(lane_mean(centered * centered) + EPSILON)
         second_normed = centered * second_inv
@@ -266,25 +286,35 @@
         r.vector_sums[4] += fold_rows(upstream * second_normed)
         r.vector_sums[5] += fold_rows(upstream)
         r.vector_sums[3] += fold_rows(first_out * d_second)
-        second_low = d_second.astype(BF16)
-        r.d_second_t[:, rows] = second_low.T
-        d_hidden = (dot_nt(second_low, flat(r.shrink[...])) * r.slope[...]).astype(BF16)
+        r.d_second[rows, :] = d_second
+        r.d_second_t[:, rows] = d_second.astype(BF16).T
+
+    by_tokens(r, body)
+
+
+def way_back(r):
+    omega_one, gain_one, _, omega_two = vector_rows(r)[:4]
+
+    def body(step, rows):
+        d_second = r.d_second[rows, :]
+        d_active = dot_nt(d_second.astype(BF16), flat(r.shrink[...]))
+        d_hidden = (d_active * r.d_hidden[rows, :].astype(F32)).astype(BF16)
         r.d_hidden[rows, :] = d_hidden
         d_first = dot_nt(d_hidden, flat(r.expand[...])) + omega_two * d_second
+        first_normed = r.straight[rows, :]
         r.vector_sums[1] += fold_rows(d_first * first_normed)
         r.vector_sums[2] += fold_rows(d_first)
         scaled = d_first * gain_one
-        d_first_sum = first_inv * (
+        d_first_sum = r.first_inv[rows, 0:1] * (
             scaled - lane_mean(scaled) - first_normed * lane_mean(scaled * first_normed)
         )
-        r.vector_sums[0] += fold_rows(inputs * d_first_sum)
+        r.vector_sums[0] += fold_rows(r.tokens[rows, :].astype(F32) * d_first_sum)
         r.straight[rows, :] = omega_one * d_first_sum
         branch_low = d_first_sum.astype(BF16)
         r.d_branch[rows, :] = branch_low
         r.d_context_t[:, rows] = dot_nt(flat(r.merger[...]), branch_low).astype(BF16)
-        return carry
-
-    lax.fori_loop(0, slots // TILE, block, 0)
+
+    by_tokens(r, body)
 
 
 def vector_total(r):
@@ -348,12 +378,28 @@
     by_columns(r.tokens.shape[1], store)
 
 
-def attend_gradient(r):
+def attend_gradient(r, part):
+    width = r.tokens.shape[1]
+    half = width // 2
+    into = r.g_attend[part]
+
     def store(step):
-        columns = aligned(step * TILE, TILE)
-        put_tile(r.g_attend, columns, dot_nt(r.tokens_t[...], r.projected_t[columns, :]))
-
-    by_columns(3 * r.tokens.shape[1], store)
+        columns = aligned(step * half, half)
+        heads = r.projected_t[aligned(step * width + part * half, half), :]
+        put_tile(into, columns, dot_nt(r.tokens_t[...], heads))
+
+    def tile(step, carry):
+        store(step)
+        return carry
+
+    lax.fori_loop(0, 3, tile, 0)
+
+
+def heads_together(parts):
+    half = parts[0].shape[1] // 3
+    return jnp.concatenate(
+        [part[:, at * half : (at + 1) * half] for at in range(3) for part in parts], axis=1
+    )
 
 
 def input_gradient(r):
@@ -382,7 +428,8 @@
         first_t=pltpu.VMEM((width, slots), BF16),
         d_second_t=pltpu.VMEM((width, slots), BF16),
         vector_sums=pltpu.VMEM((6, 8, width), F32),
-        slope=pltpu.VMEM((TILE, wide), F32),
+        first_inv=pltpu.VMEM((slots, 128), F32),
+        d_second=pltpu.VMEM((slots, width), F32),
     )
 
 
@@ -392,13 +439,33 @@
             setattr(self, name, ref)
 
 
-def spread_rows(width, columns_of):
+LOW, HIGH = "low", "high"
+REDUCED = (SHRINK, EXPAND, MERGER, LOW, HIGH)
+FOLDED = (SHRINK, EXPAND)
+
+
+def packed_rows(first, order, columns_of, width):
     places = {}
-    start = 0
-    for name in MATRICES:
-        places[name] = (start, columns_of[name] // width)
-        start += columns_of[name] // width
-    return places, start
+    for name in order:
+        places[name] = (first, columns_of[name] // width)
+        first += columns_of[name] // width
+    return places
+
+
+SQUARES, ROW_SUMS, EARLY_ROWS = 6, 7, 8
+LATE_COLUMNS, LATE_ROWS = 6, 16
+COLUMN_ROWS = 8
+ALL = slice(None)
+
+
+def late_places(columns_of, width):
+    return packed_rows(LATE_COLUMNS, (MERGER, SHRINK, ATTEND, EXPAND), columns_of, width)
+
+
+def column_places(columns_of, width):
+    places = packed_rows(0, (MERGER, EXPAND, SHRINK), columns_of, width)
+    places.update(packed_rows(COLUMN_ROWS, (ATTEND,), columns_of, width))
+    return places
 
 
 def joined(ref, start, count):
@@ -414,49 +481,54 @@
     return jnp.sum(jnp.sum(value, axis=1, keepdims=True), axis=0, keepdims=True)
 
 
-def clip_of(columns_ref, places, vector_gradient):
-    squares = {
-        name: scalar_sum(joined(columns_ref, *places[name])) for name in MATRICES
-    }
-    total = scalar_sum(vector_gradient * vector_gradient)
-    for name in MATRICES:
-        total = total + squares[name]
-    norm = jnp.sqrt(total)
-    return norm, jnp.minimum(1.0, THRESHOLD / norm), squares
-
-
-def factored_step(name, gradient, rows_old, columns_ref, early_ref, places, clip, squares, rows_all):
-    start, count = places[name]
-    wide = gradient.shape[1]
-    power = clip * clip
-    row_mean = jnp.sum(gradient * gradient, axis=1, keepdims=True) * (1.0 / wide)
-    new_rows = FORGET * column_of(rows_old) + (1.0 - FORGET) * (power * row_mean + TINY_VALUE)
-    new_columns = FORGET * joined(early_ref, start, count) + (1.0 - FORGET) * (
-        power * (joined(columns_ref, start, count) * (1.0 / rows_all)) + TINY_VALUE
-    )
-    old = early_ref[ROW_SUMS : ROW_SUMS + 1, :]
-    at = MATRICES.index(name) * 128
-    old_mean = jnp.sum(old[:, at : at + 128], axis=1, keepdims=True) * (1.0 / rows_all)
-    mean = FORGET * old_mean + (1.0 - FORGET) * (
-        power * (squares[name] * (1.0 / (rows_all * wide))) + TINY_VALUE
-    )
-    clipped = clip * gradient
-    step = clipped * lax.rsqrt(new_rows * new_columns * (1.0 / mean))
-    return clipped, new_rows, new_columns, step
+def flat_slots(value):
+    return value.reshape((-1,) + value.shape[2:])
+
+
+class Statistics:
+    def __init__(self, r, sizes, columns, vector_gradient):
+        outer, self.width, _ = sizes
+        self.devices = outer * GROUP
+        columns_of = {
+            name: getattr(r, name + "_columns").shape[1] * self.devices for name in MATRICES
+        }
+        self.early, self.late, self.columns = r.early, r.late, columns
+        self.late_at = late_places(columns_of, self.width)
+        self.column_at = column_places(columns_of, self.width)
+        self.squares = {
+            name: scalar_sum(joined(columns, *self.column_at[name])) for name in MATRICES
+        }
+        total = scalar_sum(vector_gradient * vector_gradient)
+        for name in MATRICES:
+            total = total + self.squares[name]
+        self.norm = jnp.sqrt(total)
+        self.clip = jnp.minimum(1.0, THRESHOLD / self.norm)
+
+    def lanes(self, row, name):
+        at = MATRICES.index(name) * 128
+        return jnp.sum(self.early[row : row + 1, at : at + 128], axis=1, keepdims=True)
+
+    def factored(self, name, gradient, rows_old, rows_all):
+        wide = gradient.shape[1]
+        power = self.clip * self.clip
+        row_mean = jnp.sum(gradient * gradient, axis=1, keepdims=True) * (1.0 / wide)
+        new_rows = FORGET * rows_old + (1.0 - FORGET) * (power * row_mean + TINY_VALUE)
+        now = joined(self.columns, *self.column_at[name]) * (1.0 / rows_all)
+        new_columns = FORGET * joined(self.late, *self.late_at[name]) + (1.0 - FORGET) * (
+            power * now + TINY_VALUE
+        )
+        mean = FORGET * (self.lanes(ROW_SUMS, name) * (1.0 / rows_all)) + (1.0 - FORGET) * (
+            power * (self.squares[name] * (1.0 / (rows_all * wide))) + TINY_VALUE
+        )
+        clipped = self.clip * gradient
+        step = clipped * lax.rsqrt(new_rows * new_columns * (1.0 / mean))
+        return clipped, new_rows, new_columns, step
 
 
 def vector_steps(gradient, moments, clip):
     clipped = clip * gradient
     variance = FORGET * moments + (1.0 - FORGET) * (clipped * clipped + TINY_VALUE)
     return clipped, variance, clipped * lax.rsqrt(variance)
-
-
-SQUARES = 9
-ROW_SUMS = 10
-VECTORS = 16
-MOMENTS = 24
-EARLY_ROWS = 32
-COLUMN_ROWS = 16
 
 
 def shard_kernel(layout_sizes, names, *refs):
@@ -464,6 +536,7 @@
     r = Refs(names, refs)
     r.result = r.cotangent
     r.d_branch = r.tokens
+    r.g_attend = (r.g_low, r.g_high)
     core = lax.axis_index(DP)
     chip = lax.axis_index(FSDP)
     far = chip // GROUP
@@ -472,33 +545,52 @@
     near_steps = range(1, GROUP)
     far_steps = range(1, outer)
 
-    def at_near(step):
-        return jnp.bitwise_xor(near, step)
-
-    def at_far(step):
-        return lax.rem(far + step, outer)
-
-    def from_far(step):
-        return lax.rem(far + outer - step, outer)
-
-    def near_device(step):
-        return (core, far * GROUP + at_near(step))
-
-    def far_device(step):
-        return (core, at_far(step) * GROUP + near)
-
-    def remote(source, target, device, sends, receives, index):
-        return pltpu.make_async_remote_copy(
-            src_ref=source,
-            dst_ref=target,
-            send_sem=sends.at[index],
-            recv_sem=receives.at[index],
-            device_id=device,
-            device_id_type=MESH,
-        )
-
-    def start(copy):
-        copy.start()
+    near_places = [near] + [jnp.bitwise_xor(near, step) for step in near_steps]
+    far_places = [lax.rem(far + step, outer) for step in range(outer)]
+    far_origins = [lax.rem(far + outer - step, outer) for step in range(outer)]
+    near_devices = [(core, far * GROUP + place) for place in near_places]
+    far_devices = [(core, place * GROUP + near) for place in far_places]
+    other = 1 - core
+    fold_first = jnp.bitwise_xor(near, 1 + core)
+    fold_second = jnp.bitwise_xor(near, 2 - core)
+    diagonal_place = near_places[3]
+    fold_devices = [
+        (core, far * GROUP + place) for place in (fold_first, fold_first, fold_second)
+    ]
+
+    started = {}
+    arrived = set()
+
+    class Copy:
+        def __init__(self, key, sems, index, device, source, target, landing=None):
+            self.key = key + (index,)
+            self.device = device
+            self.sems = sems
+            self.index = index
+            self.source = source
+            self.target = target
+            self.landing = target if landing is None else landing
+
+        def describe(self, source, target):
+            return pltpu.make_async_remote_copy(
+                src_ref=source[0].at[source[1]],
+                dst_ref=target[0].at[target[1]],
+                send_sem=self.sems[0].at[self.index],
+                recv_sem=self.sems[1].at[self.index],
+                device_id=self.device,
+                device_id_type=MESH,
+            )
+
+        def start(self):
+            self.describe(self.source, self.target).start()
+            started[self.key] = self
+
+        def arrive(self):
+            self.describe(self.landing, self.landing).wait_recv()
+            arrived.add(self.key)
+
+        def leave(self):
+            self.describe(self.source, self.target).wait_send()
 
     def local(source, target, index):
         return pltpu.make_async_copy(source, target, r.local_sems.at[index])
@@ -510,79 +602,89 @@
 
     barrier = pltpu.get_barrier_semaphore()
     for step in near_steps:
-        pl.semaphore_signal(barrier, inc=1, device_id=near_device(step), device_id_type=MESH)
+        pl.semaphore_signal(barrier, inc=1, device_id=near_devices[step], device_id_type=MESH)
     for step in far_steps:
-        pl.semaphore_signal(barrier, inc=1, device_id=far_device(step), device_id_type=MESH)
+        pl.semaphore_signal(barrier, inc=1, device_id=far_devices[step], device_id_type=MESH)
     pl.semaphore_signal(barrier, inc=1, device_id=sibling, device_id_type=MESH)
     pl.semaphore_wait(barrier, len(near_steps) + len(far_steps) + 1)
 
 
     class Sum:
-        def __init__(self, name):
+        def __init__(self, name, cores):
+            self.key = (name,)
             self.near = getattr(r, name + "_near")
             self.far = getattr(r, name + "_far")
-            self.sends = getattr(r, name + "_sends")
-            self.receives = getattr(r, name + "_receives")
-
-        def begin(self, value=None):
-            if value is not None:
-                self.near[near] = value
-            for step in near_steps:
-                start(
-                    remote(
-                        self.near.at[near], self.near.at[near], near_device(step),
-                        self.sends, self.receives, step - 1,
-                    )
-                )
+            self.sems = (getattr(r, name + "_sends"), getattr(r, name + "_receives"))
+            self.steps = [(0, step) for step in near_steps]
+            if cores == 2:
+                self.steps += [(1, step) for step in range(GROUP)]
+            self.mine = core if cores == 2 else 0
+            self.other = other if cores == 2 else 0
+
+        def near_copy(self, cross, step):
+            mine = (self.near, (self.mine, near))
+            whose = self.other if cross else self.mine
+            device = (other if cross else core, near_devices[step][1])
+            return Copy(
+                self.key, self.sems, cross * GROUP + step, device, mine, mine,
+                (self.near, (whose, near_places[step])),
+            )
+
+        def far_copy(self, step):
+            mine = (self.far, far)
+            return Copy(
+                self.key, self.sems, 2 * GROUP + step, far_devices[step], mine, mine,
+                (self.far, far_origins[step]),
+            )
+
+        def begin(self, value):
+            self.near[self.mine, near] = value
+            for cross, step in self.steps:
+                self.near_copy(cross, step).start()
 
         def turn(self):
-            for step in near_steps:
-                slot = self.near.at[at_near(step)]
-                remote(
-                    slot, slot, near_device(step), self.sends, self.receives, step - 1
-                ).wait_recv()
-            self.far[far] = jnp.sum(self.near[...], axis=0)
+            for cross, step in self.steps:
+                self.near_copy(cross, step).arrive()
+            self.far[far] = jnp.sum(flat_slots(self.near[...]), axis=0)
             for step in far_steps:
-                start(
-                    remote(
-                        self.far.at[far], self.far.at[far], far_device(step),
-                        self.sends, self.receives, GROUP + step - 1,
-                    )
-                )
+                self.far_copy(step).start()
 
         def end(self):
             for step in far_steps:
-                slot = self.far.at[from_far(step)]
-                remote(
-                    slot, slot, far_device(step), self.sends, self.receives, GROUP + step - 1
-                ).wait_recv()
+                self.far_copy(step).arrive()
             return jnp.sum(self.far[...], axis=0)
 
 
     class Gather:
-        def __init__(self, name):
+        def __init__(self, name, fine):
+            self.key = (name,)
+            self.fine = fine
+            self.hops = range(outer if fine else 1)
             self.held = getattr(r, name)
-            self.sends = getattr(r, name + "_sends")
-            self.receives = getattr(r, name + "_receives")
-
-        def far_copy(self, step, slot):
-            ref = self.held.at[slot, near, core]
-            return remote(ref, ref, far_device(step), self.sends, self.receives, step - 1)
-
-        def near_copy(self, step, back, slot):
-            ref = self.held.at[slot, near if back is None else back, core]
-            index = outer + (step - 1) * outer
-            return remote(ref, ref, near_device(step), self.sends, self.receives, index)
-
-        def cross(self, step, half, whose):
-            ref = self.held.at[:, whose, half]
-            index = outer * GROUP + step
-            return remote(ref, ref, sibling, self.sends, self.receives, index)
-
-        def near_piece(self, step, hop, whose, half):
-            ref = self.held.at[from_far(hop) if hop else far, whose, half]
-            index = outer + (step - 1) * outer + hop
-            return remote(ref, ref, near_device(step), self.sends, self.receives, index)
+            self.sems = (getattr(r, name + "_sends"), getattr(r, name + "_receives"))
+
+        def far_copy(self, step):
+            mine = (self.held, (far, near, core))
+            return Copy(
+                self.key, self.sems, step, far_devices[step], mine, mine,
+                (self.held, (far_origins[step], near, core)),
+            )
+
+        def near_copy(self, step, hop):
+            slot = far_origins[hop] if self.fine else ALL
+            mine = (self.held, (slot, near, core))
+            return Copy(
+                self.key, self.sems, step * outer + hop, near_devices[step], mine, mine,
+                (self.held, (slot, near_places[step], core)),
+            )
+
+        def cross(self, step):
+            whose = near_places[step]
+            mine = (self.held, (ALL, whose, core))
+            return Copy(
+                self.key, self.sems, GROUP * outer + step, sibling, mine, mine,
+                (self.held, (ALL, whose, other)),
+            )
 
         def place(self, shard):
             rows = shard.shape[0] // 2
@@ -591,61 +693,79 @@
 
         def begin(self):
             for step in far_steps:
-                start(self.far_copy(step, far))
+                self.far_copy(step).start()
+
+        def near_start(self, hop):
             for step in near_steps:
-                start(self.near_piece(step, 0, near, core))
+                self.near_copy(step, hop).start()
 
         def turn(self):
             for hop in far_steps:
-                self.far_copy(hop, from_far(hop)).wait_recv()
-                for step in near_steps:
-                    start(self.near_piece(step, hop, near, core))
-            start(self.cross(0, core, near))
+                self.far_copy(hop).arrive()
+                if self.fine:
+                    self.near_start(hop)
+            if not self.fine:
+                self.near_start(0)
+            self.cross(0).start()
 
         def pass_on(self):
             for step in near_steps:
-                for hop in range(outer):
-                    self.near_piece(step, hop, at_near(step), core).wait_recv()
-                start(self.cross(step, core, at_near(step)))
+                for hop in self.hops:
+                    self.near_copy(step, hop).arrive()
+                self.cross(step).start()
 
         def end(self):
             for step in range(GROUP):
-                self.cross(step, 1 - core, at_near(step) if step else near).wait_recv()
+                self.cross(step).arrive()
 
 
     class Reduce:
-        def __init__(self, name):
+        def __init__(self, name, folds):
+            self.key = ("sum", name)
+            self.folds = folds
             for part in ("g", "pair", "near", "far", "done"):
                 setattr(self, part, getattr(r, part + "_" + name))
-            self.sends = getattr(r, "sum_" + name + "_sends")
-            self.receives = getattr(r, "sum_" + name + "_receives")
+            self.sems = (
+                getattr(r, "sum_" + name + "_sends"), getattr(r, "sum_" + name + "_receives")
+            )
 
         def pair_copy(self):
-            return remote(
-                self.g.at[:, :, 1 - core], self.pair, sibling, self.sends, self.receives, 0
+            return Copy(
+                self.key, self.sems, 0, sibling, (self.g, (ALL, ALL, other)),
+                (self.pair, ALL),
             )
 
         def near_copy(self, step):
-            return remote(
-                self.pair.at[:, at_near(step)], self.near.at[step - 1], near_device(step),
-                self.sends, self.receives, step,
+            return Copy(
+                self.key, self.sems, step, near_devices[step],
+                (self.pair, (ALL, near_places[step])), (self.near, step - 1),
             )
 
+        def fold_copy(self, place):
+            block = (fold_first, diagonal_place, fold_second)[place]
+            return Copy(
+                self.key, self.sems, place + 1, fold_devices[place],
+                (self.pair, (ALL, block)), (self.near, place),
+            )
+
         def far_copy(self, step):
-            return remote(
-                self.pair.at[at_far(step), near], self.far.at[step - 1], far_device(step),
-                self.sends, self.receives, GROUP + step - 1,
+            return Copy(
+                self.key, self.sems, GROUP + step - 1, far_devices[step],
+                (self.pair, (far_places[step], near)), (self.far, step - 1),
             )
 
-        def done_copy(self, half):
-            ref = self.done.at[half]
-            return remote(ref, ref, sibling, self.sends, self.receives, GROUP + outer)
+        def done_copy(self):
+            mine = (self.done, core)
+            return Copy(
+                self.key, self.sems, GROUP + outer, sibling, mine, mine,
+                (self.done, other),
+            )
 
         def begin(self):
-            start(self.pair_copy())
+            self.pair_copy().start()
 
         def turn(self):
-            self.pair_copy().wait_recv()
+            self.pair_copy().arrive()
 
             def block(step, carry):
                 both = self.g[step, :, core].astype(F32) + self.pair[step].astype(F32)
@@ -653,42 +773,60 @@
                 return carry
 
             lax.fori_loop(0, outer, block, 0)
+            if self.folds:
+                self.fold_copy(0).start()
+                self.fold_copy(1).start()
+                return
             for step in near_steps:
-                start(self.near_copy(step))
+                self.near_copy(step).start()
+
+        def add(self, place, landed):
+            def block(step, carry):
+                total = self.pair[step, place].astype(F32)
+                for at in landed:
+                    total = total + self.near[at, step].astype(F32)
+                self.pair[step, place] = total.astype(BF16)
+                return carry
+
+            lax.fori_loop(0, outer, block, 0)
+
+        def fold(self):
+            self.fold_copy(1).arrive()
+            self.add(fold_second, (1,))
+            self.fold_copy(2).start()
 
         def pass_on(self):
-            for step in near_steps:
-                self.near_copy(step).wait_recv()
-
-            def block(step, carry):
-                total = self.pair[step, near].astype(F32)
-                for other in near_steps:
-                    total = total + self.near[other - 1, step].astype(F32)
-                self.pair[step, near] = total.astype(BF16)
-                return carry
-
-            lax.fori_loop(0, outer, block, 0)
+            if self.folds:
+                self.fold_copy(0).arrive()
+                self.fold_copy(2).arrive()
+                self.add(near, (0, 2))
+            else:
+                for step in near_steps:
+                    self.near_copy(step).arrive()
+                self.add(near, [step - 1 for step in near_steps])
             for step in far_steps:
-                start(self.far_copy(step))
+                self.far_copy(step).start()
 
         def collect(self):
             for step in far_steps:
-                self.far_copy(step).wait_recv()
+                self.far_copy(step).arrive()
             total = self.pair[far, near].astype(F32)
             for step in far_steps:
                 total = total + self.far[step - 1].astype(F32)
             self.done[core] = total
-            start(self.done_copy(core))
+            self.done_copy().start()
 
         def end(self):
-            self.done_copy(1 - core).wait_recv()
-
-    early = Sum("early")
-    vector_sum = Sum("vector")
-    column_sum = Sum("column")
-    step_sum = Sum("step")
-    gathers = {name: Gather(name) for name in MATRICES}
-    sums = {name: Reduce(name) for name in MATRICES}
+            self.done_copy().arrive()
+
+    early = Sum("early", 1)
+    late = Sum("late", 1)
+    vector_sum = Sum("vector", 2)
+    column_sum = Sum("column", 1)
+    last_sum = Sum("last", 2)
+    step_sum = Sum("step", 2)
+    gathers = {name: Gather(name, name == ATTEND) for name in MATRICES}
+    sums = {name: Reduce(name, name in FOLDED) for name in REDUCED}
     shards = {name: getattr(r, name + "_weight") for name in MATRICES}
 
     gathers[ATTEND].place(shards[ATTEND])
@@ -696,182 +834,184 @@
 
 
     columns_of = {name: getattr(r, name + "_columns").shape[1] * outer * GROUP for name in MATRICES}
-    places, _ = spread_rows(width, columns_of)
-    r.early_own[...] = jnp.zeros_like(r.early_own)
-    r.spread[...] = jnp.zeros_like(r.spread)
-    for name in MATRICES:
-        row, count = places[name]
-        own = getattr(r, name + "_columns")
-        size = own.shape[1]
-        if count == 1:
-            r.early_own[row : row + 1, 0:size] = own[...]
-        else:
+    late_at = late_places(columns_of, width)
+    column_at = column_places(columns_of, width)
+
+    def early_value():
+        thin = r.vectors_own.shape[1]
+        r.packed[...] = jnp.zeros_like(r.packed)
+        r.packed[0:6, 0:thin] = r.vectors_own[...]
+        vectors = pltpu.roll(r.packed[0:8, :], chip * thin, 1)
+        r.packed[0:8, :] = vectors
+        for at, name in enumerate(MATRICES):
+            lanes = slice(at * 128, at * 128 + 128)
+            shard = shards[name][...]
+            r.packed[SQUARES : SQUARES + 1, lanes] = fold_lanes(
+                jnp.sum(fold_rows(shard * shard), axis=0, keepdims=True)
+            )
+            total = jnp.sum(getattr(r, name + "_rows")[...], axis=1, keepdims=True)
+            first_lane = lax.broadcasted_iota(jnp.int32, (1, 128), 1) == 0
+            r.packed[ROW_SUMS : ROW_SUMS + 1, lanes] = jnp.where(first_lane, total, 0.0)
+        return r.packed[0:EARLY_ROWS, :]
+
+    def late_value():
+        thin = r.vectors_own.shape[1]
+        r.packed[...] = jnp.zeros_like(r.packed)
+        r.packed[0:6, 0:thin] = r.moments_own[...]
+        for name in (MERGER, SHRINK):
+            row, _ = late_at[name]
+            r.packed[row : row + 1, 0:thin] = getattr(r, name + "_columns")[...]
+        r.packed[0:8, :] = pltpu.roll(r.packed[0:8, :], chip * thin, 1)
+        for name in (ATTEND, EXPAND):
+            own = getattr(r, name + "_columns")
+            size = own.shape[1]
+            r.spread[...] = jnp.zeros_like(r.spread)
             r.spread[0:1, 0:size] = own[...]
             whole = pltpu.roll(r.spread[:, : columns_of[name]], chip * size, 1)[0:1, :]
-            split_into(r.early_wide, row, whole, width)
-            r.spread[0:1, 0:size] = jnp.zeros_like(own)
-        at = MATRICES.index(name) * 128
-        shard = shards[name][...]
-        r.early_wide[SQUARES : SQUARES + 1, at : at + 128] = fold_lanes(
-            jnp.sum(fold_rows(shard * shard), axis=0, keepdims=True)
-        )
-        rows_old = getattr(r, name + "_rows")
-        sums_row = jnp.broadcast_to(jnp.sum(rows_old[...], axis=1, keepdims=True), (1, 128))
-        first_lane = lax.broadcasted_iota(jnp.int32, (1, 128), 1) == 0
-        r.early_wide[ROW_SUMS : ROW_SUMS + 1, at : at + 128] = jnp.where(first_lane, sums_row, 0.0)
-    thin = r.vectors_own.shape[1]
-    r.early_own[VECTORS : VECTORS + 6, 0:thin] = r.vectors_own[...]
-    r.early_own[MOMENTS : MOMENTS + 6, 0:thin] = r.moments_own[...]
-    narrow = pltpu.roll(r.early_own[...], chip * thin, 1)
-    kind = lax.broadcasted_iota(jnp.int32, narrow.shape, 0)
-    taken = kind >= VECTORS
-    for name in MATRICES:
-        row, count = places[name]
-        if count == 1:
-            taken = taken | (kind == row)
-    filled = kind <= ROW_SUMS
-    early.begin(
-        jnp.where(taken, narrow, jnp.where(filled, r.early_wide[...], 0.0))
-    )
+            split_into(r.packed, late_at[name][0], whole, width)
+        return r.packed[...]
 
 
     for name in (MERGER, EXPAND, SHRINK):
         gathers[name].place(shards[name])
+    gathers[ATTEND].near_start(0)
     load_tokens.wait()
     prepare(r)
     gathers[ATTEND].turn()
-    gathers[MERGER].begin()
-    gathers[EXPAND].begin()
-    early.turn()
+    for name in (MERGER, EXPAND, SHRINK):
+        gathers[name].begin()
     gathers[ATTEND].pass_on()
-    gathers[SHRINK].begin()
+    early.begin(early_value())
+    gathers[MERGER].turn()
     gathers[ATTEND].end()
     project(r)
-    gathers[MERGER].turn()
     gathers[EXPAND].turn()
 
-    def second_hook():
+    def early_hook():
+        early.turn()
+
+    def shrink_gather_hook():
         gathers[SHRINK].turn()
 
-    def third_hook():
+    def merger_gather_hook():
         gathers[MERGER].pass_on()
 
-    attend_forward(r, ((1, second_hook), (2, third_hook)))
+    attend_forward(r, ((1, early_hook), (2, shrink_gather_hook), (3, merger_gather_hook)))
     gathers[EXPAND].pass_on()
+    early_all = early.end()
+    r.early[...] = early_all
+    r.vectors[...] = early_all.astype(BF16).astype(F32)
+    late.begin(late_value())
+    gathers[MERGER].end()
+    gathers[EXPAND].end()
+    first_half(r)
+    late.turn()
     gathers[SHRINK].pass_on()
-    r.early[...] = early.end()
-    r.vectors[...] = r.early[VECTORS : VECTORS + 8, :].astype(BF16).astype(F32)
-    for name in (MERGER, EXPAND, SHRINK):
-        gathers[name].end()
     load_cotangent.wait()
-    feed_forward(r)
+    gathers[SHRINK].end()
+    second_half(r)
     store_result = local(r.result, r.result_out, 0)
     store_result.start()
-
-
-    r.vector_pair[core] = vector_total(r)
-    vector_copy = remote(
-        r.vector_pair.at[core], r.vector_pair.at[core], sibling,
-        r.vector_sends, r.vector_receives, GROUP + outer,
-    )
-    vector_copy.start()
+    r.late[...] = late.end()
+
+
     shrink_gradient(r)
     sums[SHRINK].begin()
+    way_back(r)
+    sums[SHRINK].turn()
+    vector_sum.begin(vector_total(r))
     expand_gradient(r)
     sums[EXPAND].begin()
-    sums[SHRINK].turn()
     merger_gradient(r)
     sums[MERGER].begin()
     sums[EXPAND].turn()
-    remote(
-        r.vector_pair.at[1 - core], r.vector_pair.at[1 - core], sibling,
-        r.vector_sends, r.vector_receives, GROUP + outer,
-    ).wait_recv()
-    vector_sum.begin(r.vector_pair[0] + r.vector_pair[1])
-
-    def merger_hook():
+
+    def hook_one():
+        sums[SHRINK].fold()
+        vector_sum.turn()
+
+    def hook_two():
         sums[MERGER].turn()
-        vector_sum.turn()
-
-    def shrink_hook():
+
+    def hook_three():
+        attend_gradient(r, 0)
+        sums[LOW].begin()
+
+    def hook_four():
         sums[SHRINK].pass_on()
-
-    attend_backward(r, ((1, merger_hook), (3, shrink_hook)))
-    attend_gradient(r)
-    sums[ATTEND].begin()
+        sums[LOW].turn()
+
+    def hook_five():
+        sums[EXPAND].fold()
+
+    attend_backward(
+        r, ((1, hook_one), (2, hook_two), (4, hook_three), (5, hook_four), (6, hook_five))
+    )
+    attend_gradient(r, 1)
+    sums[HIGH].begin()
     sums[EXPAND].pass_on()
-    sums[ATTEND].turn()
     sums[MERGER].pass_on()
+    sums[HIGH].turn()
     input_gradient(r)
     store_input = local(r.straight, r.input_out, 1)
     store_input.start()
     r.vector_out[...] = vector_sum.end()
+
+
+    def keep(name, whole):
+        getattr(r, "out_" + name)[...] = whole
+        squares = jnp.sum(whole * whole, axis=0, keepdims=True)
+        split_into(r.packed, column_at[name][0], squares, width)
+
     sums[SHRINK].collect()
+    sums[LOW].pass_on()
     sums[EXPAND].collect()
-    sums[ATTEND].pass_on()
     sums[MERGER].collect()
-    sums[ATTEND].collect()
-
-
-    r.column_near[near] = jnp.zeros(r.column_near.shape[1:], F32)
-    grads = {}
-    for name in (SHRINK, EXPAND, MERGER, ATTEND):
+    r.packed[...] = jnp.zeros_like(r.packed)
+    for name in (SHRINK, EXPAND, MERGER):
         sums[name].end()
-        if name == SHRINK:
-            whole = flat(r.done_shrink[...]).T
-        else:
-            whole = flat(getattr(r, "done_" + name)[...])
-        grads[name] = whole
-        getattr(r, "out_" + name)[...] = whole
-        row, _ = places[name]
-        squares = jnp.sum(whole * whole, axis=0, keepdims=True)
-        split_into(r.column_near.at[near], row, squares, width)
-    column_sum.begin()
+        whole = flat(getattr(r, "done_" + name)[...])
+        keep(name, whole.T if name == SHRINK else whole)
+    column_sum.begin(r.packed[0:COLUMN_ROWS, :])
+    sums[HIGH].pass_on()
+    sums[LOW].collect()
     column_sum.turn()
-    r.column_out[...] = column_sum.end()
+    sums[HIGH].collect()
+    attend_half = heads_together([getattr(r, "done_" + name)[core] for name in (LOW, HIGH)])
+    squares = jnp.sum(attend_half * attend_half, axis=0, keepdims=True)
+    split_into(r.packed, 0, squares, width)
+    last_sum.begin(r.packed[0:COLUMN_ROWS, :])
+    sums[LOW].end()
+    sums[HIGH].end()
+    r.out_attend[...] = heads_together([flat(getattr(r, "done_" + name)[...]) for name in (LOW, HIGH)])
+    r.column_out[0:COLUMN_ROWS, :] = column_sum.end()
+    last_sum.turn()
     r.early_out[...] = r.early[...]
-    norm, clip, squares = clip_of(r.column_out, places, r.vector_out[...])
+    r.late_out[...] = r.late[...]
+    r.column_out[COLUMN_ROWS : 2 * COLUMN_ROWS, :] = last_sum.end()
+    facts = Statistics(r, layout_sizes, r.column_out, r.vector_out[...])
+
+    def my_half(value):
+        half = value.shape[0] // 2
+        return jnp.where(core == 0, value[:half], value[half:])
+
+    rows = []
     for name in MATRICES:
-        rows_all = float(getattr(r, name + "_rows").shape[1] * outer * GROUP)
-        _, _, _, step = factored_step(
-            name, grads[name], getattr(r, name + "_rows")[...], r.column_out, r.early, places,
-            clip, squares, rows_all,
-        )
-        at = MATRICES.index(name)
-        r.step_near[near, at : at + 1, :] = fold_lanes(
-            jnp.sum(step * step, axis=0, keepdims=True)
-        )
-    r.step_near[near, 4:8, :] = jnp.zeros((4, 128), F32)
-    step_sum.begin()
+        rows_old = getattr(r, name + "_rows")[...]
+        whole = getattr(r, "out_" + name)
+        half = whole.shape[0] // 2
+        mine = whole[pl.ds(pl.multiple_of(core * half, half), half), :]
+        step = facts.factored(
+            name, mine, my_half(column_of(rows_old)), float(rows_old.shape[1] * outer * GROUP)
+        )[3]
+        rows.append(fold_lanes(jnp.sum(step * step, axis=0, keepdims=True)))
+    step_sum.begin(jnp.concatenate(rows + [jnp.zeros((4, 128), F32)], axis=0))
     step_sum.turn()
     r.step_out[...] = step_sum.end()
 
 
-    for name in MATRICES:
-        gather, total = gathers[name], sums[name]
-        for step in far_steps:
-            gather.far_copy(step, far).wait_send()
-            total.far_copy(step).wait_send()
-        for step in near_steps:
-            for hop in range(outer):
-                gather.near_piece(step, hop, near, core).wait_send()
-            total.near_copy(step).wait_send()
-        for step in range(GROUP):
-            gather.cross(step, core, at_near(step) if step else near).wait_send()
-        total.pair_copy().wait_send()
-        total.done_copy(core).wait_send()
-    for small in (early, vector_sum, column_sum, step_sum):
-        for step in near_steps:
-            slot = small.near.at[near]
-            remote(
-                slot, slot, near_device(step), small.sends, small.receives, step - 1
-            ).wait_send()
-        for step in far_steps:
-            slot = small.far.at[far]
-            remote(
-                slot, slot, far_device(step), small.sends, small.receives, GROUP + step - 1
-            ).wait_send()
-    vector_copy.wait_send()
+    for copy in started.values():
+        copy.leave()
     store_result.wait()
     store_input.wait()
 
@@ -880,8 +1020,6 @@
     outer, width, wide = layout_sizes
     r = Refs(names, refs)
     chip = lax.axis_index(FSDP)
-    columns_of = {name: getattr(r, name + "_columns").shape[1] * outer * GROUP for name in MATRICES}
-    places, _ = spread_rows(width, columns_of)
     copies = [
         pltpu.make_async_copy(r.result_in, r.block_output, r.sems.at[0]),
         pltpu.make_async_copy(r.input_in, r.input_gradient, r.sems.at[1]),
@@ -889,21 +1027,18 @@
     for copy in copies:
         copy.start()
     vector_gradient = r.vector_sum[...]
-    norm, clip, squares = clip_of(r.column_sum, places, vector_gradient)
-    r.global_norm[...] = norm
+    facts = Statistics(r, layout_sizes, r.column_sum, vector_gradient)
+    r.global_norm[...] = facts.norm
     for name in MATRICES:
         weight = getattr(r, name + "_weight")[...]
         rows_all = float(weight.shape[0] * outer * GROUP)
         count = rows_all * weight.shape[1]
-        clipped, new_rows, new_columns, step = factored_step(
-            name, getattr(r, name + "_sum")[...], getattr(r, name + "_rows")[...], r.column_sum,
-            r.early, places, clip, squares, rows_all,
+        clipped, new_rows, new_columns, step = facts.factored(
+            name, getattr(r, name + "_sum")[...], column_of(getattr(r, name + "_rows")[...]), rows_all
         )
         at = MATRICES.index(name)
         step_square = jnp.sum(r.step_sum[at : at + 1, :], axis=1, keepdims=True)
-        weight_square = jnp.sum(
-            r.early[SQUARES : SQUARES + 1, at * 128 : at * 128 + 128], axis=1, keepdims=True
-        )
+        weight_square = facts.lanes(SQUARES, name)
         shrunk = jnp.maximum(1.0, jnp.sqrt(step_square * (1.0 / count)) * (1.0 / UPDATE_LIMIT))
         stride = LEARN_RATE * jnp.maximum(0.001, jnp.sqrt(weight_square * (1.0 / count)))
         updated = weight - (stride / shrunk) * step
@@ -913,11 +1048,12 @@
         getattr(r, name + "_newrows")[...] = row_of(new_rows)
         size = getattr(r, name + "_newcols").shape[1]
         wide_row = jnp.broadcast_to(new_columns, (8, new_columns.shape[1]))
-        own = pltpu.roll(wide_row, lax.rem(new_columns.shape[1] - chip * size, columns_of[name]), 1)
+        whole = new_columns.shape[1]
+        own = pltpu.roll(wide_row, lax.rem(whole - chip * size, whole), 1)
         getattr(r, name + "_newcols")[...] = own[0:1, 0:size]
-    vectors = r.early[VECTORS : VECTORS + 8, :]
+    vectors = r.early[...]
     clipped, variance, step = vector_steps(
-        vector_gradient, r.early[MOMENTS : MOMENTS + 8, :], clip
+        vector_gradient, r.late[0:8, :], facts.clip
     )
     shrunk = jnp.maximum(1.0, jnp.sqrt(lane_mean(step * step)) * (1.0 / UPDATE_LIMIT))
     stride = LEARN_RATE * jnp.maximum(0.001, jnp.sqrt(lane_mean(vectors * vectors)))
@@ -974,7 +1110,8 @@
         input_out=shape((slots, width), F32),
         vector_out=shape((8, width), F32),
         early_out=shape((EARLY_ROWS, width), F32),
-        column_out=shape((COLUMN_ROWS, width), F32),
+        late_out=shape((LATE_ROWS, width), F32),
+        column_out=shape((2 * COLUMN_ROWS, width), F32),
         step_out=shape((8, 128), F32),
         **{"out_" + name: shape(weights[name].shape, F32) for name in MATRICES},
     )
@@ -985,36 +1122,42 @@
         straight=pltpu.VMEM((slots, width), F32),
         vectors=pltpu.VMEM((8, width), F32),
         early=pltpu.VMEM((EARLY_ROWS, width), F32),
-        early_own=pltpu.VMEM((EARLY_ROWS, width), F32),
-        early_wide=pltpu.VMEM((EARLY_ROWS, width), F32),
+        late=pltpu.VMEM((LATE_ROWS, width), F32),
+        packed=pltpu.VMEM((LATE_ROWS, width), F32),
         spread=pltpu.VMEM((8, wide), F32),
-        vector_pair=pltpu.VMEM((2, 8, width), F32),
         local_sems=pltpu.SemaphoreType.DMA((2,)),
     )
-    for name, size in (
-        ("early", (EARLY_ROWS, width)),
-        ("vector", (8, width)),
-        ("column", (COLUMN_ROWS, width)),
-        ("step", (8, 128)),
+    for name, cores, size in (
+        ("early", 1, (EARLY_ROWS, width)),
+        ("late", 1, (LATE_ROWS, width)),
+        ("vector", 2, (8, width)),
+        ("column", 1, (COLUMN_ROWS, width)),
+        ("last", 2, (COLUMN_ROWS, width)),
+        ("step", 2, (8, 128)),
     ):
-        scratch[name + "_near"] = pltpu.VMEM((GROUP,) + size, F32)
+        scratch[name + "_near"] = pltpu.VMEM((cores, GROUP) + size, F32)
         scratch[name + "_far"] = pltpu.VMEM((outer,) + size, F32)
-        scratch[name + "_sends"] = pltpu.SemaphoreType.DMA((GROUP + outer + 1,))
-        scratch[name + "_receives"] = pltpu.SemaphoreType.DMA((GROUP + outer + 1,))
+        for way in ("_sends", "_receives"):
+            scratch[name + way] = pltpu.SemaphoreType.DMA((2 * GROUP + outer,))
     for name in MATRICES:
         held, wide_now = weights[name].shape
         scratch[name] = pltpu.VMEM((outer, GROUP, 2, held // 2, wide_now), BF16)
+        for way in ("_sends", "_receives"):
+            scratch[name + way] = pltpu.SemaphoreType.DMA((GROUP * outer + GROUP,))
+    for name in REDUCED:
+        held, wide_now = weights[ATTEND if name in (LOW, HIGH) else name].shape
         half = (held // 2, wide_now)
         if name == SHRINK:
             half = (wide_now // 2, held)
+        elif name in (LOW, HIGH):
+            half = (held // 2, wide_now // 2)
         scratch["g_" + name] = pltpu.VMEM((outer, GROUP, 2) + half, BF16)
         scratch["pair_" + name] = pltpu.VMEM((outer, GROUP) + half, BF16)
         scratch["near_" + name] = pltpu.VMEM((GROUP - 1, outer) + half, BF16)
         scratch["far_" + name] = pltpu.VMEM((max(1, outer - 1),) + half, BF16)
         scratch["done_" + name] = pltpu.VMEM((2,) + half, F32)
-        for kind, count in (("", GROUP * outer + GROUP), ("sum_", GROUP + outer + 1)):
-            for way in ("_sends", "_receives"):
-                scratch[kind + name + way] = pltpu.SemaphoreType.DMA((count,))
+        for way in ("_sends", "_receives"):
+            scratch["sum_" + name + way] = pltpu.SemaphoreType.DMA((GROUP + outer + 1,))
     got = call(
         shard_kernel, sizes, inputs, outputs, scratch,
         ("tokens_in", "cotangent_in", "result_out", "input_out"),
@@ -1025,7 +1168,7 @@
     )
     inputs = dict(
         result_in=got["result_out"], input_in=got["input_out"], vector_sum=got["vector_out"],
-        early=got["early_out"], column_sum=got["column_out"], step_sum=got["step_out"],
+        early=got["early_out"], late=got["late_out"], column_sum=got["column_out"], step_sum=got["step_out"],
         **{name + "_sum": got["out_" + name] for name in MATRICES},
         **weight_in, **row_in, **column_in,
     )
@@ -1044,8 +1187,8 @@
         outputs[name] = shape(vectors.shape, F32)
     out = call(
         update_kernel, sizes, inputs, outputs, dict(sems=pltpu.SemaphoreType.DMA((2,))),
-        ("result_in", "input_in", "block_output", "input_gradient"),
-        pltpu.CompilerParams(vmem_limit_bytes=VMEM_LIMIT // 2),
+        ("block_output", "input_gradient"),
+        pltpu.CompilerParams(vmem_limit_bytes=VMEM_LIMIT),
         "update",
     )
     out["block_output"] = out["block_output"][None]
@@ -1062,13 +1205,17 @@
     prepare(r)
     project(r)
     attend_forward(r, ())
-    feed_forward(r)
+    first_half(r)
+    second_half(r)
+    shrink_gradient(r)
+    way_back(r)
     r.g_vectors[...] = vector_total(r)
-    shrink_gradient(r)
     expand_gradient(r)
     merger_gradient(r)
     attend_backward(r, ())
-    attend_gradient(r)
+    r.g_attend = (r.g_attend_low, r.g_attend_high)
+    attend_gradient(r, 0)
+    attend_gradient(r, 1)
     input_gradient(r)
 
 
@@ -1089,7 +1236,8 @@
         result=shape((slots, width), BF16),
         straight=shape((slots, width), F32),
         g_vectors=shape((8, width), F32),
-        g_attend=shape((width, 3 * width), BF16),
+        g_attend_low=shape((width, 3 * width // 2), BF16),
+        g_attend_high=shape((width, 3 * width // 2), BF16),
         g_merger=shape((width, width), BF16),
         g_expand=shape((width, wide), BF16),
         g_shrink=shape((width, wide), BF16),
@@ -1107,6 +1255,7 @@
         name="row",
     )(*inputs.values())
     got = dict(zip(outputs, got, strict=True))
+    got["g_" + ATTEND] = heads_together((got["g_attend_low"], got["g_attend_high"]))
     grads = []
     for name in MATRICES:
         value = lax.psum(got["g_" + name], DP).astype(F32)

time: 164 us -> 136 us (0.83)
  Pallas kernels: 153 us -> 135 us
  local copies, waits for them, and re-layouts: 9.5 us -> 0 us
    pallas_call x2, Pallas kernels: 153 us -> 135 us  [call(): pl.pallas_call(functools.partial(kernel, sizes, names), in_specs=[anywher...]
    unnamed x44 -> x0, local copies, waits for them, and re-layouts: 9.5 us -> none
where the time goes in v2:
time: 136 us
  Pallas kernels  135 us (99%)
    pallas_call x2, Pallas kernels, call(): pl.pallas_call(functools.partial(kernel, sizes, names), in_specs=[anywher...  135 us

profile of v2, /device:TPU:0, one launch (start us, length us, event | category | flops | bytes accessed | tf_op | source)
XLA Modules:
  0.0 135.9 jit_solution(16471538026126644890)
XLA Ops:
  0.7 129.6 %row_and_sums.1 = (bf16[1024,512]{1,0:T(8,128)(2,1)}, f32[1024,512]{1,0:T(8,128)}, f32[8,512]{1,0:T(8,128)}, f32[8,512]{1,0:T(8,128)}, f32[16,512]{1,0:T(8,128)}...) custom-call(bf16[1024,512]{1,0:T(8,128)(2,1)} %bitcast.21, ...), custom_call_target="tpu_custom_call" | custom-call | tf_op jit(solution)/shard_map/row_and_sums/pallas_call | solution.py:1083
  130.3 5.5 %update.1 = (bf16[1024,512]{1,0:T(8,128)(2,1)}, f32[1024,512]{1,0:T(8,128)}, f32[1,1]{1,0:T(1,128)}, f32[32,1536]{1,0:T(8,128)}, f32[1,32]{1,0:T(1,128)}, /*inde...) custom-call(bf16[1024,512]{1,0:T(8,128)(2,1)} %get-tuple-element.63., ...), custom_call_target="tpu_custom_call" | custom-call | tf_op jit(solution)/shard_map/update/pallas_call | solution.py:1083

commit v3 on v2

--- a/solution.py
+++ b/solution.py
@@ -23,7 +23,7 @@
 GELU_B = 0.044715 * GELU_A
 
 REACH = 256
-QUERY_BLOCK = 256
+QUERY_BLOCK = 128
 TILE = 256
 GROUP = 4
 DP, FSDP = "dp", "fsdp"
@@ -53,6 +53,10 @@
 
 def flat(value):
     return value.reshape(-1, value.shape[-1])
+
+
+def whole(parts):
+    return jnp.concatenate([flat(part[...]) for part in parts], axis=1)
 
 
 def fold_rows(value):
@@ -126,24 +130,19 @@
         r.mask[place : place + high - low, :] = jnp.where(fits, 1.0, 0.0).astype(BF16)
 
 
-def project(r):
+def project(r, part):
     width = r.tokens.shape[1]
-
-    def tile(step, carry):
-        columns = aligned(step * TILE, TILE)
-        r.projected_t[columns, :] = dot_tn(flat(r.attend[..., columns]), r.tokens_t[...]).astype(
-            BF16
-        )
-        return carry
-
-    lax.fori_loop(0, 3 * width // TILE, tile, 0)
-
-    def turn(step, carry):
-        columns = aligned(step * TILE, TILE)
-        r.key_value[:, columns] = r.projected_t[aligned(width + step * TILE, TILE), :].T
-        return carry
-
-    lax.fori_loop(0, 2 * width // TILE, turn, 0)
+    half = width // 2
+    columns = flat(r.attend[part][...])
+    for at in range(3):
+        rows = slice(at * width + part * half, at * width + (part + 1) * half)
+        value = dot_tn(columns[:, at * half : (at + 1) * half], r.tokens_t[...]).astype(BF16)
+        r.projected_t[rows, :] = value
+    for at in range(2):
+        start = at * width + part * half
+        r.key_value[:, start : start + half] = r.projected_t[
+            width + start : width + start + half, :
+        ].T
 
 
 def beside_zeros(value, head):
@@ -151,99 +150,142 @@
     return jnp.concatenate([value, zeros] if head == 0 else [zeros, value], axis=0)
 
 
-def attend_forward(r, hooks):
+def head_rows(part, width, pair, head):
+    return pl.ds(pl.multiple_of(part * width + pair * 128 + HEAD_DIM * head, HEAD_DIM), HEAD_DIM)
+
+
+def by_pairs(first, last, hooks, body):
+    def pair(step, carry):
+        for at, hook in hooks:
+            pl.when(step == at)(hook)
+        body(step)
+        return carry
+
+    lax.fori_loop(first, last, pair, 0)
+
+
+def attend_forward(r, first_pair, last_pair, hooks):
     slots, width = r.tokens.shape
     factor = HEAD_DIM ** -0.5 * LOG2_E
-
-    def pair(step, carry):
-        start = pl.multiple_of(step * 128, 128)
-        for head in (0, 1):
-            for at, hook in hooks:
-                if at % 2 == head:
-                    pl.when(step == at // 2)(hook)
-            for first, low, high, place in band(slots)[0]:
-                keys = r.key_value[low:high, pl.ds(start, 128)]
-                fits = r.mask[place : place + high - low, :].astype(F32) > 0.5
-                mine = pl.ds(start + 64 * head, 64)
-                queries = r.projected_t[mine, first : first + QUERY_BLOCK]
-                scores = dot_nn(keys, beside_zeros(queries, head))
-                scores = jnp.where(fits, scores * factor, NEGATIVE)
-                highest = jnp.max(scores, axis=0, keepdims=True)
-                weights = jnp.exp2(scores - highest)
-                inverse = 1.0 / jnp.sum(weights, axis=0, keepdims=True)
-                probs = (weights * inverse).astype(BF16)
-                r.probs[2 * step + head, place : place + high - low, :] = probs
-                values = r.projected_t[pl.ds(2 * width + start + 64 * head, 64), low:high]
-                r.context_t[mine, first : first + QUERY_BLOCK] = dot_nn(values, probs).astype(BF16)
-        return carry
-
-    lax.fori_loop(0, width // 128, pair, 0)
-
-
-def attend_backward(r, hooks):
+    items = [(head,) + piece for head in (0, 1) for piece in band(slots)[0]]
+
+    def body(pair):
+        lanes = pl.ds(pl.multiple_of(pair * 128, 128), 128)
+
+        def scores_of(item):
+            head, first, low, high, _ = item
+            queries = r.projected_t[head_rows(0, width, pair, head), first : first + QUERY_BLOCK]
+            return dot_nn(r.key_value[low:high, lanes], beside_zeros(queries, head))
+
+        def probs_of(item, scores):
+            head, _, low, high, place = item
+            fits = r.mask[place : place + high - low, :].astype(F32) > 0.5
+            scores = jnp.where(fits, scores * factor, NEGATIVE)
+            weights = jnp.exp2(scores - jnp.max(scores, axis=0, keepdims=True))
+            inverse = 1.0 / jnp.sum(weights, axis=0, keepdims=True)
+            probs = (weights * inverse).astype(BF16)
+            r.probs[2 * pair + head, place : place + high - low, :] = probs
+            return probs
+
+        def put_context(item, probs):
+            head, first, low, high, _ = item
+            values = r.projected_t[head_rows(2, width, pair, head), low:high]
+            r.context_t[head_rows(0, width, pair, head), first : first + QUERY_BLOCK] = dot_nn(
+                values, probs
+            ).astype(BF16)
+
+        scores = [scores_of(item) for item in items]
+        probs = [probs_of(item, value) for item, value in zip(items, scores)]
+        for item, value in zip(items, probs):
+            put_context(item, value)
+
+    by_pairs(first_pair, last_pair, hooks, body)
+
+
+def attend_backward(r, first_pair, last_pair, hooks):
     slots, width = r.tokens.shape
     scale = HEAD_DIM ** -0.5
-
-    def pair(step, carry):
-        start = pl.multiple_of(step * 128, 128)
-        for head in (0, 1):
-            for at, hook in hooks:
-                if at % 2 == head:
-                    pl.when(step == at // 2)(hook)
-            mine = pl.ds(start + 64 * head, 64)
-            mine_keys = pl.ds(width + start + 64 * head, 64)
-            mine_values = pl.ds(2 * width + start + 64 * head, 64)
-            queries = r.projected_t[mine, :]
-            keys_t = r.projected_t[mine_keys, :]
-            upstream = r.d_context_t[mine, :]
-            open_keys = None
-            open_values = None
-            for first, low, high, place in band(slots)[0]:
-                values = r.key_value[low:high, pl.ds(width + start, 128)]
-                arriving = upstream[:, first : first + QUERY_BLOCK]
-                d_probs = dot_nn(values, beside_zeros(arriving, head))
-                probs = r.probs[2 * step + head, place : place + high - low, :]
-                wide = probs.astype(F32)
-                inner = jnp.sum(wide * d_probs, axis=0, keepdims=True)
-                d_scores = (wide * (d_probs - inner)).astype(BF16)
-                r.projected_t[mine, first : first + QUERY_BLOCK] = (
-                    dot_nn(keys_t[:, low:high], d_scores) * scale
-                ).astype(BF16)
-                d_keys = dot_nt(queries[:, first : first + QUERY_BLOCK], d_scores)
-                d_values = dot_nt(arriving, probs)
-                done = first - low
-                if done:
-                    r.projected_t[mine_keys, low:first] = (
-                        (open_keys + d_keys[:, :done]) * scale
-                    ).astype(BF16)
-                    r.projected_t[mine_values, low:first] = (
-                        open_values + d_values[:, :done]
-                    ).astype(BF16)
-                open_keys = d_keys[:, done:]
-                open_values = d_values[:, done:]
-            r.projected_t[mine_keys, slots - QUERY_BLOCK :] = (open_keys * scale).astype(BF16)
-            r.projected_t[mine_values, slots - QUERY_BLOCK :] = open_values.astype(BF16)
-        return carry
-
-    lax.fori_loop(0, width // 128, pair, 0)
+    pieces = band(slots)[0]
+    count = len(pieces)
+    items = [(head, at) for head in (0, 1) for at in range(count)]
+
+    def body(pair):
+        lanes = pl.ds(pl.multiple_of(width + pair * 128, 128), 128)
+        queries = [r.projected_t[head_rows(0, width, pair, head), :] for head in (0, 1)]
+        keys_t = [r.projected_t[head_rows(1, width, pair, head), :] for head in (0, 1)]
+        upstream = [r.d_context_t[head_rows(0, width, pair, head), :] for head in (0, 1)]
+
+        def probs_of(item):
+            _, low, high, place = pieces[item[1]]
+            return r.probs[2 * pair + item[0], place : place + high - low, :]
+
+        def d_probs_of(item):
+            first, low, high, _ = pieces[item[1]]
+            arriving = upstream[item[0]][:, first : first + QUERY_BLOCK]
+            return dot_nn(r.key_value[low:high, lanes], beside_zeros(arriving, item[0]))
+
+        def d_scores_of(item, d_probs):
+            wide = probs_of(item).astype(F32)
+            inner = jnp.sum(wide * d_probs, axis=0, keepdims=True)
+            return (wide * (d_probs - inner)).astype(BF16)
+
+        def put_queries(item, d_scores):
+            first, low, high, _ = pieces[item[1]]
+            value = dot_nn(keys_t[item[0]][:, low:high], d_scores) * scale
+            r.projected_t[
+                head_rows(0, width, pair, item[0]), first : first + QUERY_BLOCK
+            ] = value.astype(BF16)
+
+        def put_keys_and_values(item, known):
+            head, at = item
+            begin = pieces[at][0]
+            seen = [i for i in range(count) if pieces[i][1] <= begin <= pieces[i][0]]
+            span = slice(pieces[seen[0]][0], pieces[seen[-1]][0] + QUERY_BLOCK)
+            here = slice(begin, begin + QUERY_BLOCK)
+
+            def together(values):
+                parts = []
+                for i, value in zip(seen, values):
+                    start = begin - pieces[i][1]
+                    parts.append(value[start : start + QUERY_BLOCK, :])
+                return jnp.concatenate(parts, axis=1)
+
+            d_scores = together([known[(head, i)] for i in seen])
+            probs = together([probs_of((head, i)) for i in seen])
+            r.projected_t[head_rows(1, width, pair, head), here] = (
+                dot_nt(queries[head][:, span], d_scores) * scale
+            ).astype(BF16)
+            r.projected_t[head_rows(2, width, pair, head), here] = dot_nt(
+                upstream[head][:, span], probs
+            ).astype(BF16)
+
+        d_probs = [d_probs_of(item) for item in items]
+        known = {item: d_scores_of(item, value) for item, value in zip(items, d_probs)}
+        for item in items:
+            put_queries(item, known[item])
+        for item in items:
+            put_keys_and_values(item, known)
+
+    by_pairs(first_pair, last_pair, hooks, body)
 
 
 def vector_rows(r):
     return [r.vectors[place : place + 1, :] for place in range(6)]
 
 
-def by_tokens(r, body):
-    def block(step, carry):
-        body(step, aligned(step * TILE, TILE))
-        return carry
-
-    lax.fori_loop(0, r.tokens.shape[0] // TILE, block, 0)
+def token_blocks(r):
+    return [slice(start, start + TILE) for start in range(0, r.tokens.shape[0], TILE)]
+
+
+def keep_sums(r, places, folded):
+    for place, parts in zip(places, zip(*folded)):
+        r.vector_sums[place] = sum(parts[1:], parts[0])
 
 
 def first_half(r):
     omega_one, gain_one, shift_one = vector_rows(r)[:3]
 
-    def body(step, rows):
+    def front(rows):
         inputs = r.tokens[rows, :].astype(F32)
         first_sum = omega_one * inputs + dot_tn(r.context_t[:, rows], flat(r.merger[...]))
         centered = first_sum - lane_mean(first_sum)
@@ -253,68 +295,88 @@
         r.straight[rows, :] = first_normed
         first_low = (first_normed * gain_one + shift_one).astype(BF16)
         r.first_t[:, rows] = first_low.T
-        hidden = dot_nn(first_low, flat(r.expand[...]))
+        return first_low
+
+    def gelu(rows, hidden):
         square = hidden * hidden
-        bend = jnp.tanh(hidden * (GELU_A + GELU_B * square))
-        half = 0.5 * hidden
-        lifted = 1.0 + bend
-        r.active[rows, :] = (half * lifted).astype(BF16)
-        slope = 0.5 * lifted + half * (1.0 - bend * bend) * (GELU_A + 3 * GELU_B * square)
+        part = 0.5 + 0.5 * jnp.tanh(hidden * (GELU_A + GELU_B * square))
+        active = hidden * part
+        r.active[rows, :] = active.astype(BF16)
+        slope = part + active * (1.0 - part) * (2 * GELU_A + 6 * GELU_B * square)
         r.d_hidden[rows, :] = slope.astype(BF16)
 
-    by_tokens(r, body)
+    blocks = token_blocks(r)
+    lows = [front(rows) for rows in blocks]
+    for rows, low in zip(blocks, lows):
+        gelu(rows, dot_nn(low, whole(r.expand)))
 
 
 def second_half(r):
     _, gain_one, shift_one, omega_two, gain_two, shift_two = vector_rows(r)
-    r.vector_sums[...] = jnp.zeros_like(r.vector_sums)
-
-    def body(step, rows):
+
+    def rest(rows, product):
         first_out = r.straight[rows, :] * gain_one + shift_one
-        second_sum = omega_two * first_out + dot_nn(r.active[rows, :], flat(r.shrink[...]))
+        second_sum = omega_two * first_out + product
         centered = second_sum - lane_mean(second_sum)
         second_inv = lax.rsqrt(lane_mean(centered * centered) + EPSILON)
         second_normed = centered * second_inv
         arriving = r.cotangent[rows, :].astype(F32)
         r.result[rows, :] = (second_normed * gain_two + shift_two).astype(BF16)
-        place = (lax.broadcasted_iota(jnp.int32, (TILE, 1), 0) + step * TILE).astype(F32)
+        place = (lax.broadcasted_iota(jnp.int32, (TILE, 1), 0) + rows.start).astype(F32)
         upstream = arriving * jnp.where(place < r.total[0:1, 0:1], 1.0, 0.0)
         scaled = upstream * gain_two
         d_second = second_inv * (
             scaled - lane_mean(scaled) - second_normed * lane_mean(scaled * second_normed)
         )
-        r.vector_sums[4] += fold_rows(upstream * second_normed)
-        r.vector_sums[5] += fold_rows(upstream)
-        r.vector_sums[3] += fold_rows(first_out * d_second)
         r.d_second[rows, :] = d_second
         r.d_second_t[:, rows] = d_second.astype(BF16).T
-
-    by_tokens(r, body)
-
-
-def way_back(r):
+        return (
+            fold_rows(upstream * second_normed),
+            fold_rows(upstream),
+            fold_rows(first_out * d_second),
+        )
+
+    blocks = token_blocks(r)
+    products = [dot_nn(r.active[rows, :], whole(r.shrink)) for rows in blocks]
+    keep_sums(r, (4, 5, 3), [rest(rows, value) for rows, value in zip(blocks, products)])
+
+
+def way_back(r, hook=None):
     omega_one, gain_one, _, omega_two = vector_rows(r)[:4]
 
-    def body(step, rows):
-        d_second = r.d_second[rows, :]
-        d_active = dot_nt(d_second.astype(BF16), flat(r.shrink[...]))
+    def to_hidden(rows):
+        d_active = dot_nt(r.d_second[rows, :].astype(BF16), whole(r.shrink))
         d_hidden = (d_active * r.d_hidden[rows, :].astype(F32)).astype(BF16)
         r.d_hidden[rows, :] = d_hidden
-        d_first = dot_nt(d_hidden, flat(r.expand[...])) + omega_two * d_second
+        return d_hidden
+
+    def to_branch(rows, product):
+        d_first = product + omega_two * r.d_second[rows, :]
         first_normed = r.straight[rows, :]
-        r.vector_sums[1] += fold_rows(d_first * first_normed)
-        r.vector_sums[2] += fold_rows(d_first)
         scaled = d_first * gain_one
         d_first_sum = r.first_inv[rows, 0:1] * (
             scaled - lane_mean(scaled) - first_normed * lane_mean(scaled * first_normed)
         )
-        r.vector_sums[0] += fold_rows(r.tokens[rows, :].astype(F32) * d_first_sum)
+        inputs = r.tokens[rows, :].astype(F32)
         r.straight[rows, :] = omega_one * d_first_sum
         branch_low = d_first_sum.astype(BF16)
         r.d_branch[rows, :] = branch_low
-        r.d_context_t[:, rows] = dot_nt(flat(r.merger[...]), branch_low).astype(BF16)
-
-    by_tokens(r, body)
+        folded = (
+            fold_rows(inputs * d_first_sum),
+            fold_rows(d_first * first_normed),
+            fold_rows(d_first),
+        )
+        return branch_low, folded
+
+    blocks = token_blocks(r)
+    hidden = [to_hidden(rows) for rows in blocks]
+    if hook is not None:
+        hook()
+    products = [dot_nt(value, whole(r.expand)) for value in hidden]
+    got = [to_branch(rows, value) for rows, value in zip(blocks, products)]
+    for rows, value in zip(blocks, got):
+        r.d_context_t[:, rows] = dot_nt(flat(r.merger[...]), value[0]).astype(BF16)
+    keep_sums(r, (0, 1, 2), [value[1] for value in got])
 
 
 def vector_total(r):
@@ -322,77 +384,41 @@
     return jnp.concatenate(rows + [jnp.zeros((2, rows[0].shape[1]), F32)], axis=0)
 
 
-def by_columns(columns, store):
-    def tile(step, carry):
-        store(step)
-        return carry
-
-    lax.fori_loop(0, columns // TILE, tile, 0)
-
-
 def put_tile(ref, columns, value):
     ref[..., columns] = value.astype(ref.dtype).reshape(ref.shape[:-1] + (value.shape[1],))
 
 
-def shrink_gradient(r):
-    width, wide = r.tokens.shape[1], r.active.shape[1]
-    if len(r.g_shrink.shape) == 2:
-
-        def store(step):
-            columns = aligned(step * TILE, TILE)
-            r.g_shrink[:, columns] = dot_nn(r.d_second_t[...], r.active[:, columns]).astype(
-                r.g_shrink.dtype
-            )
-
-        by_columns(wide, store)
-        return
-    owned = r.g_shrink.shape[-1]
-    per_tile = max(1, TILE // owned)
-    span = owned * per_tile
-
-    def tile(step, carry):
-        value = dot_nn(r.d_second_t[...], r.active[:, aligned(step * span, span)]).astype(BF16)
-        for piece in range(per_tile):
-            owner = step * per_tile + piece
-            r.g_shrink[owner // GROUP, lax.rem(owner, GROUP)] = value[
-                :, piece * owned : (piece + 1) * owned
-            ].reshape(2, width // 2, owned)
-        return carry
-
-    lax.fori_loop(0, wide // span, tile, 0)
-
-
-def expand_gradient(r):
-    def store(step):
-        columns = aligned(step * TILE, TILE)
-        put_tile(r.g_expand, columns, dot_nn(r.first_t[...], r.d_hidden[:, columns]))
-
-    by_columns(r.active.shape[1], store)
+def shrink_gradient(r, part):
+    into = r.g_shrink[part]
+    half = r.tokens.shape[1] // 2
+    owned = into.shape[-1]
+    rows = r.d_second_t[part * half : (part + 1) * half, :]
+    value = dot_nn(rows, r.active[...]).astype(BF16)
+    for owner in range(value.shape[1] // owned):
+        into[owner // GROUP, owner % GROUP] = value[
+            :, owner * owned : (owner + 1) * owned
+        ].reshape(2, half // 2, owned)
+
+
+def expand_gradient(r, part):
+    half = r.active.shape[1] // 2
+    columns = slice(part * half, (part + 1) * half)
+    put_tile(r.g_expand[part], slice(None), dot_nn(r.first_t[...], r.d_hidden[:, columns]))
 
 
 def merger_gradient(r):
-    def store(step):
-        columns = aligned(step * TILE, TILE)
-        put_tile(r.g_merger, columns, dot_nn(r.context_t[...], r.d_branch[:, columns]))
-
-    by_columns(r.tokens.shape[1], store)
-
-
-def attend_gradient(r, part):
+    put_tile(r.g_merger, slice(None), dot_nn(r.context_t[...], r.d_branch[...]))
+
+
+def half_heads(r, part, slots):
     width = r.tokens.shape[1]
     half = width // 2
-    into = r.g_attend[part]
-
-    def store(step):
-        columns = aligned(step * half, half)
-        heads = r.projected_t[aligned(step * width + part * half, half), :]
-        put_tile(into, columns, dot_nt(r.tokens_t[...], heads))
-
-    def tile(step, carry):
-        store(step)
-        return carry
-
-    lax.fori_loop(0, 3, tile, 0)
+    starts = [at * width + part * half for at in range(3)]
+    return jnp.concatenate([r.projected_t[start : start + half, slots] for start in starts], axis=0)
+
+
+def attend_gradient(r, part):
+    put_tile(r.g_attend[part], slice(None), dot_nt(r.tokens_t[...], half_heads(r, part, slice(None))))
 
 
 def heads_together(parts):
@@ -402,13 +428,28 @@
     )
 
 
+def heads_apart(whole):
+    half = whole.shape[1] // 6
+    return [
+        jnp.concatenate(
+            [whole[:, (2 * at + part) * half : (2 * at + part + 1) * half] for at in range(3)],
+            axis=1,
+        )
+        for part in range(2)
+    ]
+
+
 def input_gradient(r):
-    def tile(step, carry):
-        rows = aligned(step * TILE, TILE)
-        r.straight[rows, :] += dot_nn(flat(r.attend[...]), r.projected_t[:, rows]).T
-        return carry
-
-    lax.fori_loop(0, r.tokens.shape[0] // TILE, tile, 0)
+    blocks = token_blocks(r)
+    products = []
+    for rows in blocks:
+        halves = [
+            dot_general(half_heads(r, part, rows), flat(r.attend[part][...]), 0, 1)
+            for part in range(2)
+        ]
+        products.append(halves[0] + halves[1])
+    for rows, value in zip(blocks, products):
+        r.straight[rows, :] += value
 
 
 def row_scratch(slots, width, wide):
@@ -440,8 +481,24 @@
 
 
 LOW, HIGH = "low", "high"
-REDUCED = (SHRINK, EXPAND, MERGER, LOW, HIGH)
-FOLDED = (SHRINK, EXPAND)
+EXPAND_A, EXPAND_B, SHRINK_A, SHRINK_B = "ea", "eb", "sa", "sb"
+PARTS_OF = {
+    ATTEND: (LOW, HIGH),
+    MERGER: (MERGER,),
+    EXPAND: (EXPAND_A, EXPAND_B),
+    SHRINK: (SHRINK_A, SHRINK_B),
+}
+PARTS = (LOW, HIGH, MERGER, EXPAND_A, EXPAND_B, SHRINK_A, SHRINK_B)
+NEAR_FIRST = (EXPAND_B,)
+FAR_FIRST = (SHRINK_A, MERGER)
+
+
+def in_parts(name, value):
+    if name == ATTEND:
+        return heads_apart(value)
+    count = len(PARTS_OF[name])
+    size = value.shape[1] // count
+    return [value[:, at * size : (at + 1) * size] for at in range(count)]
 
 
 def packed_rows(first, order, columns_of, width):
@@ -536,7 +593,9 @@
     r = Refs(names, refs)
     r.result = r.cotangent
     r.d_branch = r.tokens
-    r.g_attend = (r.g_low, r.g_high)
+    for name in (ATTEND, EXPAND, SHRINK):
+        setattr(r, name, [getattr(r, part) for part in PARTS_OF[name]])
+        setattr(r, "g_" + name, [getattr(r, "g_" + part) for part in PARTS_OF[name]])
     core = lax.axis_index(DP)
     chip = lax.axis_index(FSDP)
     far = chip // GROUP
@@ -551,13 +610,6 @@
     near_devices = [(core, far * GROUP + place) for place in near_places]
     far_devices = [(core, place * GROUP + near) for place in far_places]
     other = 1 - core
-    fold_first = jnp.bitwise_xor(near, 1 + core)
-    fold_second = jnp.bitwise_xor(near, 2 - core)
-    diagonal_place = near_places[3]
-    fold_devices = [
-        (core, far * GROUP + place) for place in (fold_first, fold_first, fold_second)
-    ]
-
     started = {}
     arrived = set()
 
@@ -656,22 +708,22 @@
 
 
     class Gather:
-        def __init__(self, name, fine):
+        def __init__(self, name):
             self.key = (name,)
-            self.fine = fine
-            self.hops = range(outer if fine else 1)
+            self.near_first = name in NEAR_FIRST
             self.held = getattr(r, name)
             self.sems = (getattr(r, name + "_sends"), getattr(r, name + "_receives"))
 
         def far_copy(self, step):
-            mine = (self.held, (far, near, core))
+            block = ALL if self.near_first else near
+            mine = (self.held, (far, block, core))
             return Copy(
                 self.key, self.sems, step, far_devices[step], mine, mine,
-                (self.held, (far_origins[step], near, core)),
+                (self.held, (far_origins[step], block, core)),
             )
 
         def near_copy(self, step, hop):
-            slot = far_origins[hop] if self.fine else ALL
+            slot = far_origins[hop]
             mine = (self.held, (slot, near, core))
             return Copy(
                 self.key, self.sems, step * outer + hop, near_devices[step], mine, mine,
@@ -679,19 +731,20 @@
             )
 
         def cross(self, step):
-            whose = near_places[step]
-            mine = (self.held, (ALL, whose, core))
+            if self.near_first:
+                block = (far_origins[step], ALL)
+            else:
+                block = (ALL, near_places[step])
+            mine = (self.held, block + (core,))
             return Copy(
                 self.key, self.sems, GROUP * outer + step, sibling, mine, mine,
-                (self.held, (ALL, whose, other)),
+                (self.held, block + (other,)),
             )
 
-        def place(self, shard):
-            rows = shard.shape[0] // 2
-            mine = shard[pl.ds(pl.multiple_of(core * rows, rows), rows), :]
+        def place(self, mine):
             self.held[far, near, core] = mine.astype(BF16)
 
-        def begin(self):
+        def far_start(self):
             for step in far_steps:
                 self.far_copy(step).start()
 
@@ -699,30 +752,41 @@
             for step in near_steps:
                 self.near_copy(step, hop).start()
 
+        def begin(self):
+            if not self.near_first:
+                self.far_start()
+
         def turn(self):
-            for hop in far_steps:
-                self.far_copy(hop).arrive()
-                if self.fine:
+            if self.near_first:
+                for step in near_steps:
+                    self.near_copy(step, 0).arrive()
+                self.far_start()
+            else:
+                for hop in far_steps:
+                    self.far_copy(hop).arrive()
                     self.near_start(hop)
-            if not self.fine:
-                self.near_start(0)
             self.cross(0).start()
 
         def pass_on(self):
+            if self.near_first:
+                for step in far_steps:
+                    self.far_copy(step).arrive()
+                    self.cross(step).start()
+                return
             for step in near_steps:
-                for hop in self.hops:
+                for hop in range(outer):
                     self.near_copy(step, hop).arrive()
                 self.cross(step).start()
 
         def end(self):
-            for step in range(GROUP):
+            for step in range(outer if self.near_first else GROUP):
                 self.cross(step).arrive()
 
 
     class Reduce:
-        def __init__(self, name, folds):
+        def __init__(self, name):
             self.key = ("sum", name)
-            self.folds = folds
+            self.far_first = name in FAR_FIRST
             for part in ("g", "pair", "near", "far", "done"):
                 setattr(self, part, getattr(r, part + "_" + name))
             self.sems = (
@@ -736,22 +800,17 @@
             )
 
         def near_copy(self, step):
+            block = far if self.far_first else ALL
             return Copy(
                 self.key, self.sems, step, near_devices[step],
-                (self.pair, (ALL, near_places[step])), (self.near, step - 1),
+                (self.pair, (block, near_places[step])), (self.near, step - 1),
             )
 
-        def fold_copy(self, place):
-            block = (fold_first, diagonal_place, fold_second)[place]
-            return Copy(
-                self.key, self.sems, place + 1, fold_devices[place],
-                (self.pair, (ALL, block)), (self.near, place),
-            )
-
         def far_copy(self, step):
+            block = ALL if self.far_first else near
             return Copy(
                 self.key, self.sems, GROUP + step - 1, far_devices[step],
-                (self.pair, (far_places[step], near)), (self.far, step - 1),
+                (self.pair, (far_places[step], block)), (self.far, step - 1),
             )
 
         def done_copy(self):
@@ -773,46 +832,48 @@
                 return carry
 
             lax.fori_loop(0, outer, block, 0)
-            if self.folds:
-                self.fold_copy(0).start()
-                self.fold_copy(1).start()
+            if self.far_first:
+                for step in far_steps:
+                    self.far_copy(step).start()
+            else:
+                for step in near_steps:
+                    self.near_copy(step).start()
+
+        def pass_on(self):
+            if self.far_first:
+                for step in far_steps:
+                    self.far_copy(step).arrive()
+                total = self.pair[far].astype(F32)
+                for step in far_steps:
+                    total = total + self.far[step - 1].astype(F32)
+                self.pair[far] = total.astype(BF16)
+                for step in near_steps:
+                    self.near_copy(step).start()
                 return
             for step in near_steps:
-                self.near_copy(step).start()
-
-        def add(self, place, landed):
+                self.near_copy(step).arrive()
+
             def block(step, carry):
-                total = self.pair[step, place].astype(F32)
-                for at in landed:
-                    total = total + self.near[at, step].astype(F32)
-                self.pair[step, place] = total.astype(BF16)
+                total = self.pair[step, near].astype(F32)
+                for place in near_steps:
+                    total = total + self.near[place - 1, step].astype(F32)
+                self.pair[step, near] = total.astype(BF16)
                 return carry
 
             lax.fori_loop(0, outer, block, 0)
-
-        def fold(self):
-            self.fold_copy(1).arrive()
-            self.add(fold_second, (1,))
-            self.fold_copy(2).start()
-
-        def pass_on(self):
-            if self.folds:
-                self.fold_copy(0).arrive()
-                self.fold_copy(2).arrive()
-                self.add(near, (0, 2))
-            else:
+            for step in far_steps:
+                self.far_copy(step).start()
+
+        def collect(self):
+            total = self.pair[far, near].astype(F32)
+            if self.far_first:
                 for step in near_steps:
                     self.near_copy(step).arrive()
-                self.add(near, [step - 1 for step in near_steps])
-            for step in far_steps:
-                self.far_copy(step).start()
-
-        def collect(self):
-            for step in far_steps:
-                self.far_copy(step).arrive()
-            total = self.pair[far, near].astype(F32)
-            for step in far_steps:
-                total = total + self.far[step - 1].astype(F32)
+                    total = total + self.near[step - 1].astype(F32)
+            else:
+                for step in far_steps:
+                    self.far_copy(step).arrive()
+                    total = total + self.far[step - 1].astype(F32)
             self.done[core] = total
             self.done_copy().start()
 
@@ -825,12 +886,26 @@
     column_sum = Sum("column", 1)
     last_sum = Sum("last", 2)
     step_sum = Sum("step", 2)
-    gathers = {name: Gather(name, name == ATTEND) for name in MATRICES}
-    sums = {name: Reduce(name, name in FOLDED) for name in REDUCED}
+    gathers = {name: Gather(name) for name in PARTS}
+    sums = {name: Reduce(name) for name in PARTS}
     shards = {name: getattr(r, name + "_weight") for name in MATRICES}
 
-    gathers[ATTEND].place(shards[ATTEND])
-    gathers[ATTEND].begin()
+    def my_rows(shard):
+        half = shard.shape[0] // 2
+        return shard[pl.ds(pl.multiple_of(core * half, half), half), :]
+
+    def place(name):
+        for part, mine in zip(PARTS_OF[name], in_parts(name, my_rows(shards[name]))):
+            gathers[part].place(mine)
+
+    place(ATTEND)
+    gathers[LOW].begin()
+    gathers[LOW].near_start(0)
+    gathers[HIGH].begin()
+    place(EXPAND)
+    for part in NEAR_FIRST:
+        gathers[part].near_start(0)
+    gathers[HIGH].near_start(0)
 
 
     columns_of = {name: getattr(r, name + "_columns").shape[1] * outer * GROUP for name in MATRICES}
@@ -872,90 +947,96 @@
         return r.packed[...]
 
 
-    for name in (MERGER, EXPAND, SHRINK):
-        gathers[name].place(shards[name])
-    gathers[ATTEND].near_start(0)
+    place(MERGER)
+    place(SHRINK)
+    early.begin(early_value())
     load_tokens.wait()
     prepare(r)
-    gathers[ATTEND].turn()
-    for name in (MERGER, EXPAND, SHRINK):
-        gathers[name].begin()
-    gathers[ATTEND].pass_on()
-    early.begin(early_value())
+    gathers[LOW].turn()
+    later = [part for part in PARTS[2:] if part not in NEAR_FIRST]
+    for part in later:
+        gathers[part].begin()
+    gathers[HIGH].turn()
+    early.turn()
+    for part in later:
+        gathers[part].near_start(0)
+    for part in NEAR_FIRST:
+        gathers[part].turn()
+    gathers[LOW].pass_on()
+    gathers[LOW].end()
+    project(r, 0)
     gathers[MERGER].turn()
-    gathers[ATTEND].end()
-    project(r)
-    gathers[EXPAND].turn()
-
-    def early_hook():
-        early.turn()
-
-    def shrink_gather_hook():
-        gathers[SHRINK].turn()
-
-    def merger_gather_hook():
-        gathers[MERGER].pass_on()
-
-    attend_forward(r, ((1, early_hook), (2, shrink_gather_hook), (3, merger_gather_hook)))
-    gathers[EXPAND].pass_on()
+    attend_forward(r, 0, 2, ())
+    gathers[HIGH].pass_on()
+    gathers[EXPAND_A].turn()
+    gathers[HIGH].end()
+    project(r, 1)
+    gathers[SHRINK_A].turn()
+    gathers[SHRINK_B].turn()
+    attend_forward(r, 2, 4, ())
+    gathers[MERGER].pass_on()
     early_all = early.end()
     r.early[...] = early_all
     r.vectors[...] = early_all.astype(BF16).astype(F32)
+    gathers[EXPAND_A].pass_on()
+    gathers[MERGER].end()
+    gathers[EXPAND_B].pass_on()
+    gathers[EXPAND_A].end()
+    gathers[EXPAND_B].end()
+    first_half(r)
     late.begin(late_value())
-    gathers[MERGER].end()
-    gathers[EXPAND].end()
-    first_half(r)
-    late.turn()
-    gathers[SHRINK].pass_on()
     load_cotangent.wait()
-    gathers[SHRINK].end()
+    gathers[SHRINK_A].pass_on()
+    gathers[SHRINK_B].pass_on()
+    gathers[SHRINK_A].end()
+    gathers[SHRINK_B].end()
     second_half(r)
     store_result = local(r.result, r.result_out, 0)
     store_result.start()
-    r.late[...] = late.end()
-
-
-    shrink_gradient(r)
-    sums[SHRINK].begin()
-    way_back(r)
-    sums[SHRINK].turn()
+
+
+    shrink_gradient(r, 0)
+    sums[SHRINK_A].begin()
+    shrink_gradient(r, 1)
+    sums[SHRINK_B].begin()
+    sums[SHRINK_A].turn()
+    late.turn()
+    way_back(r, sums[SHRINK_B].turn)
+    expand_gradient(r, 0)
+    sums[EXPAND_A].begin()
+    expand_gradient(r, 1)
+    sums[EXPAND_B].begin()
     vector_sum.begin(vector_total(r))
-    expand_gradient(r)
-    sums[EXPAND].begin()
     merger_gradient(r)
     sums[MERGER].begin()
-    sums[EXPAND].turn()
+    sums[EXPAND_A].turn()
 
     def hook_one():
-        sums[SHRINK].fold()
+        sums[EXPAND_B].turn()
+        sums[MERGER].turn()
+
+    def hook_three():
+        sums[LOW].turn()
         vector_sum.turn()
-
-    def hook_two():
-        sums[MERGER].turn()
-
-    def hook_three():
-        attend_gradient(r, 0)
-        sums[LOW].begin()
-
-    def hook_four():
-        sums[SHRINK].pass_on()
-        sums[LOW].turn()
-
-    def hook_five():
-        sums[EXPAND].fold()
-
-    attend_backward(
-        r, ((1, hook_one), (2, hook_two), (4, hook_three), (5, hook_four), (6, hook_five))
-    )
+        sums[SHRINK_A].pass_on()
+
+    pairs = width // 128
+    attend_backward(r, 0, pairs // 2, ((1, hook_one),))
+    attend_gradient(r, 0)
+    sums[LOW].begin()
+    attend_backward(r, pairs // 2, pairs, ((pairs // 2 + 1, hook_three),))
     attend_gradient(r, 1)
     sums[HIGH].begin()
-    sums[EXPAND].pass_on()
+    sums[SHRINK_B].pass_on()
+    sums[HIGH].turn()
     sums[MERGER].pass_on()
-    sums[HIGH].turn()
     input_gradient(r)
     store_input = local(r.straight, r.input_out, 1)
     store_input.start()
+    sums[EXPAND_A].pass_on()
+    r.late[...] = late.end()
     r.vector_out[...] = vector_sum.end()
+    sums[LOW].pass_on()
 
 
     def keep(name, whole):
@@ -963,24 +1044,29 @@
         squares = jnp.sum(whole * whole, axis=0, keepdims=True)
         split_into(r.packed, column_at[name][0], squares, width)
 
-    sums[SHRINK].collect()
-    sums[LOW].pass_on()
-    sums[EXPAND].collect()
+    sums[SHRINK_A].collect()
+    sums[EXPAND_B].pass_on()
     sums[MERGER].collect()
+    sums[SHRINK_B].collect()
+    sums[LOW].collect()
+    sums[HIGH].pass_on()
+    sums[EXPAND_A].collect()
+    sums[EXPAND_B].collect()
     r.packed[...] = jnp.zeros_like(r.packed)
     for name in (SHRINK, EXPAND, MERGER):
-        sums[name].end()
-        whole = flat(getattr(r, "done_" + name)[...])
-        keep(name, whole.T if name == SHRINK else whole)
+        for part in PARTS_OF[name]:
+            sums[part].end()
+        done = [flat(getattr(r, "done_" + part)[...]) for part in PARTS_OF[name]]
+        if name == SHRINK:
+            done = [value.T for value in done]
+        keep(name, jnp.concatenate(done, axis=1))
     column_sum.begin(r.packed[0:COLUMN_ROWS, :])
-    sums[HIGH].pass_on()
-    sums[LOW].collect()
-    column_sum.turn()
     sums[HIGH].collect()
     attend_half = heads_together([getattr(r, "done_" + name)[core] for name in (LOW, HIGH)])
     squares = jnp.sum(attend_half * attend_half, axis=0, keepdims=True)
     split_into(r.packed, 0, squares, width)
     last_sum.begin(r.packed[0:COLUMN_ROWS, :])
+    column_sum.turn()
     sums[LOW].end()
     sums[HIGH].end()
     r.out_attend[...] = heads_together([flat(getattr(r, "done_" + name)[...]) for name in (LOW, HIGH)])
@@ -998,11 +1084,8 @@
     rows = []
     for name in MATRICES:
         rows_old = getattr(r, name + "_rows")[...]
-        whole = getattr(r, "out_" + name)
-        half = whole.shape[0] // 2
-        mine = whole[pl.ds(pl.multiple_of(core * half, half), half), :]
         step = facts.factored(
-            name, mine, my_half(column_of(rows_old)), float(rows_old.shape[1] * outer * GROUP)
+            name, my_rows(getattr(r, "out_" + name)), my_half(column_of(rows_old)), float(rows_old.shape[1] * outer * GROUP)
         )[3]
         rows.append(fold_lanes(jnp.sum(step * step, axis=0, keepdims=True)))
     step_sum.begin(jnp.concatenate(rows + [jnp.zeros((4, 128), F32)], axis=0))
@@ -1020,15 +1103,22 @@
     outer, width, wide = layout_sizes
     r = Refs(names, refs)
     chip = lax.axis_index(FSDP)
-    copies = [
-        pltpu.make_async_copy(r.result_in, r.block_output, r.sems.at[0]),
-        pltpu.make_async_copy(r.input_in, r.input_gradient, r.sems.at[1]),
+    into = [
+        pltpu.make_async_copy(r.result_in, r.result, r.sems.at[0]),
+        pltpu.make_async_copy(r.input_in, r.straight, r.sems.at[1]),
     ]
-    for copy in copies:
+    out_of = [
+        pltpu.make_async_copy(r.result, r.block_output, r.sems.at[2]),
+        pltpu.make_async_copy(r.straight, r.input_gradient, r.sems.at[3]),
+    ]
+    for copy in into:
         copy.start()
     vector_gradient = r.vector_sum[...]
     facts = Statistics(r, layout_sizes, r.column_sum, vector_gradient)
     r.global_norm[...] = facts.norm
+    for coming, going in zip(into, out_of):
+        coming.wait()
+        going.start()
     for name in MATRICES:
         weight = getattr(r, name + "_weight")[...]
         rows_all = float(weight.shape[0] * outer * GROUP)
@@ -1066,7 +1156,7 @@
         (r.vector_updated, updated),
     ):
         ref[...] = pltpu.roll(value, turn, 1)[0:6, 0:thin]
-    for copy in copies:
+    for copy in out_of:
         copy.wait()
 
 
@@ -1092,6 +1182,21 @@
     return dict(zip(outputs, results, strict=True))
 
 
+def add_part(scratch, outer, name, held, half):
+    far_first = name in FAR_FIRST
+    near_block = half if far_first else (outer,) + half
+    far_block = (GROUP,) + half if far_first else half
+    scratch[name] = pltpu.VMEM((outer, GROUP, 2) + held, BF16)
+    scratch["g_" + name] = pltpu.VMEM((outer, GROUP, 2) + half, BF16)
+    scratch["pair_" + name] = pltpu.VMEM((outer, GROUP) + half, BF16)
+    scratch["near_" + name] = pltpu.VMEM((GROUP - 1,) + near_block, BF16)
+    scratch["far_" + name] = pltpu.VMEM((max(1, outer - 1),) + far_block, BF16)
+    scratch["done_" + name] = pltpu.VMEM((2,) + half, F32)
+    for way in ("_sends", "_receives"):
+        scratch[name + way] = pltpu.SemaphoreType.DMA((GROUP * outer + GROUP,))
+        scratch["sum_" + name + way] = pltpu.SemaphoreType.DMA((GROUP + outer + 1,))
+
+
 def staged_shards(devices, tokens, lengths, weights, vectors, rows, columns, moments, cotangent):
     outer = devices // GROUP
     slots, width = tokens.shape[1:]
@@ -1139,25 +1244,13 @@
         scratch[name + "_far"] = pltpu.VMEM((outer,) + size, F32)
         for way in ("_sends", "_receives"):
             scratch[name + way] = pltpu.SemaphoreType.DMA((2 * GROUP + outer,))
-    for name in MATRICES:
-        held, wide_now = weights[name].shape
-        scratch[name] = pltpu.VMEM((outer, GROUP, 2, held // 2, wide_now), BF16)
-        for way in ("_sends", "_receives"):
-            scratch[name + way] = pltpu.SemaphoreType.DMA((GROUP * outer + GROUP,))
-    for name in REDUCED:
-        held, wide_now = weights[ATTEND if name in (LOW, HIGH) else name].shape
-        half = (held // 2, wide_now)
-        if name == SHRINK:
-            half = (wide_now // 2, held)
-        elif name in (LOW, HIGH):
-            half = (held // 2, wide_now // 2)
-        scratch["g_" + name] = pltpu.VMEM((outer, GROUP, 2) + half, BF16)
-        scratch["pair_" + name] = pltpu.VMEM((outer, GROUP) + half, BF16)
-        scratch["near_" + name] = pltpu.VMEM((GROUP - 1, outer) + half, BF16)
-        scratch["far_" + name] = pltpu.VMEM((max(1, outer - 1),) + half, BF16)
-        scratch["done_" + name] = pltpu.VMEM((2,) + half, F32)
-        for way in ("_sends", "_receives"):
-            scratch["sum_" + name + way] = pltpu.SemaphoreType.DMA((GROUP + outer + 1,))
+    for of in MATRICES:
+        for name in PARTS_OF[of]:
+            rows, all_columns = weights[of].shape
+            wide_now = all_columns // len(PARTS_OF[of])
+            held = (rows // 2, wide_now)
+            half = (wide_now // 2, rows) if of == SHRINK else held
+            add_part(scratch, outer, name, held, half)
     got = call(
         shard_kernel, sizes, inputs, outputs, scratch,
         ("tokens_in", "cotangent_in", "result_out", "input_out"),
@@ -1186,8 +1279,13 @@
     for name in ("vector_gradient", "vector_variance", "vector_updated"):
         outputs[name] = shape(vectors.shape, F32)
     out = call(
-        update_kernel, sizes, inputs, outputs, dict(sems=pltpu.SemaphoreType.DMA((2,))),
-        ("block_output", "input_gradient"),
+        update_kernel, sizes, inputs, outputs,
+        dict(
+            sems=pltpu.SemaphoreType.DMA((4,)),
+            result=pltpu.VMEM((slots, width), BF16),
+            straight=pltpu.VMEM((slots, width), F32),
+        ),
+        ("result_in", "input_in", "block_output", "input_gradient"),
         pltpu.CompilerParams(vmem_limit_bytes=VMEM_LIMIT),
         "update",
     )
@@ -1200,23 +1298,40 @@
     return tuple(out.values())
 
 
+def tiled_gradient(into, left, right):
+    def tile(step, carry):
+        columns = aligned(step * 2 * TILE, 2 * TILE)
+        into[:, columns] = dot_nn(left[...], right[:, columns]).astype(into.dtype)
+        return carry
+
+    lax.fori_loop(0, into.shape[1] // (2 * TILE), tile, 0)
+
+
 def row_kernel(names, *refs):
     r = Refs(names, refs)
-    prepare(r)
-    project(r)
-    attend_forward(r, ())
-    first_half(r)
-    second_half(r)
-    shrink_gradient(r)
-    way_back(r)
+    r.attend = (r.attend_low, r.attend_high)
+    r.expand, r.shrink = (r.expand,), (r.shrink,)
+    r.g_attend = (r.g_attend_low, r.g_attend_high)
+    pairs = r.tokens.shape[1] // 128
+    steps = (
+        functools.partial(prepare, r),
+        functools.partial(project, r, 0),
+        functools.partial(project, r, 1),
+        functools.partial(attend_forward, r, 0, pairs, ()),
+        functools.partial(first_half, r),
+        functools.partial(second_half, r),
+        functools.partial(tiled_gradient, r.g_shrink, r.d_second_t, r.active),
+        functools.partial(way_back, r),
+        functools.partial(tiled_gradient, r.g_expand, r.first_t, r.d_hidden),
+        functools.partial(tiled_gradient, r.g_merger, r.context_t, r.d_branch),
+        functools.partial(attend_backward, r, 0, pairs, ()),
+        functools.partial(attend_gradient, r, 0),
+        functools.partial(attend_gradient, r, 1),
+        functools.partial(input_gradient, r),
+    )
+    for step in steps:
+        pl.when(lax.axis_index(FSDP) >= 0)(step)
     r.g_vectors[...] = vector_total(r)
-    expand_gradient(r)
-    merger_gradient(r)
-    attend_backward(r, ())
-    r.g_attend = (r.g_attend_low, r.g_attend_high)
-    attend_gradient(r, 0)
-    attend_gradient(r, 1)
-    input_gradient(r)
 
 
 def plain_shards(devices, tokens, lengths, weights, vectors, rows, columns, moments, cotangent):
@@ -1229,6 +1344,7 @@
     }
     vector_rows = lax.all_gather(vectors.astype(BF16), FSDP, axis=1, tiled=True).astype(F32)
     vector_rows = jnp.concatenate([vector_rows, jnp.zeros((2, width), F32)], axis=0)
+    whole["attend_low"], whole["attend_high"] = heads_apart(whole.pop(ATTEND))
     inputs = dict(
         tokens=tokens[0], lengths=lengths, cotangent=cotangent[0], vectors=vector_rows, **whole
     )

time: 136 us -> 119 us (0.88)
  Pallas kernels: 135 us -> 118 us
    pallas_call x2, Pallas kernels: 135 us -> 118 us  [call(): pl.pallas_call(functools.partial(kernel, sizes, names), in_specs=[anywher...]
where the time goes in v3:
time: 119 us; the launch traced here: 118 us
  Pallas kernels  118 us (99%)
    pallas_call x2, Pallas kernels, call(): pl.pallas_call(functools.partial(kernel, sizes, names), in_specs=[anywher...  118 us

profile of v3, /device:TPU:0, one launch (start us, length us, event | category | flops | bytes accessed | tf_op | source)
XLA Modules:
  0.0 118.4 jit_solution(15043106415197643042)
XLA Ops:
  0.7 111.3 %row_and_sums.1 = (bf16[1024,512]{1,0:T(8,128)(2,1)}, f32[1024,512]{1,0:T(8,128)}, f32[8,512]{1,0:T(8,128)}, f32[8,512]{1,0:T(8,128)}, f32[16,512]{1,0:T(8,128)}...) custom-call(bf16[1024,512]{1,0:T(8,128)(2,1)} %bitcast.21, ...), custom_call_target="tpu_custom_call" | custom-call | tf_op jit(solution)/shard_map/row_and_sums/pallas_call | solution.py:1173
  112.0 6.2 %update.1 = (bf16[1024,512]{1,0:T(8,128)(2,1)}, f32[1024,512]{1,0:T(8,128)}, f32[1,1]{1,0:T(1,128)}, f32[32,1536]{1,0:T(8,128)}, f32[1,32]{1,0:T(1,128)}, /*inde...) custom-call(bf16[1024,512]{1,0:T(8,128)(2,1)} %get-tuple-element.63., ...), custom_call_target="tpu_custom_call" | custom-call | tf_op jit(solution)/shard_map/update/pallas_call | solution.py:1173

commit v4 on v3

--- a/solution.py
+++ b/solution.py
@@ -511,7 +511,7 @@
 
 SQUARES, ROW_SUMS, EARLY_ROWS = 6, 7, 8
 LATE_COLUMNS, LATE_ROWS = 6, 16
-COLUMN_ROWS = 8
+COLUMN_ROWS, LAST_ROWS = 8, 4
 ALL = slice(None)
 
 
@@ -1029,52 +1029,55 @@
     sums[HIGH].begin()
     sums[SHRINK_B].pass_on()
     sums[HIGH].turn()
-    sums[MERGER].pass_on()
-    input_gradient(r)
-    store_input = local(r.straight, r.input_out, 1)
-    store_input.start()
-    sums[EXPAND_A].pass_on()
-    r.late[...] = late.end()
-    r.vector_out[...] = vector_sum.end()
-    sums[LOW].pass_on()
-
-
-    def keep(name, whole):
-        getattr(r, "out_" + name)[...] = whole
-        squares = jnp.sum(whole * whole, axis=0, keepdims=True)
-        split_into(r.packed, column_at[name][0], squares, width)
-
-    sums[SHRINK_A].collect()
-    sums[EXPAND_B].pass_on()
-    sums[MERGER].collect()
-    sums[SHRINK_B].collect()
-    sums[LOW].collect()
-    sums[HIGH].pass_on()
-    sums[EXPAND_A].collect()
-    sums[EXPAND_B].collect()
-    r.packed[...] = jnp.zeros_like(r.packed)
-    for name in (SHRINK, EXPAND, MERGER):
+
+
+    def keep(name):
         for part in PARTS_OF[name]:
             sums[part].end()
         done = [flat(getattr(r, "done_" + part)[...]) for part in PARTS_OF[name]]
         if name == SHRINK:
             done = [value.T for value in done]
-        keep(name, jnp.concatenate(done, axis=1))
-    column_sum.begin(r.packed[0:COLUMN_ROWS, :])
+        whole_done = jnp.concatenate(done, axis=1)
+        getattr(r, "out_" + name)[...] = whole_done
+        squares = jnp.sum(whole_done * whole_done, axis=0, keepdims=True)
+        split_into(r.packed, column_at[name][0], squares, width)
+
+    sums[MERGER].pass_on()
+    sums[EXPAND_A].pass_on()
+    sums[LOW].pass_on()
+    sums[SHRINK_A].collect()
+    sums[EXPAND_B].pass_on()
+    sums[SHRINK_B].collect()
+    sums[MERGER].collect()
+    r.late[...] = late.end()
+    r.vector_out[...] = vector_sum.end()
+    r.packed[...] = jnp.zeros_like(r.packed)
+    sums[HIGH].pass_on()
+    sums[LOW].collect()
+    keep(SHRINK)
+    keep(MERGER)
+    sums[EXPAND_A].collect()
+    sums[EXPAND_B].collect()
     sums[HIGH].collect()
     attend_half = heads_together([getattr(r, "done_" + name)[core] for name in (LOW, HIGH)])
     squares = jnp.sum(attend_half * attend_half, axis=0, keepdims=True)
-    split_into(r.packed, 0, squares, width)
-    last_sum.begin(r.packed[0:COLUMN_ROWS, :])
+    row = COLUMN_ROWS
+    split_into(r.packed, row, squares, width)
+    last_sum.begin(r.packed[row : row + LAST_ROWS, :])
+    keep(EXPAND)
+    column_sum.begin(r.packed[0:COLUMN_ROWS, :])
+    input_gradient(r)
+    store_input = local(r.straight, r.input_out, 1)
+    store_input.start()
+    last_sum.turn()
     column_sum.turn()
     sums[LOW].end()
     sums[HIGH].end()
     r.out_attend[...] = heads_together([flat(getattr(r, "done_" + name)[...]) for name in (LOW, HIGH)])
-    r.column_out[0:COLUMN_ROWS, :] = column_sum.end()
-    last_sum.turn()
     r.early_out[...] = r.early[...]
     r.late_out[...] = r.late[...]
-    r.column_out[COLUMN_ROWS : 2 * COLUMN_ROWS, :] = last_sum.end()
+    r.column_out[row : row + LAST_ROWS, :] = last_sum.end()
+    r.column_out[0:COLUMN_ROWS, :] = column_sum.end()
     facts = Statistics(r, layout_sizes, r.column_out, r.vector_out[...])
 
     def my_half(value):
@@ -1085,7 +1088,8 @@
     for name in MATRICES:
         rows_old = getattr(r, name + "_rows")[...]
         step = facts.factored(
-            name, my_rows(getattr(r, "out_" + name)), my_half(column_of(rows_old)), float(rows_old.shape[1] * outer * GROUP)
+            name, my_rows(getattr(r, "out_" + name)), my_half(column_of(rows_old)),
+            float(rows_old.shape[1] * outer * GROUP),
         )[3]
         rows.append(fold_lanes(jnp.sum(step * step, axis=0, keepdims=True)))
     step_sum.begin(jnp.concatenate(rows + [jnp.zeros((4, 128), F32)], axis=0))
@@ -1103,22 +1107,15 @@
     outer, width, wide = layout_sizes
     r = Refs(names, refs)
     chip = lax.axis_index(FSDP)
-    into = [
-        pltpu.make_async_copy(r.result_in, r.result, r.sems.at[0]),
-        pltpu.make_async_copy(r.input_in, r.straight, r.sems.at[1]),
+    out_of = [
+        pltpu.make_async_copy(r.result_in, r.block_output, r.sems.at[2]),
+        pltpu.make_async_copy(r.input_in, r.input_gradient, r.sems.at[3]),
     ]
-    out_of = [
-        pltpu.make_async_copy(r.result, r.block_output, r.sems.at[2]),
-        pltpu.make_async_copy(r.straight, r.input_gradient, r.sems.at[3]),
-    ]
-    for copy in into:
+    for copy in out_of:
         copy.start()
     vector_gradient = r.vector_sum[...]
     facts = Statistics(r, layout_sizes, r.column_sum, vector_gradient)
     r.global_norm[...] = facts.norm
-    for coming, going in zip(into, out_of):
-        coming.wait()
-        going.start()
     for name in MATRICES:
         weight = getattr(r, name + "_weight")[...]
         rows_all = float(weight.shape[0] * outer * GROUP)
@@ -1237,7 +1234,7 @@
         ("late", 1, (LATE_ROWS, width)),
         ("vector", 2, (8, width)),
         ("column", 1, (COLUMN_ROWS, width)),
-        ("last", 2, (COLUMN_ROWS, width)),
+        ("last", 2, (LAST_ROWS, width)),
         ("step", 2, (8, 128)),
     ):
         scratch[name + "_near"] = pltpu.VMEM((cores, GROUP) + size, F32)
@@ -1282,10 +1279,8 @@
         update_kernel, sizes, inputs, outputs,
         dict(
             sems=pltpu.SemaphoreType.DMA((4,)),
-            result=pltpu.VMEM((slots, width), BF16),
-            straight=pltpu.VMEM((slots, width), F32),
         ),
-        ("result_in", "input_in", "block_output", "input_gradient"),
+        ("block_output", "input_gradient"),
         pltpu.CompilerParams(vmem_limit_bytes=VMEM_LIMIT),
         "update",
     )

time: 119 us -> 117 us (0.983)
  Pallas kernels: 118 us -> 116 us
    pallas_call x2, Pallas kernels: 118 us -> 116 us  [call(): pl.pallas_call(functools.partial(kernel, sizes, names), in_specs=[anywher...]
where the time goes in v4:
time: 117 us
  Pallas kernels  116 us (99%)
    pallas_call x2, Pallas kernels, call(): pl.pallas_call(functools.partial(kernel, sizes, names), in_specs=[anywher...  116 us

profile of v4, /device:TPU:0, one launch (start us, length us, event | category | flops | bytes accessed | tf_op | source)
XLA Modules:
  0.0 117.2 jit_solution(15266943113527674543)
XLA Ops:
  0.7 110.9 %row_and_sums.1 = (bf16[1024,512]{1,0:T(8,128)(2,1)}, f32[1024,512]{1,0:T(8,128)}, f32[8,512]{1,0:T(8,128)}, f32[8,512]{1,0:T(8,128)}, f32[16,512]{1,0:T(8,128)}...) custom-call(bf16[1024,512]{1,0:T(8,128)(2,1)} %bitcast.21, ...), custom_call_target="tpu_custom_call" | custom-call | tf_op jit(solution)/shard_map/row_and_sums/pallas_call | solution.py:1170
  111.5 5.5 %update.1 = (bf16[1024,512]{1,0:T(8,128)(2,1)}, f32[1024,512]{1,0:T(8,128)}, f32[1,1]{1,0:T(1,128)}, f32[32,1536]{1,0:T(8,128)}, f32[1,32]{1,0:T(1,128)}, /*inde...) custom-call(bf16[1024,512]{1,0:T(8,128)(2,1)} %get-tuple-element.63., ...), custom_call_target="tpu_custom_call" | custom-call | tf_op jit(solution)/shard_map/update/pallas_call | solution.py:1170
